TPU v7x, 32 devices: a whole 2x2x4 slice. The times are simulated.
32 devices in a mesh: seq: 8 (over y, x, core), fsdp: 4 (over z).
Axes of the slice: x: 2, y: 2, z: 4, core: 2. Of those that a mesh axis runs over, the one named last changes fastest.
Arguments:
- inputs: bfloat16 [4, 1024, 1536], P('fsdp', 'seq'), may hold values from -6 to 6
- cotangent: bfloat16 [4, 1024, 1536], P('fsdp', 'seq'), may hold values from -6 to 6
- mix_weight: float32 [2, 1536, 6144], P(None, ('seq', 'fsdp')), may hold values from -0.15625 to 0.15625
- mix_first: float32 [2, 1536, 6144], P(None, ('seq', 'fsdp')), may hold values from -40 to 40
- mix_second: float32 [2, 1536, 6144], P(None, ('seq', 'fsdp')), may hold values from 215.57895 to 862.3158
- feed_weight: float32 [2, 1536, 13824], P(None, ('seq', 'fsdp')), may hold values from -0.15625 to 0.15625
- feed_first: float32 [2, 1536, 13824], P(None, ('seq', 'fsdp')), may hold values from -20 to 20
- feed_second: float32 [2, 1536, 13824], P(None, ('seq', 'fsdp')), may hold values from 53.894737 to 215.57895
- down_weight: float32 [2, 6912, 1536], P(None, ('seq', 'fsdp')), may hold values from -0.078125 to 0.078125
- down_first: float32 [2, 6912, 1536], P(None, ('seq', 'fsdp')), may hold values from -20 to 20
- down_second: float32 [2, 6912, 1536], P(None, ('seq', 'fsdp')), may hold values from 53.894737 to 215.57895
- gain_weight: float32 [2, 2, 1536], P(None, None, ('seq', 'fsdp')), may hold values from 0.5 to 1.5
- gain_first: float32 [2, 2, 1536], P(None, None, ('seq', 'fsdp')), may hold values from -64 to 64
- gain_second: float32 [2, 2, 1536], P(None, None, ('seq', 'fsdp')), may hold values from 485.05264 to 1940.2106
- tap_weight: float32 [2, 3, 1536], P(None, None, ('seq', 'fsdp')), may hold values from -3.5 to 3.5
- tap_first: float32 [2, 3, 1536], P(None, None, ('seq', 'fsdp')), may hold values from -40 to 40
- tap_second: float32 [2, 3, 1536], P(None, None, ('seq', 'fsdp')), may hold values from 215.57895 to 862.3158
Outputs:
- outputs: bfloat16 [4, 1024, 1536], P('fsdp', 'seq')
- input_grad: float32 [4, 1024, 1536], P('fsdp', 'seq')
- mix_first_new: float32 [2, 1536, 6144], P(None, ('seq', 'fsdp'))
- mix_second_new: float32 [2, 1536, 6144], P(None, ('seq', 'fsdp'))
- mix_weight_new: float32 [2, 1536, 6144], P(None, ('seq', 'fsdp'))
- feed_first_new: float32 [2, 1536, 13824], P(None, ('seq', 'fsdp'))
- feed_second_new: float32 [2, 1536, 13824], P(None, ('seq', 'fsdp'))
- feed_weight_new: float32 [2, 1536, 13824], P(None, ('seq', 'fsdp'))
- down_first_new: float32 [2, 6912, 1536], P(None, ('seq', 'fsdp'))
- down_second_new: float32 [2, 6912, 1536], P(None, ('seq', 'fsdp'))
- down_weight_new: float32 [2, 6912, 1536], P(None, ('seq', 'fsdp'))
- gain_first_new: float32 [2, 2, 1536], P(None, None, ('seq', 'fsdp'))
- gain_second_new: float32 [2, 2, 1536], P(None, None, ('seq', 'fsdp'))
- gain_weight_new: float32 [2, 2, 1536], P(None, None, ('seq', 'fsdp'))
- tap_first_new: float32 [2, 3, 1536], P(None, None, ('seq', 'fsdp'))
- tap_second_new: float32 [2, 3, 1536], P(None, None, ('seq', 'fsdp'))
- tap_weight_new: float32 [2, 3, 1536], P(None, None, ('seq', 'fsdp'))
All inputs are finite; a program needn't handle non-finite values.
Results may differ from a plain program's by a relative error of at most 0.019.
The roundings to bfloat16 on the way count: a program that leaves them out, or rounds other values in their place, can miss the bound.
Values may be sent and summed in bfloat16 or wider, within the bound.
No kernel may reach another device: no remote copies, remote signals or barrier semaphores. Data moves between devices by JAX's collectives and lax.ppermute only.
A program may use at most 640 MiB of HBM per device.

v0:
```python
import jax
import jax.numpy as jnp
from jax import lax
from jax.sharding import PartitionSpec as P

LAYERS = 2
STEP = 10


eps_norm = 1e-05
eps_adam = 1e-08
beta_one = 0.9
beta_two = 0.95
rate_matrix = 0.05
rate_vector = 0.6
decay_matrix = 0.1


def from_behind(array, axis, by):
    devices = lax.axis_size(axis)
    pairs = [(i, i + by) for i in range(devices) if 0 <= i + by < devices]
    return lax.ppermute(array, axis, pairs)


def matmul(left, right):
    return jnp.dot(left, right, preferred_element_type=jnp.float32)


def matmul_nt(left, right):
    return lax.dot_general(
        left, right, (((1,), (1,)), ((), ())), preferred_element_type=jnp.float32
    )


def matmul_tn(left, right):
    return lax.dot_general(
        left, right, (((0,), (0,)), ((), ())), preferred_element_type=jnp.float32
    )


def layer_pieces(params, layer_index):
    return tuple((part[layer_index].astype(jnp.bfloat16) for part in params))


def gather_forward(params, layer_index):
    mix_part, feed_part, down_part, gain_part, tap_part = layer_pieces(params, layer_index)
    return (
        lax.all_gather(mix_part, ("seq", "fsdp"), axis=0, tiled=True),
        lax.all_gather(feed_part, ("seq", "fsdp"), axis=0, tiled=True),
        lax.all_gather(down_part, ("seq", "fsdp"), axis=0, tiled=True),
        lax.all_gather(gain_part, ("seq", "fsdp"), axis=1, tiled=True),
        lax.all_gather(tap_part, ("seq", "fsdp"), axis=1, tiled=True),
    )


def gather_backward(params, layer_index):
    mix_part, feed_part, down_part, gain_part, tap_part = layer_pieces(params, layer_index)
    return (
        lax.all_gather(mix_part, ("seq", "fsdp"), axis=0, tiled=True),
        lax.all_gather(feed_part, ("seq", "fsdp"), axis=0, tiled=True),
        lax.all_gather(down_part, ("seq", "fsdp"), axis=0, tiled=True),
        lax.all_gather(gain_part, ("seq", "fsdp"), axis=1, tiled=True),
        lax.all_gather(tap_part, ("seq", "fsdp"), axis=1, tiled=True),
    )


def column_term(left, right):
    return matmul_tn(left, right)


def mix_term(normed, projected_flow, mixed, middle_low):

    def term_rows(start, count):
        first_part = matmul_tn(normed, projected_flow)
        second_part = matmul_tn(mixed, middle_low)
        return jnp.concatenate([first_part, second_part], axis=1)

    return term_rows


def unit_rows(values):
    row_scale = lax.rsqrt(jnp.mean(values * values, axis=-1, keepdims=True) + eps_norm)
    return (values * row_scale, row_scale)


def norm_back(flow_in, unit_values, row_scale, gain_row):
    gain_grad = jnp.sum(flow_in * unit_values, axis=0)
    scaled = flow_in * gain_row
    inner_mean = jnp.mean(scaled * unit_values, axis=-1, keepdims=True)
    return (row_scale * (scaled - unit_values * inner_mean), gain_grad)


def block_forward(stream, pieces, sequences):
    mix_matrix, feed_matrix, down_matrix, gain_part, tap_part = pieces
    features = stream.shape[-1]
    gain_rows = gain_part.astype(jnp.float32)
    tap_rows = tap_part.astype(jnp.float32)
    unit_one, scale_one = unit_rows(stream)
    normed = (unit_one * gain_rows[0]).astype(jnp.bfloat16)
    projected = matmul(normed, mix_matrix[:, : 3 * features])
    b_part = projected[:, :features]
    c_part = projected[:, features : 2 * features]
    x_part = projected[:, 2 * features :]
    gated = (b_part * x_part).astype(jnp.bfloat16).reshape(sequences, -1, features)
    length = gated.shape[1]
    before = from_behind(gated[:, length - 2 :, :], "seq", 1)
    padded = jnp.concatenate([before, gated], axis=1).astype(jnp.float32)
    conv_out = (
        tap_rows[0] * padded[:, :length]
        + tap_rows[1] * padded[:, 1 : length + 1]
        + tap_rows[2] * padded[:, 2:]
    )
    conv_out = conv_out.reshape(-1, features)
    mixed = (c_part * conv_out).astype(jnp.bfloat16)
    middle = stream + matmul(mixed, mix_matrix[:, 3 * features :])
    unit_two, scale_two = unit_rows(middle)
    normed_two = (unit_two * gain_rows[1]).astype(jnp.bfloat16)
    gate_up = matmul(normed_two, feed_matrix)
    half_width = feed_matrix.shape[1] // 2
    gate_part = gate_up[:, :half_width]
    up_part = gate_up[:, half_width:]
    hidden = (jax.nn.silu(gate_part) * up_part).astype(jnp.bfloat16)
    result = middle + matmul(hidden, down_matrix)
    kept_values = (
        unit_one,
        scale_one,
        normed,
        b_part,
        c_part,
        x_part,
        padded,
        conv_out,
        mixed,
        unit_two,
        scale_two,
        normed_two,
        gate_part,
        up_part,
        hidden,
    )
    return (result, kept_values)


def block_backward(flow_out, pieces, kept_values, sequences):
    mix_matrix, feed_matrix, down_matrix, gain_part, tap_part = pieces
    (
        unit_one,
        scale_one,
        normed,
        b_part,
        c_part,
        x_part,
        padded,
        conv_out,
        mixed,
        unit_two,
        scale_two,
        normed_two,
        gate_part,
        up_part,
        hidden,
    ) = kept_values
    features = flow_out.shape[-1]
    all_devices = lax.axis_size("seq") * lax.axis_size("fsdp")
    gain_rows = gain_part.astype(jnp.float32)
    tap_rows = tap_part.astype(jnp.float32)
    flow_low = flow_out.astype(jnp.bfloat16)
    hidden_flow = matmul_nt(flow_low, down_matrix)
    sigmoid_gate = jax.nn.sigmoid(gate_part)
    gate_flow = hidden_flow * up_part * (sigmoid_gate * (1.0 + gate_part * (1.0 - sigmoid_gate)))
    up_flow = hidden_flow * (gate_part * sigmoid_gate)
    gate_up_flow = jnp.concatenate([gate_flow, up_flow], axis=1).astype(jnp.bfloat16)
    down_shard = lax.psum_scatter(
        column_term(hidden, flow_low), ("seq", "fsdp"), scatter_dimension=0, tiled=True
    )
    feed_shard = lax.psum_scatter(
        column_term(normed_two, gate_up_flow), ("seq", "fsdp"), scatter_dimension=0, tiled=True
    )
    normed_two_flow = matmul_nt(gate_up_flow, feed_matrix)
    norm_flow_two, gain_grad_two = norm_back(normed_two_flow, unit_two, scale_two, gain_rows[1])
    middle_flow = flow_out + norm_flow_two
    middle_low = middle_flow.astype(jnp.bfloat16)
    mixed_flow = matmul_nt(middle_low, mix_matrix[:, 3 * features :])
    c_flow = mixed_flow * conv_out
    conv_flow = (mixed_flow * c_part).reshape(sequences, -1, features)
    length = conv_flow.shape[1]
    after = from_behind(conv_flow[:, :2, :], "seq", -1)
    extended = jnp.concatenate([conv_flow, after], axis=1)
    gated_flow = (
        tap_rows[2] * extended[:, :length]
        + tap_rows[1] * extended[:, 1 : length + 1]
        + tap_rows[0] * extended[:, 2:]
    )
    tap_grad = jnp.stack(
        [
            jnp.sum(conv_flow * padded[:, :length], axis=(0, 1)),
            jnp.sum(conv_flow * padded[:, 1 : length + 1], axis=(0, 1)),
            jnp.sum(conv_flow * padded[:, 2:], axis=(0, 1)),
        ]
    )
    gated_flow = gated_flow.reshape(-1, features)
    projected_flow = jnp.concatenate(
        [gated_flow * x_part, c_flow, gated_flow * b_part], axis=1
    ).astype(jnp.bfloat16)
    normed_flow = matmul_nt(projected_flow, mix_matrix[:, : 3 * features])
    norm_flow_one, gain_grad_one = norm_back(normed_flow, unit_one, scale_one, gain_rows[0])
    stream_flow = middle_flow + norm_flow_one
    gain_grad = jnp.stack([gain_grad_one, gain_grad_two])
    mix_fn = mix_term(normed, projected_flow, mixed, middle_low)
    mix_shard = lax.psum_scatter(
        mix_fn(jnp.int32(0), features // all_devices * lax.axis_size(("seq", "fsdp"))),
        ("seq", "fsdp"),
        scatter_dimension=0,
        tiled=True,
    )
    gain_shard, tap_shard = (
        lax.psum_scatter(gain_grad, ("seq", "fsdp"), scatter_dimension=1, tiled=True),
        lax.psum_scatter(tap_grad, ("seq", "fsdp"), scatter_dimension=1, tiled=True),
    )
    return (stream_flow, (mix_shard, feed_shard, down_shard, gain_shard, tap_shard))


def adam_update(weight, first, second, gradient, rate, decay):
    first_new = beta_one * first + (1.0 - beta_one) * gradient
    second_new = beta_two * second + (1.0 - beta_two) * gradient * gradient
    first_hat = first_new / (1.0 - beta_one**STEP)
    second_hat = second_new / (1.0 - beta_two**STEP)
    weight_new = weight - rate * (first_hat / (jnp.sqrt(second_hat) + eps_adam) + decay * weight)
    return (first_new, second_new, weight_new)


def local(
    inputs,
    cotangent,
    mix_weight,
    mix_first,
    mix_second,
    feed_weight,
    feed_first,
    feed_second,
    down_weight,
    down_first,
    down_second,
    gain_weight,
    gain_first,
    gain_second,
    tap_weight,
    tap_first,
    tap_second,
):
    params = (mix_weight, feed_weight, down_weight, gain_weight, tap_weight)
    sequences, length, features = inputs.shape
    stream = inputs.reshape(sequences * length, features).astype(jnp.float32)
    kept_all = []
    pieces = None
    for layer_index in range(LAYERS):
        pieces = gather_forward(params, layer_index)
        stream, kept_values = block_forward(stream, pieces, sequences)
        kept_all.append(kept_values)
    outputs = stream.astype(jnp.bfloat16).reshape(sequences, length, features)
    flow = cotangent.reshape(sequences * length, features).astype(jnp.float32)
    shards_all = [None] * LAYERS
    for layer_index in reversed(range(LAYERS)):
        if layer_index == LAYERS - 1:
            current = gather_backward(params, layer_index)
        else:
            current = gather_backward(params, layer_index)
        flow, shards = block_backward(flow, current, kept_all[layer_index], sequences)
        shards_all[layer_index] = shards
    grads = [
        jnp.stack([shards_all[layer_index][member] for layer_index in range(LAYERS)])
        for member in range(5)
    ]
    input_grad = flow.reshape(sequences, length, features)
    mix_new = adam_update(mix_weight, mix_first, mix_second, grads[0], rate_matrix, decay_matrix)
    feed_new = adam_update(
        feed_weight, feed_first, feed_second, grads[1], rate_matrix, decay_matrix
    )
    down_new = adam_update(
        down_weight, down_first, down_second, grads[2], rate_matrix, decay_matrix
    )
    gain_new = adam_update(gain_weight, gain_first, gain_second, grads[3], rate_vector, 0.0)
    tap_new = adam_update(tap_weight, tap_first, tap_second, grads[4], rate_vector, 0.0)
    return (
        outputs,
        input_grad,
        mix_new[0],
        mix_new[1],
        mix_new[2],
        feed_new[0],
        feed_new[1],
        feed_new[2],
        down_new[0],
        down_new[1],
        down_new[2],
        gain_new[0],
        gain_new[1],
        gain_new[2],
        tap_new[0],
        tap_new[1],
        tap_new[2],
    )


def solution(mesh):
    return jax.shard_map(
        local,
        mesh=mesh,
        in_specs=(
            P("fsdp", "seq", None),
            P("fsdp", "seq", None),
            P(None, ("seq", "fsdp"), None),
            P(None, ("seq", "fsdp"), None),
            P(None, ("seq", "fsdp"), None),
            P(None, ("seq", "fsdp"), None),
            P(None, ("seq", "fsdp"), None),
            P(None, ("seq", "fsdp"), None),
            P(None, ("seq", "fsdp"), None),
            P(None, ("seq", "fsdp"), None),
            P(None, ("seq", "fsdp"), None),
            P(None, None, ("seq", "fsdp")),
            P(None, None, ("seq", "fsdp")),
            P(None, None, ("seq", "fsdp")),
            P(None, None, ("seq", "fsdp")),
            P(None, None, ("seq", "fsdp")),
            P(None, None, ("seq", "fsdp")),
        ),
        out_specs=(
            P("fsdp", "seq", None),
            P("fsdp", "seq", None),
            P(None, ("seq", "fsdp"), None),
            P(None, ("seq", "fsdp"), None),
            P(None, ("seq", "fsdp"), None),
            P(None, ("seq", "fsdp"), None),
            P(None, ("seq", "fsdp"), None),
            P(None, ("seq", "fsdp"), None),
            P(None, ("seq", "fsdp"), None),
            P(None, ("seq", "fsdp"), None),
            P(None, ("seq", "fsdp"), None),
            P(None, None, ("seq", "fsdp")),
            P(None, None, ("seq", "fsdp")),
            P(None, None, ("seq", "fsdp")),
            P(None, None, ("seq", "fsdp")),
            P(None, None, ("seq", "fsdp")),
            P(None, None, ("seq", "fsdp")),
        ),
        check_vma=False,
    )
```

profile of v0, /device:TPU:8, one launch (start us, length us, event | category | flops | bytes accessed | tf_op | source)
XLA Modules:
  0.0 4450.3 jit_solution(11308740922751653822)
XLA Ops:
  19.1 81.2 %all-gather.5 = bf16[1,2,1536]{1,0,2:T(2,128)(2,1)S(1)} all-gather(bf16[1,2,48]{1,0,2:T(2,128)(2,1)S(1)} %get-tuple-element.132), channel_id=7, replica_groups=mesh['seq'=8,'fsdp'=4] {'seq','fsdp'}, dimensions={2}, use_global_device_ids=true | all-gather | bytes 6336 | tf_op jit(solution)/shard_map/all_gather | solution.py:51
  101.1 83.7 %all-gather = bf16[1,2,1536]{1,0,2:T(2,128)(2,1)S(1)} all-gather(bf16[1,2,48]{1,0,2:T(2,128)(2,1)S(1)} %get-tuple-element.133), channel_id=2, replica_groups=mesh['seq'=8,'fsdp'=4] {'seq','fsdp'}, dimensions={2}, use_global_device_ids=true | all-gather | bytes 6336 | tf_op jit(solution)/shard_map/all_gather | solution.py:51
  185.7 81.5 %all-gather.2 = bf16[1,3,1536]{1,0,2:T(2,128)(2,1)S(1)} all-gather(bf16[1,3,48]{1,0,2:T(2,128)(2,1)S(1)} %get-tuple-element.131), channel_id=4, replica_groups=mesh['seq'=8,'fsdp'=4] {'seq','fsdp'}, dimensions={2}, use_global_device_ids=true | all-gather | bytes 9504 | tf_op jit(solution)/shard_map/all_gather | solution.py:52
  268.3 25.1 slice_reduce_fusion.5
  293.4 46.2 %slice_reduce_fusion.8 = (f32[1536]{0:T(1024)S(1)}, f32[1536]{0:T(1024)S(1)}, f32[1536]{0:T(1024)S(1)}) fusion(f32[1,3,1536]{1,0,2:T(1,128)S(1)} %convert_element_type.179), kind=kLoop, calls=%fused_computation.111 | loop fusion | bytes 36864 | tf_op jit(solution)/shard_map/slice | solution.py:109
  347.7 25.1 slice_reduce_fusion
  372.8 82.6 %all-gather.7 = bf16[1,3,1536]{1,0,2:T(2,128)(2,1)S(1)} all-gather(bf16[1,3,48]{1,0,2:T(2,128)(2,1)S(1)} %get-tuple-element.130), channel_id=9, replica_groups=mesh['seq'=8,'fsdp'=4] {'seq','fsdp'}, dimensions={2}, use_global_device_ids=true | all-gather | bytes 9504 | tf_op jit(solution)/shard_map/all_gather | solution.py:52
  462.8 19.7 fusion.6
  486.5 69.5 %all-gather.21.cloned.1.call-done = bf16[1,6912,1536]{2,1,0:T(8,128)(2,1)} async-done(((bf16[1,216,1536]{2,1,0:T(8,128)(2,1)}), bf16[1,6912,1536]{2,1,0:T(8,128)(2,1)}) %all-gather.21.cloned.1.call-update) | async-done | bytes 21233680 | tf_op jit(solution)/shard_map/all_gather | solution.py:50
  566.9 115.5 %all-gather.23.cloned.1.call-done = bf16[1,1536,6144]{2,1,0:T(8,128)(2,1)} async-done(((bf16[1,48,6144]{2,1,0:T(8,128)(2,1)}), bf16[1,1536,6144]{2,1,0:T(8,128)(2,1)}) %all-gather.23.cloned.1.call-update) | async-done | bytes 18874384 | tf_op jit(solution)/shard_map/all_gather | solution.py:48
  691.3 46.6 %slice_reduce_fusion.3 = (f32[1536]{0:T(1024)S(1)}, f32[1536]{0:T(1024)S(1)}, f32[1536]{0:T(1024)S(1)}) fusion(f32[1,3,1536]{1,0,2:T(1,128)S(1)} %copy-done.9), kind=kLoop, calls=%fused_computation.106 | loop fusion | bytes 36864 | tf_op jit(solution)/shard_map/slice | solution.py:109
  743.4 177.6 %all-gather.25.cloned.1.call-done = bf16[1,1536,13824]{2,1,0:T(8,128)(2,1)} async-done(((bf16[1,48,13824]{2,1,0:T(8,128)(2,1)}), bf16[1,1536,13824]{2,1,0:T(8,128)(2,1)}) %all-gather.25.cloned.1.call-update) | async-done | bytes 42467344 | tf_op jit(solution)/shard_map/all_gather | solution.py:49
  921.0 19.8 fusion.2
  940.7 117.2 %all-gather.27.cloned.1.call-done = bf16[1,6912,1536]{2,1,0:T(8,128)(2,1)} async-done(((bf16[1,216,1536]{2,1,0:T(8,128)(2,1)}), bf16[1,6912,1536]{2,1,0:T(8,128)(2,1)}) %all-gather.27.cloned.1.call-update) | async-done | bytes 21233680 | tf_op jit(solution)/shard_map/all_gather | solution.py:50
  1057.9 14.2 multiply_convert_fusion.3
  1072.2 19.8 multiply_reduce_fusion.6
  1129.8 14.0 multiply_convert_fusion.1
  1143.8 19.3 multiply_reduce_fusion.8
  1189.9 25.4 pad_maximum_fusion.1
  1233.0 25.1 pad_maximum_fusion
  1259.6 16.5 fusion.89
  1277.6 17.6 fusion.97
  1296.4 31.6 fusion.56
  1329.1 31.9 fusion.55
  1376.2 27.2 reduce-scatter.35.cloned.1.call-done
  1406.0 97.5 %reduce-scatter.31.cloned.1.call-done = f32[48,2]{1,0:T(8,128)} async-done(((f32[1536,2]{1,0:T(8,128)}), f32[48,2]{1,0:T(8,128)}) %reduce-scatter.31.cloned.1.call-update) | async-done | bytes 400
  1504.9 351.7 %reduce-scatter.21.cloned.1.call-done = f32[48,6144]{1,0:T(8,128)} async-done(((f32[1536,6144]{1,0:T(8,128)}), f32[48,6144]{1,0:T(8,128)}) %reduce-scatter.21.cloned.1.call-update) | async-done | bytes 1179664 | tf_op jit(solution)/shard_map/reduce_scatter | solution.py:210
  1856.7 355.4 %reduce-scatter.19.cloned.1.call-done = f32[48,6144]{1,0:T(8,128)} async-done(((f32[1536,6144]{1,0:T(8,128)}), f32[48,6144]{1,0:T(8,128)}) %reduce-scatter.19.cloned.1.call-update) | async-done | bytes 1179664 | tf_op jit(solution)/shard_map/reduce_scatter | solution.py:210
  2220.1 376.2 %reduce-scatter.29.cloned.1.call-done = f32[216,1536]{1,0:T(8,128)} async-done(((f32[6912,1536]{1,0:T(8,128)}), f32[216,1536]{1,0:T(8,128)}) %reduce-scatter.29.cloned.1.call-update) | async-done | bytes 1327120 | tf_op jit(solution)/shard_map/reduce_scatter | solution.py:173
  2596.3 385.5 %reduce-scatter.27.cloned.1.call-done = f32[216,1536]{1,0:T(8,128)} async-done(((f32[6912,1536]{1,0:T(8,128)}), f32[216,1536]{1,0:T(8,128)}) %reduce-scatter.27.cloned.1.call-update) | async-done | bytes 1327120 | tf_op jit(solution)/shard_map/reduce_scatter | solution.py:173
  2987.8 717.9 %reduce-scatter.25.cloned.1.call-done = f32[48,13824]{1,0:T(8,128)} async-done(((f32[1536,13824]{1,0:T(8,128)}), f32[48,13824]{1,0:T(8,128)}) %reduce-scatter.25.cloned.1.call-update) | async-done | bytes 2654224 | tf_op jit(solution)/shard_map/reduce_scatter | solution.py:176
  3705.7 725.3 %reduce-scatter.23.cloned.1.call-done = f32[48,13824]{1,0:T(8,128)} async-done(((f32[1536,13824]{1,0:T(8,128)}), f32[48,13824]{1,0:T(8,128)}) %reduce-scatter.23.cloned.1.call-update) | async-done | bytes 2654224 | tf_op jit(solution)/shard_map/reduce_scatter | solution.py:176
  (270 shorter events, 191.4 us)
Async XLA Ops:
  7.2 332.4 %all-gather.17.cloned.1.call-start = ((), (), s32[]{:S(2)}) async-start(), calls=%async_computation.16 | async-start | bytes 19464192 | tf_op jit(solution)/shard_map/all_gather | solution.py:48
  10.1 452.6 %all-gather.19.cloned.1.call-start = ((), (), s32[]{:S(2)}) async-start(), calls=%async_computation.17 | async-start | bytes 43794432 | tf_op jit(solution)/shard_map/all_gather | solution.py:49
  14.7 541.3 %all-gather.21.cloned.1.call-start = ((), (), s32[]{:S(2)}) async-start(), calls=%async_computation.18 | async-start | bytes 21897216 | tf_op jit(solution)/shard_map/all_gather | solution.py:50
  17.0 665.3 %all-gather.23.cloned.1.call-start = ((), (), s32[]{:S(2)}) async-start(), calls=%async_computation.19 | async-start | bytes 19464192 | tf_op jit(solution)/shard_map/all_gather | solution.py:48
  17.6 903.4 %all-gather.25.cloned.1.call-start = ((), (), s32[]{:S(2)}) async-start(), calls=%async_computation.20 | async-start | bytes 43794432 | tf_op jit(solution)/shard_map/all_gather | solution.py:49
  18.2 1039.8 %all-gather.27.cloned.1.call-start = ((), (), s32[]{:S(2)}) async-start(), calls=%async_computation.21 | async-start | bytes 21897216 | tf_op jit(solution)/shard_map/all_gather | solution.py:50
  18.8 1353.3 %reduce-scatter.37.cloned.1.call-start = ((), (), s32[]{:S(2)}) async-start(), calls=%async_computation.25 | async-start | bytes 811008
  19.1 249.0 %copy-start.22 = (bf16[1,128,1536]{2,1,0:T(8,128)(2,1)S(1)}, bf16[1,128,1536]{2,1,0:T(8,128)(2,1)}, u32[]{:S(2)}) copy-start(bf16[1,128,1536]{2,1,0:T(8,128)(2,1)} %param.17) | copy-start | bytes 1179652
  293.4 869.8 %copy-start.39 = (f32[1536]{0:T(1024)}, f32[1536]{0:T(1024)S(1)}, u32[]{:S(2)}) copy-start(f32[1536]{0:T(1024)S(1)} %get-tuple-element.87) | copy-start | bytes 18436
  339.6 117.7 %copy-start.50 = (f32[1536]{0:T(1024)}, f32[1536]{0:T(1024)S(1)}, u32[]{:S(2)}) copy-start(f32[1536]{0:T(1024)S(1)} %get-tuple-element.89) | copy-start | bytes 18436
  339.6 117.7 %copy-start.52 = (f32[1536]{0:T(1024)}, f32[1536]{0:T(1024)S(1)}, u32[]{:S(2)}) copy-start(f32[1536]{0:T(1024)S(1)} %get-tuple-element.90) | copy-start | bytes 18436
  339.6 117.7 %copy-start.53 = (f32[1536]{0:T(1024)}, f32[1536]{0:T(1024)S(1)}, u32[]{:S(2)}) copy-start(f32[1536]{0:T(1024)S(1)} %get-tuple-element.91) | copy-start | bytes 18436
  346.4 110.8 %collective-permute-start = (bf16[1,2,1536]{2,1,0:T(2,128)(2,1)S(1)}, bf16[1,2,1536]{2,1,0:T(2,128)(2,1)S(1)}, u32[]{:S(2)}, u32[]{:S(2)}) collective-permute-start(bf16[1,2,1536]{2,1,0:T(2,128)(2,1)S(1)} %slice.251), channel_id=1, source_target_pairs={{0,4},{4,8},{8,12},{12,16},{16,20},{20,24},{24,28},{1,5},{5,9},{9,... | collective-permute-start | bytes 18440 | tf_op jit(solution)/shard_map/ppermute | solution.py:22
  372.8 719.1 %copy-start.41 = (f32[1536]{0:T(1024)}, f32[1536]{0:T(1024)S(1)}, u32[]{:S(2)}) copy-start(f32[1536]{0:T(1024)S(1)} %get-tuple-element.82) | copy-start | bytes 18436
  462.7 700.5 %copy-start.46 = (f32[128]{0:T(128)}, f32[128]{0:T(128)S(1)}, u32[]{:S(2)}) copy-start(f32[128]{0:T(128)S(1)} %add_rsqrt_fusion.2) | copy-start | bytes 1540
  689.0 48.9 %collective-permute-start.1 = (bf16[1,2,1536]{2,1,0:T(2,128)(2,1)S(1)}, bf16[1,2,1536]{2,1,0:T(2,128)(2,1)S(1)}, u32[]{:S(2)}, u32[]{:S(2)}) collective-permute-start(bf16[1,2,1536]{2,1,0:T(2,128)(2,1)S(1)} %slice.272), channel_id=1, source_target_pairs={{0,4},{4,8},{8,12},{12,16},{16,20},{20,24},{24,28},{1,5},{5,9},{9,... | collective-permute-start | bytes 18440 | tf_op jit(solution)/shard_map/ppermute | solution.py:22
  743.4 348.6 %copy-start.48 = (f32[128]{0:T(128)}, f32[128]{0:T(128)S(1)}, u32[]{:S(2)}) copy-start(f32[128]{0:T(128)S(1)} %add_rsqrt_fusion) | copy-start | bytes 1540
  1104.2 3.1 collective-permute-start.2
  1106.7 268.7 %reduce-scatter.33.cloned.1.call-start = ((), (), s32[]{:S(2)}) async-start(), calls=%async_computation.23 | async-start | bytes 811008
  1171.1 4.6 collective-permute-start.3
  1172.4 231.0 %reduce-scatter.35.cloned.1.call-start = ((), (), s32[]{:S(2)}) async-start(), calls=%async_computation.24 | async-start | bytes 811008
  1174.4 329.1 %reduce-scatter.31.cloned.1.call-start = ((), (), s32[]{:S(2)}) async-start(), calls=%async_computation.22 | async-start | bytes 811008
  1189.9 666.8 %reduce-scatter.21.cloned.1.call-start = ((), (), s32[]{:S(2)}) async-start(), calls=%async_computation.11 | async-start | bytes 38928384 | tf_op jit(solution)/shard_map/reduce_scatter | solution.py:210
  1215.4 996.7 %reduce-scatter.19.cloned.1.call-start = ((), (), s32[]{:S(2)}) async-start(), calls=%async_computation.10 | async-start | bytes 38928384 | tf_op jit(solution)/shard_map/reduce_scatter | solution.py:210
  1258.1 1338.2 %reduce-scatter.29.cloned.1.call-start = ((), (), s32[]{:S(2)}) async-start(), calls=%async_computation.15 | async-start | bytes 43794432 | tf_op jit(solution)/shard_map/reduce_scatter | solution.py:173
  1276.2 1705.6 %reduce-scatter.27.cloned.1.call-start = ((), (), s32[]{:S(2)}) async-start(), calls=%async_computation.14 | async-start | bytes 43794432 | tf_op jit(solution)/shard_map/reduce_scatter | solution.py:173
  1295.3 2410.5 %reduce-scatter.25.cloned.1.call-start = ((), (), s32[]{:S(2)}) async-start(), calls=%async_computation.13 | async-start | bytes 87588864 | tf_op jit(solution)/shard_map/reduce_scatter | solution.py:176
  1328.0 3103.0 %reduce-scatter.23.cloned.1.call-start = ((), (), s32[]{:S(2)}) async-start(), calls=%async_computation.12 | async-start | bytes 87588864 | tf_op jit(solution)/shard_map/reduce_scatter | solution.py:176
  1361.2 143.1 %copy-start.63 = (f32[2,2,48]{2,1,0:T(2,128)S(1)}, f32[2,2,48]{2,1,0:T(2,128)}, u32[]{:S(2)}) copy-start(f32[2,2,48]{2,1,0:T(2,128)} %param.28) | copy-start | bytes 2308
  1361.2 143.1 %copy-start.66 = (f32[2,2,48]{2,1,0:T(2,128)S(1)}, f32[2,2,48]{2,1,0:T(2,128)}, u32[]{:S(2)}) copy-start(f32[2,2,48]{2,1,0:T(2,128)} %param.30) | copy-start | bytes 2308
  1361.2 143.1 %copy-start.67 = (f32[2,2,48]{2,1,0:T(2,128)S(1)}, f32[2,2,48]{2,1,0:T(2,128)}, u32[]{:S(2)}) copy-start(f32[2,2,48]{2,1,0:T(2,128)} %param.29) | copy-start | bytes 2308
  2212.1 769.8 %copy-start.14 = (f32[2,216,1536]{2,1,0:T(8,128)S(1)}, f32[2,216,1536]{2,1,0:T(8,128)}, u32[]{:S(2)}) copy-start(f32[2,216,1536]{2,1,0:T(8,128)} %param.25) | copy-start | bytes 7962628
  (57 other events, 936.7 us)
Sparse Core Ops, SparseCore 0:
  11.4 141.9 all-gather.16
  156.8 257.3 all-gather.18
  417.5 138.4 all-gather.20
  559.2 123.0 all-gather.22
  685.5 235.3 all-gather.24
  923.6 134.2 all-gather.26
  1106.8 97.0 reduce-scatter.36
  1209.0 94.5 reduce-scatter.32
  1308.8 94.5 reduce-scatter.34
  1408.9 94.5 reduce-scatter.30
  1509.9 346.6 reduce-scatter.20
  1864.1 347.9 reduce-scatter.18
  2218.5 377.8 reduce-scatter.28
  2603.8 378.0 reduce-scatter.26
  2988.1 717.6 reduce-scatter.24
  3713.2 717.8 reduce-scatter.22
where the time goes:
time: 4460 us; the launch traced here: 4450 us
  waiting for transfers between devices  3520 us (79%)
  blocking collectives  329 us (7%)
  matrix products  307 us (7%)
  local copies, waits for them, and re-layouts  168 us (4%)
  other arithmetic  104 us (2%)
    reduce_scatter x2, waiting for transfers between devices, block_backward(): lax.psum_scatter(column_term(normed_two, gate_up_flow), ('seq', 'fsdp'),...  1440 us
    reduce_scatter x2, waiting for transfers between devices, block_backward(): lax.psum_scatter(column_term(hidden, flow_low), ('seq', 'fsdp'), scatter_...  762 us
    reduce_scatter x2, waiting for transfers between devices, block_backward(): lax.psum_scatter(mix_fn(jnp.int32(0), features // all_devices * lax.axis_...  707 us
    all_gather x2, waiting for transfers between devices, gather_forward(): lax.all_gather(down_part, ('seq', 'fsdp'), axis=0, tiled=True)  187 us
    all_gather x2, waiting for transfers between devices, gather_forward(): lax.all_gather(feed_part, ('seq', 'fsdp'), axis=0, tiled=True)  178 us
    all_gather x2, blocking collectives, gather_forward(): lax.all_gather(gain_part, ('seq', 'fsdp'), axis=1, tiled=True)  165 us
    all_gather x2, blocking collectives, gather_forward(): lax.all_gather(tap_part, ('seq', 'fsdp'), axis=1, tiled=True)  164 us
    dot_general x8, matrix products, matmul_tn(): lax.dot_general(left, right, (((0,), (0,)), ((), ())), preferred_element_...  131 us
  transfers between devices with their start and end apart: 20, of which 14 were waited for; matrix products, arithmetic and copies ran while one was open for 11% of the time, Pallas kernels for 0%

commit v1 on v0

v1 whole, which is shorter than its diff:
```python
import jax
import jax.numpy as jnp
from jax import lax
from jax.experimental import pallas as pl
from jax.experimental.pallas import tpu as pltpu
from jax.sharding import PartitionSpec as P

LAYERS = 2
STEP = 10

eps_norm = 1e-05
eps_adam = 1e-08
beta_one = 0.9
beta_two = 0.95
rate_matrix = 0.05
rate_vector = 0.6
decay_matrix = 0.1

low = jnp.bfloat16


def dot(left, right, sides=((1,), (0,))):
    return lax.dot_general(left, right, (sides, ((), ())), preferred_element_type=jnp.float32)


nt = ((1,), (1,))
tn = ((0,), (0,))


def seq_order():
    count = lax.axis_size("seq")
    return list(range(0, count, 2)) + list(range(1, count, 2))


def seq_swap(array, by):
    count = lax.axis_size("seq")
    return lax.ppermute(array, "seq", [(i, i ^ by) for i in range(count)])


def send_seq(array):
    return [array] + [seq_swap(array, by) for by in range(2, lax.axis_size("seq"), 2)]


def fsdp_shift(array, by):
    count = lax.axis_size("fsdp")
    return lax.ppermute(array, "fsdp", [(i, (i + by) % count) for i in range(count)])


def gather_fsdp(array):
    count = lax.axis_size("fsdp")
    return [array] + [fsdp_shift(array, -by) for by in range(1, count)]


def small_scatter_seq(parts):
    half = parts.shape[0] // 2
    total = parts[:half] + seq_swap(parts[half:], 1)
    for i in range(1, half):
        total = total.at[0].add(seq_swap(total[i], 2 * i))
    return total[0]


def small_scatter_fsdp(parts):
    total = parts[0]
    for by in range(1, parts.shape[0]):
        total = total + fsdp_shift(parts[by], by)
    return total


def stack_pairs(blocks, earlier=(), carried=()):
    def body(*refs):
        for i in range(len(blocks)):
            refs[-1][i] = refs[i][...]

    shape = (len(blocks),) + blocks[0].shape
    even, *rest = plain_call(
        body, [shaped(shape, blocks[0].dtype)], earlier=earlier, carried=carried
    )(*blocks)
    return even, seq_swap(even, 1), *rest


def pad_last(array, width):
    return jnp.pad(array, [(0, 0)] * (array.ndim - 1) + [(0, width - array.shape[-1])])


def place_of(axis):
    return lax.axis_index(axis).astype(jnp.int32).reshape(1)


scalar = pl.BlockSpec(memory_space=pltpu.SMEM)
held = pl.BlockSpec(memory_space=pltpu.VMEM)


def shaped(shape, kind=jnp.float32):
    return jax.ShapeDtypeStruct(shape, kind)


class Order:
    mark = None


mark_shape = jax.ShapeDtypeStruct((8, 128), jnp.float32)
anywhere = pl.BlockSpec(memory_space=pl.ANY)


def ordered_call(body, operands, in_specs, out_specs, out_shape, aliases, scratch, grid, cost):
    given, made = len(operands), len(out_shape)

    def marked(*refs):
        body(*refs[:given], *refs[given + 1 : given + 1 + made], *refs[given + 2 + made :])

    outs = pl.pallas_call(
        marked,
        in_specs=list(in_specs) + [anywhere],
        out_specs=list(out_specs) + [anywhere],
        out_shape=list(out_shape) + [mark_shape],
        scratch_shapes=list(scratch),
        input_output_aliases=aliases,
        compiler_params=pltpu.CompilerParams(vmem_limit_bytes=56 * 1024 * 1024),
        cost_estimate=pl.CostEstimate(
            flops=cost[0], bytes_accessed=cost[1], transcendentals=0
        ),
        **grid,
    )(*operands, Order.mark)
    Order.mark = outs[-1]
    return outs[:-1]


def kernel_call(
    body, grid, in_specs, out_specs, out_shape, aliases=None, scratch=(), cost=(0, 0)
):
    single = not isinstance(out_shape, list)

    def run(*operands):
        outs = ordered_call(
            body,
            operands,
            in_specs,
            [out_specs] if single else out_specs,
            [out_shape] if single else out_shape,
            aliases or {},
            scratch,
            dict(grid=grid),
            cost,
        )
        return outs[0] if single else outs

    return run


def plain_call(
    body, out_shape, scalars=0, scratch=(), earlier=(), carried=(), cost=(0, 0)
):
    def run(*operands):
        given, made, more = len(operands), len(out_shape), len(earlier) + len(carried)

        def rest(*refs):
            outs = refs[given + more :]
            body(*refs[:given], *outs[:made], *outs[made + len(carried) :])

        first = given + len(earlier)
        return ordered_call(
            rest,
            (*operands, *earlier, *carried),
            [scalar] * scalars + [held] * (given - scalars) + [anywhere] * more,
            [held] * made + [anywhere] * len(carried),
            [*out_shape, *(jax.ShapeDtypeStruct(x.shape, x.dtype) for x in carried)],
            {first + i: made + i for i in range(len(carried))},
            scratch,
            {},
            cost,
        )

    return run


def whole(shape):
    return pl.BlockSpec(shape, lambda i: (0,) * len(shape))


def pack_mix(mix_weight, layer, wide):
    seqs = lax.axis_size("seq")
    rows, columns = mix_weight.shape[1:]
    features = columns // 4
    chunk = features // seqs
    outer = features // (3 * wide)

    def body(place, weight, out):
        for s in range(seqs):
            slot = lax.bitwise_xor(place[0], jnp.int32(s))
            for g in range(3):
                start = g * features + s * chunk
                piece = weight[0, :, start : start + chunk].astype(low)
                if wide > chunk:
                    piece = jnp.concatenate([piece, jnp.zeros((rows, wide - chunk), low)], axis=1)
                out[slot, :, g * wide : (g + 1) * wide] = piece
        for i in range(outer):
            start = 3 * features + i * 3 * wide
            out[seqs + i] = weight[0, :, start : start + 3 * wide].astype(low)

    shape = (seqs + outer, rows, 3 * wide)
    return kernel_call(
        body,
        (1,),
        [scalar, pl.BlockSpec((1, rows, columns), lambda i: (layer, 0, 0))],
        whole(shape),
        jax.ShapeDtypeStruct(shape, low),
    )(place_of("seq"), mix_weight)


def assemble_mix(pieces, wide, features):
    seqs, rings = lax.axis_size("seq"), lax.axis_size("fsdp")
    outer, rows, _ = pieces[0].shape
    outer = outer - seqs
    rotated = isinstance(pieces, list)
    pieces = pieces if rotated else [pieces]

    def body(place_seq, place_fsdp, *refs):
        inner_out, outer_out = refs[-2:]
        refs = refs if rotated else [refs[0].at[j] for j in range(rings)]
        for j in range(rings):
            f = lax.rem(place_fsdp[0] + j, rings) if rotated else j
            for s in range(seqs):
                inner_out[lax.bitwise_xor(place_seq[0], jnp.int32(s)), f] = refs[j][s]
            for i in range(outer):
                outer_out[f, :, i * 3 * wide : (i + 1) * 3 * wide] = refs[j][seqs + i]

    inner_shape = (seqs, rings, rows, 3 * wide)
    outer_shape = (rings, rows, features)
    inner, out = plain_call(
        body, [shaped(inner_shape, low), shaped(outer_shape, low)], scalars=2
    )(place_of("seq"), place_of("fsdp"), *pieces)
    return inner.reshape(features, 3 * wide), out.reshape(rings * rows, features)


def swap_mix(packed):
    seqs = lax.axis_size("seq")
    return [packed[:1]] + [seq_swap(packed[by : by + 1], by) for by in range(1, seqs)]


def join_mix(parts, packed):
    seqs = len(parts)

    def body(*refs):
        out = refs[-1]
        for s in range(seqs):
            out[s] = refs[s][0]
        out[seqs:] = refs[seqs][seqs:]

    return plain_call(body, [shaped(packed.shape, low)])(*parts, packed)[0]


def tall_of(block):
    step = 128 // min(lax.axis_size("seq"), 128)
    return -(-block // step) * step


def pack_feed(feed_weight, layer):
    seqs, rings = lax.axis_size("seq"), lax.axis_size("fsdp")
    rows, columns = feed_weight.shape[1:]
    half = columns // 2
    block = half // (seqs * rings)
    tall = tall_of(block)

    def body(place, weight, out):
        for f in range(rings):
            slot = lax.rem(f - place[0] + rings, rings)
            for g in range(2):
                for s in range(seqs):
                    start = g * half + (s * rings + f) * block
                    piece = weight[0, :, start : start + block].astype(low)
                    if tall > block:
                        piece = jnp.concatenate(
                            [piece, jnp.zeros((rows, tall - block), low)], axis=1
                        )
                    to = (g * seqs + s) * tall
                    out[slot, :, to : to + tall] = piece

    shape = (rings, rows, 2 * seqs * tall)
    return kernel_call(
        body,
        (1,),
        [scalar, pl.BlockSpec((1, rows, columns), lambda i: (layer, 0, 0))],
        whole(shape),
        jax.ShapeDtypeStruct(shape, low),
    )(place_of("fsdp"), feed_weight)


def assemble_feed(pieces):
    rings = len(pieces)

    def body(place, *refs):
        out = refs[rings]
        for j in range(rings):
            out[lax.rem(place[0] - j + rings, rings)] = refs[j][0]

    shape = (rings,) + pieces[0].shape[1:]
    return kernel_call(
        body,
        (1,),
        [scalar] + [whole(piece.shape) for piece in pieces],
        whole(shape),
        jax.ShapeDtypeStruct(shape, low),
    )(place_of("fsdp"), *pieces)


def swap_feed(packed):
    rings = lax.axis_size("fsdp")
    return [packed[:1]] + [fsdp_shift(packed[by : by + 1], by) for by in range(1, rings)]


def gather_rows(part):
    return lax.all_gather(part.reshape(-1, part.shape[-1]), "seq", axis=0, tiled=True)


def pack_down(down_weight, layer):
    block = down_weight.shape[1]
    return jnp.pad(down_weight[layer].astype(low), ((0, tall_of(block) - block), (0, 0)))


def adam_kernel(load, scalars, grads, state, layer, previous, scratch=()):
    weight = state[0]
    rows, columns = weight.shape[1:]
    tile = 16 if rows % 16 == 0 else rows
    width = 768
    specs = [pl.BlockSpec((tile, grad.shape[-1]), lambda i: (i, 0)) for grad in grads]
    part = pl.BlockSpec((1, tile, columns), lambda i: (layer, i, 0))
    kept = 0 if previous is None else 3
    before = len(scalars) + len(grads)

    def body(*refs):
        weight, first, second = refs[before : before + 3]
        weight_out, first_out, second_out, total = refs[before + 3 + kept : before + 7 + kept]
        load(refs[: len(scalars)], refs[len(scalars) : before], refs[before + 7 + kept :], total)
        for start in range(0, columns, width):
            at = slice(start, start + width)
            gradient = total[:, at]
            old = weight[0, :, at]
            first_new = beta_one * first[0, :, at] + (1.0 - beta_one) * gradient
            second_new = beta_two * second[0, :, at] + (1.0 - beta_two) * gradient * gradient
            first_hat = first_new / (1.0 - beta_one**STEP)
            second_hat = second_new / (1.0 - beta_two**STEP)
            step = first_hat / (jnp.sqrt(second_hat) + eps_adam) + decay_matrix * old
            first_out[0, :, at] = first_new
            second_out[0, :, at] = second_new
            weight_out[0, :, at] = old - rate_matrix * step

    return kernel_call(
        body,
        (rows // tile,),
        [scalar] * len(scalars)
        + specs
        + [part] * 3
        + [anywhere] * kept,
        [part] * 3,
        [shaped(weight.shape)] * 3,
        aliases={before + 3 + i: i for i in range(kept)},
        scratch=[pltpu.VMEM((tile, columns), jnp.float32), *(make(tile) for make in scratch)],
        cost=(0, 26 * rows * columns),
    )(*scalars, *grads, *state, *(previous or ()))


def mix_reduce(pieces):
    seqs, rings = lax.axis_size("seq"), lax.axis_size("fsdp")
    count, rows, width = pieces[0].shape
    outer = count - seqs

    def body(place, *refs):
        inner_out, outer_out = refs[rings:]
        for s in range(seqs):
            total = refs[0][s].astype(jnp.float32)
            for j in range(1, rings):
                total = total + refs[j][s].astype(jnp.float32)
            inner_out[lax.bitwise_xor(place[0], jnp.int32(s))] = total.astype(low)
        for i in range(outer):
            total = refs[0][seqs + i].astype(jnp.float32)
            for j in range(1, rings):
                total = total + refs[j][seqs + i].astype(jnp.float32)
            outer_out[:, i * width : (i + 1) * width] = total

    inner, last = plain_call(
        body,
        [shaped((seqs, rows, width), low), shaped((rows, outer * width))],
        scalars=1,
    )(place_of("seq"), *pieces)
    return [inner[0]] + [seq_swap(inner[j], j) for j in range(1, seqs)] + [last]


def mix_adam(grads, state, layer, previous, wide):
    seqs = lax.axis_size("seq")
    features = state[0].shape[2] // 4
    chunk = features // seqs

    def load(scalars, grads, scratch, total):
        for s in range(seqs):
            scratch[0][lax.bitwise_xor(scalars[0][0], jnp.int32(s))] = grads[s][...]
        for s in range(seqs):
            for g in range(3):
                start = g * features + s * chunk
                piece = scratch[0][s, :, g * wide : g * wide + chunk]
                total[:, start : start + chunk] = piece.astype(jnp.float32)
        total[:, 3 * features :] = grads[seqs][...]

    return adam_kernel(
        load,
        [place_of("seq")],
        grads,
        state,
        layer,
        previous,
        [lambda tile: pltpu.VMEM((seqs, tile, 3 * wide), low)],
    )


def scatter_rows(grad):
    return lax.psum_scatter(grad, "seq", scatter_dimension=0, tiled=True)


def split_feed(part, rows):
    rings = lax.axis_size("fsdp")
    part = part.reshape(rings, rows, -1)

    def body(place, part, *outs):
        for j in range(rings):
            outs[j][...] = part[lax.rem(place[0] + j, rings)]

    pieces = plain_call(body, [shaped(part.shape[1:], low)] * rings, scalars=1)(
        place_of("fsdp"), part
    )
    return return_sums(pieces)


def feed_adam(grads, state, layer, previous):
    seqs, rings = lax.axis_size("seq"), lax.axis_size("fsdp")
    half = state[0].shape[2] // 2
    block = half // (seqs * rings)
    tall = tall_of(block)

    def load(scalars, grads, scratch, total):
        for j in range(rings):
            scratch[0][lax.rem(scalars[0][0] - j + rings, rings)] = grads[j][...]
        for f in range(rings):
            for g in range(2):
                for s in range(seqs):
                    start = g * half + (s * rings + f) * block
                    at = (g * seqs + s) * tall
                    piece = scratch[0][f, :, at : at + block]
                    total[:, start : start + block] = piece.astype(jnp.float32)

    return adam_kernel(
        load,
        [place_of("fsdp")],
        grads,
        state,
        layer,
        previous,
        [lambda tile: pltpu.VMEM((rings, tile, 2 * seqs * tall), low)],
    )


def down_adam(part, state, layer, previous):
    part = part[: state[0].shape[1]]

    def load(scalars, grads, scratch, total):
        total[...] = grads[0][...].astype(jnp.float32)

    return adam_kernel(load, [], [part], state, layer, previous)


def place_blocks(blocks, owners, place, earlier=()):
    def body(place, *refs):
        if len(blocks[0].shape) == len(refs[-1].shape):
            refs = [ref.at[i] for ref in refs[:-1] for i in range(ref.shape[0])] + [refs[-1]]
        for block, owner in zip(refs, owners(place[0])):
            refs[-1][owner] = block[...]

    shape = blocks[0].shape
    if len(blocks) == 2:
        shape = (2 * shape[0],) + shape[1:]
    else:
        shape = (len(blocks),) + shape
    return plain_call(body, [shaped(shape, blocks[0].dtype)], scalars=1, earlier=earlier)(
        place, *blocks
    )[0]


def vectors_start(gain_weight, tap_weight):
    gains = gain_weight.reshape(2 * LAYERS, -1)
    taps = tap_weight.reshape(3 * LAYERS, -1)
    return gather_fsdp(jnp.concatenate([gains, taps], axis=0).astype(low))


def vectors_middle(blocks, earlier):
    rings = lax.axis_size("fsdp")
    both = place_blocks(
        blocks,
        lambda place: [lax.rem(place + j, rings) for j in range(rings)],
        place_of("fsdp"),
        earlier,
    )
    return both, send_seq(both)


def vectors_end(both, blocks):
    spread = place_blocks(
        stack_pairs(blocks),
        lambda place: [lax.bitwise_xor(place, jnp.int32(i)) for i in seq_order()],
        place_of("seq"),
    )
    gains = jnp.transpose(spread[:, :, : 2 * LAYERS], (2, 0, 1, 3)).astype(jnp.float32)
    taps = jnp.transpose(both[:, 2 * LAYERS :], (1, 0, 2)).astype(jnp.float32)
    return gains.reshape(LAYERS, 2, 1, -1), taps.reshape(LAYERS, 3, -1)


def vector_gradients(gain_grads, tap_grads, short):
    seqs, rings = lax.axis_size("seq"), lax.axis_size("fsdp")
    place_seq, place_fsdp = lax.axis_index("seq"), lax.axis_index("fsdp")
    gains = gain_grads.reshape(2 * LAYERS, seqs, -1)
    owner = place_seq ^ jnp.array(seq_order())
    pick = (owner[:, None] == jnp.arange(seqs)[None, :]).astype(jnp.float32)
    gains = jnp.einsum("jo,koc->jkc", pick, gains, precision=lax.Precision.HIGHEST)
    gains = small_scatter_seq(gains)
    taps = tap_grads.reshape(3 * LAYERS, -1)[:, : rings * short]
    both = jnp.concatenate([gains, taps], axis=0).reshape(5 * LAYERS, rings, short)
    owner = (place_fsdp + jnp.arange(rings)) % rings
    pick = (owner[:, None] == jnp.arange(rings)[None, :]).astype(jnp.float32)
    both = jnp.einsum("jo,koc->jkc", pick, both, precision=lax.Precision.HIGHEST)
    both = small_scatter_fsdp(both)
    return (
        both[: 2 * LAYERS].reshape(LAYERS, 2, short),
        both[2 * LAYERS :].reshape(LAYERS, 3, short),
    )


def unit_rows(values):
    row_scale = lax.rsqrt(jnp.mean(values * values, axis=-1, keepdims=True) + eps_norm)
    return values * row_scale, row_scale


def first_norm(inputs, gain, earlier):
    def body(inputs, gain, stream_out, normed_out):
        stream = inputs[...].astype(jnp.float32)
        stream_out[...] = stream
        normed_out[...] = (unit_rows(stream)[0] * gain[...]).astype(low)

    return plain_call(
        body, [shaped(inputs.shape), shaped(inputs.shape, low)], earlier=earlier
    )(inputs, gain)


def finish(base, sums, gain):
    def body(*refs):
        total = refs[0][...]
        for part in refs[1 : 1 + len(sums)]:
            total = total + part[...].astype(jnp.float32)
        if gain is None:
            refs[-1][...] = total.astype(low)
        else:
            refs[-2][...] = total
            refs[-1][...] = (unit_rows(total)[0] * refs[1 + len(sums)][...]).astype(low)

    if gain is None:
        return plain_call(body, [shaped(base.shape, low)])(base, *sums)[0]
    return plain_call(body, [shaped(base.shape), shaped(base.shape, low)])(base, *sums, gain)


def finish_back(flow, sums, stream, gain, carried=()):
    def body(flow, stream, gain, *refs):
        total = refs[0][...].astype(jnp.float32)
        for part in refs[1 : len(sums)]:
            total = total + part[...].astype(jnp.float32)
        unit, row_scale = unit_rows(stream[...])
        scaled = total * gain[...]
        inner_mean = jnp.mean(scaled * unit, axis=-1, keepdims=True)
        result = flow[...].astype(jnp.float32) + row_scale * (scaled - unit * inner_mean)
        refs[-3][...] = result
        refs[-2][...] = result.astype(low)
        refs[-1][...] = jnp.sum(total * unit, axis=0, keepdims=True)

    return plain_call(
        body,
        [shaped(flow.shape), shaped(flow.shape, low), shaped((1, flow.shape[1]))],
        carried=carried,
    )(flow, stream, gain, *sums)


def pair_sum(even, received):
    half, tokens, features = even.shape

    def body(even, received, *outs):
        for i in range(half):
            total = even[i] + received[i].astype(jnp.float32)
            outs[i][...] = total.astype(outs[i].dtype)

    outs = plain_call(
        body,
        [shaped((tokens, features))] + [shaped((tokens, features), low)] * (half - 1),
    )(even, received)
    return [outs[0]] + [seq_swap(outs[i], 2 * i) for i in range(1, half)]


def block_neighbour(place, i, count, step):
    order = list(range(0, count, 2)) + list(range(1, count, 2))
    owner = lax.bitwise_xor(place, jnp.int32(order[i])) + step
    inside = jnp.logical_and(owner >= 0, owner < count)
    number = lax.bitwise_xor(place, jnp.where(inside, owner, place))
    return lax.div(number, 2) + lax.rem(number, 2) * (count // 2), inside


def conv_forward(place, taps, gated, i, count):
    here = gated[i]
    tokens, chunk = here.shape
    at, inside = block_neighbour(place, i, count, -1)
    before = jnp.where(inside, gated[at, tokens - 8 :, :], 0.0)
    row = lax.broadcasted_iota(jnp.int32, (tokens, chunk), 0)
    last, second = before[7:8, :], before[6:7, :]
    one = jnp.where(row == 0, last, pltpu.roll(here, 1, 0))
    two = jnp.where(row == 0, second, jnp.where(row == 1, last, pltpu.roll(here, 2, 0)))
    return taps[0:1, :] * two + taps[1:2, :] * one + taps[2:3, :] * here, one, two


def mixer_forward(blocks, inner, outer, taps):
    half, tokens, features = blocks[0].shape
    count = 2 * half
    chunk = outer.shape[0]
    wide = inner.shape[1] // 3

    def body(place, even_in, odd_in, inner, outer, taps, *refs):
        projected, even, odd, gated, mixed = refs
        for k, rows in enumerate((even_in, odd_in)):
            rows = rows[...].reshape(half * tokens, features)
            for g in range(3):
                columns = slice(g * wide, (g + 1) * wide)
                part = dot(rows, inner[:, columns]).reshape(half, tokens, wide)
                projected[k * half : (k + 1) * half, :, columns] = part

        for i in range(count):
            product = projected[i, :, :wide] * projected[i, :, 2 * wide :]
            gated[i] = product[:, :chunk].astype(low).astype(jnp.float32)
        taps = taps[...]
        for i in range(count):
            conv_out = conv_forward(place[0], taps, gated, i, count)[0]
            mixed[i] = (projected[i, :, wide : wide + chunk] * conv_out).astype(low)
        rows = mixed[:half].reshape(half * tokens, chunk)
        even[...] = dot(rows, outer[...]).reshape(half, tokens, features)
        rows = mixed[half:].reshape(half * tokens, chunk)
        odd[...] = dot(rows, outer[...]).reshape(half, tokens, features).astype(low)

    return plain_call(
        body,
        [
            shaped((count, tokens, 3 * wide)),
            shaped((half, tokens, features)),
            shaped((half, tokens, features), low),
        ],
        scalars=1,
        scratch=[
            pltpu.VMEM((count, tokens, chunk), jnp.float32),
            pltpu.VMEM((count, tokens, chunk), low),
        ],
    )(place_of("seq"), *blocks, inner, outer, taps)


def mixer_backward(blocks, projected, inner, outer, taps):
    half, tokens, features = blocks[0].shape
    count = 2 * half
    chunk = outer.shape[0]
    wide = inner.shape[1] // 3

    def body(place, even_in, odd_in, projected, inner, outer, taps, *refs):
        even, odd, flows, mixed, tap_out, gated, flow = refs
        for i in range(count):
            product = projected[i, :, :wide] * projected[i, :, 2 * wide :]
            gated[i] = product[:, :chunk].astype(low).astype(jnp.float32)
        taps = taps[...]
        tap_sums = [jnp.zeros((1, chunk), jnp.float32)] * 3
        for k in range(2):
            rows = (even_in, odd_in)[k][...].reshape(half * tokens, features)
            back = dot(rows, outer[...], nt).reshape(half, tokens, chunk)
            for i in range(k * half, (k + 1) * half):
                conv_out, one, two = conv_forward(place[0], taps, gated, i, count)
                gate = projected[i, :, wide : wide + chunk]
                mixed[i] = (gate * conv_out).astype(low)
                mixed_flow = back[i - k * half]
                conv_flow = mixed_flow * gate
                flow[i] = conv_flow
                for j, shifted in enumerate((two, one, gated[i])):
                    term = jnp.sum(conv_flow * shifted, axis=0, keepdims=True)
                    tap_sums[j] = tap_sums[j] + term
                flows[i, :, wide : wide + chunk] = (mixed_flow * conv_out).astype(low)
        for j in range(3):
            tap_out[j : j + 1, :] = tap_sums[j]
        row = lax.broadcasted_iota(jnp.int32, (tokens, chunk), 0)
        for i in range(count):
            here = flow[i]
            at, inside = block_neighbour(place[0], i, count, 1)
            beyond = jnp.where(inside, flow[at, :8, :], 0.0)
            first, second = beyond[0:1, :], beyond[1:2, :]
            one = jnp.where(row == tokens - 1, first, pltpu.roll(here, tokens - 1, 0))
            two = jnp.where(
                row == tokens - 1,
                second,
                jnp.where(row == tokens - 2, first, pltpu.roll(here, tokens - 2, 0)),
            )
            gated_flow = taps[2:3, :] * here + taps[1:2, :] * one + taps[0:1, :] * two
            x_part = projected[i, :, 2 * wide : 2 * wide + chunk]
            b_part = projected[i, :, :chunk]
            flows[i, :, :chunk] = (gated_flow * x_part).astype(low)
            flows[i, :, 2 * wide : 2 * wide + chunk] = (gated_flow * b_part).astype(low)
            if wide > chunk:
                for g in range(3):
                    gap = jnp.zeros((tokens, wide - chunk), low)
                    flows[i, :, g * wide + chunk : (g + 1) * wide] = gap
        rows = flows[:half].reshape(half * tokens, 3 * wide)
        even[...] = dot(rows, inner[...], nt).reshape(half, tokens, features)
        rows = flows[half:].reshape(half * tokens, 3 * wide)
        odd[...] = dot(rows, inner[...], nt).reshape(half, tokens, features).astype(low)

    return plain_call(
        body,
        [
            shaped((half, tokens, features)),
            shaped((half, tokens, features), low),
            shaped((count, tokens, 3 * wide), low),
            shaped((count, tokens, chunk), low),
            shaped((3, chunk)),
        ],
        scalars=1,
        scratch=[pltpu.VMEM((count, tokens, chunk), jnp.float32)] * 2,
    )(place_of("seq"), *blocks, projected, inner, outer, taps)


def mixer_grads(normed, flows, mixed, lows, rows):
    seqs, rings = lax.axis_size("seq"), lax.axis_size("fsdp")
    features, width = normed[0].shape[-1], flows.shape[-1]
    half = normed[0].shape[0]
    wide = width // 3
    count = features // width

    def body(place, normed_even, normed_odd, flows, mixed, low_even, low_odd, *refs):
        outs, inner, outer = refs[:rings], refs[rings], refs[rings + 1]
        long = lambda array: array.reshape(-1, array.shape[-1])
        for g in range(3):
            at = slice(g * wide, (g + 1) * wide)
            part = dot(long(normed_even[...]), long(flows[:half, :, at]), tn)
            part = part + dot(long(normed_odd[...]), long(flows[half:, :, at]), tn)
            part = part.astype(low)
            for i in range(seqs * rings):
                inner[i // rings, i % rings, :, at] = part[i * rows : (i + 1) * rows]
        part = dot(long(mixed[:half]), long(low_even[...]), tn)
        part = part + dot(long(mixed[half:]), long(low_odd[...]), tn)
        part = part.astype(low)
        for f in range(rings):
            outer[f] = part[f * rows : (f + 1) * rows]
        for j in range(rings):
            f = lax.rem(place[0] + j, rings)
            for s in range(seqs):
                outs[j][s] = inner[s, f]
            for i in range(count):
                outs[j][seqs + i] = outer[f, :, i * width : (i + 1) * width]

    return plain_call(
        body,
        [shaped((seqs + count, rows, width), low)] * rings,
        scalars=1,
        scratch=[
            pltpu.VMEM((seqs, rings, rows, width), low),
            pltpu.VMEM((rings, rows, features), low),
        ],
        cost=(24 * half * normed[0].size, 8 * normed[0].size),
    )(place_of("fsdp"), *normed, flows, mixed, *lows)


def hidden_tile(hidden):
    return 256 if hidden % 256 == 0 else 128


def feed_specs(features, hidden):
    tile = hidden_tile(hidden)
    steps = hidden // tile
    return (
        pl.BlockSpec((features, tile), lambda i: (0, i)),
        pl.BlockSpec((features, tile), lambda i: (0, i + steps)),
        pl.BlockSpec((tile, features), lambda i: (i, 0)),
    )


def feed_forward(blocks, up_matrix, down, own):
    count = len(blocks)
    tokens, features = blocks[0].shape
    hidden = down.shape[0]
    tile = hidden_tile(hidden)
    steps = hidden // tile

    def body(*refs):
        gate_matrix, up_matrix, down = refs[count : count + 3]
        outs = refs[count + 3 : 2 * count + 3]
        gate_out, up_out, hidden_out, rows, total = refs[2 * count + 3 :]
        step = pl.program_id(0)

        @pl.when(step == 0)
        def _():
            for i in range(count):
                rows[i * tokens : (i + 1) * tokens] = refs[i][...]
            total[...] = jnp.zeros_like(total)

        gate = dot(rows[...], gate_matrix[...])
        up = dot(rows[...], up_matrix[...])
        gate_out[...] = gate
        up_out[...] = up
        value = (gate * jax.nn.sigmoid(gate) * up).astype(low)
        hidden_out[...] = value
        total[...] += dot(value, down[...])

        @pl.when(step == steps - 1)
        def _():
            for i in range(count):
                outs[i][...] = total[i * tokens : (i + 1) * tokens].astype(outs[i].dtype)

    columns = pl.BlockSpec((count * tokens, tile), lambda i: (0, i))
    outs = kernel_call(
        body,
        (steps,),
        [whole((tokens, features))] * count + list(feed_specs(features, hidden)),
        [whole((tokens, features))] * count + [columns] * 3,
        [
            shaped((tokens, features), jnp.float32 if own and i == 0 else low)
            for i in range(count)
        ]
        + [shaped((count * tokens, hidden), kind) for kind in (jnp.float32, jnp.float32, low)],
        scratch=[
            pltpu.VMEM((count * tokens, features), low),
            pltpu.VMEM((count * tokens, features), jnp.float32),
        ],
    )(*blocks, up_matrix, up_matrix, down)
    return outs[:count], outs[count:]


def feed_backward(blocks, gates, ups, up_matrix, down, own):
    count = len(blocks)
    tokens, features = blocks[0].shape
    hidden = down.shape[0]
    tile = hidden_tile(hidden)
    steps = hidden // tile

    def body(*refs):
        gate_part, up_part, gate_matrix, up_matrix, down = refs[count : count + 5]
        outs = refs[count + 5 : 2 * count + 5]
        gate_out, up_out, rows, total = refs[2 * count + 5 :]
        step = pl.program_id(0)

        @pl.when(step == 0)
        def _():
            for i in range(count):
                rows[i * tokens : (i + 1) * tokens] = refs[i][...]
            total[...] = jnp.zeros_like(total)

        flow = dot(rows[...], down[...], nt)
        gate = gate_part[...]
        smooth = jax.nn.sigmoid(gate)
        gate_flow = flow * up_part[...] * (smooth * (1.0 + gate * (1.0 - smooth)))
        gate_flow = gate_flow.astype(low)
        up_flow = (flow * (gate * smooth)).astype(low)
        gate_out[...] = gate_flow
        up_out[...] = up_flow
        total[...] += dot(gate_flow, gate_matrix[...], nt) + dot(up_flow, up_matrix[...], nt)

        @pl.when(step == steps - 1)
        def _():
            for i in range(count):
                outs[i][...] = total[i * tokens : (i + 1) * tokens].astype(outs[i].dtype)

    columns = pl.BlockSpec((count * tokens, tile), lambda i: (0, i))
    outs = kernel_call(
        body,
        (steps,),
        [whole((tokens, features))] * count + [columns] * 2 + list(feed_specs(features, hidden)),
        [whole((tokens, features))] * count + [columns] * 2,
        [
            shaped((tokens, features), jnp.float32 if own and i == 0 else low)
            for i in range(count)
        ]
        + [shaped((count * tokens, hidden), low)] * 2,
        scratch=[
            pltpu.VMEM((count * tokens, features), low),
            pltpu.VMEM((count * tokens, features), jnp.float32),
        ],
    )(*blocks, gates, ups, up_matrix, up_matrix, down)
    return outs[:count], outs[count:]


def feed_grads(normed, gate_flows, up_flows):
    count, groups = len(normed), len(gate_flows)
    tokens, features = normed[0].shape
    size, hidden = gate_flows[0].shape
    tile = hidden_tile(hidden)
    steps = hidden // tile

    def body(*refs):
        flows = refs[count : count + 2 * groups]
        out, rows, columns = refs[count + 2 * groups :]
        step = pl.program_id(0)

        @pl.when(step == 0)
        def _():
            for i in range(count):
                rows[i * tokens : (i + 1) * tokens] = refs[i][...]

        for half in range(2):

            @pl.when(lax.div(step, steps) == half)
            def _():
                for i in range(groups):
                    columns[i * size : (i + 1) * size] = flows[half * groups + i][...]

        out[...] = dot(rows[...], columns[...], tn).astype(low)

    gate_spec = pl.BlockSpec((size, tile), lambda i: (0, jnp.minimum(i, steps - 1)))
    up_spec = pl.BlockSpec((size, tile), lambda i: (0, jnp.maximum(i - steps, 0)))
    return kernel_call(
        body,
        (2 * steps,),
        [whole((tokens, features))] * count
        + [gate_spec] * groups
        + [up_spec] * groups,
        pl.BlockSpec((features, tile), lambda i: (0, i)),
        shaped((features, 2 * hidden), low),
        scratch=[
            pltpu.VMEM((count * tokens, features), low),
            pltpu.VMEM((groups * size, tile), low),
        ],
        cost=(12 * count * tokens * features * hidden, 24 * features * hidden),
    )(*normed, *gate_flows, *up_flows)


def down_grads(hiddens, flows):
    count, groups = len(flows), len(hiddens)
    tokens, features = flows[0].shape
    size, hidden = hiddens[0].shape
    tile = hidden_tile(hidden)

    def body(*refs):
        hiddens = refs[count : count + groups]
        out, rows, columns = refs[count + groups :]

        @pl.when(pl.program_id(0) == 0)
        def _():
            for i in range(count):
                rows[i * tokens : (i + 1) * tokens] = refs[i][...]

        for i in range(groups):
            columns[i * size : (i + 1) * size] = hiddens[i][...]
        out[...] = dot(columns[...], rows[...], tn).astype(low)

    return kernel_call(
        body,
        (hidden // tile,),
        [whole((tokens, features))] * count
        + [pl.BlockSpec((size, tile), lambda i: (0, i))] * groups,
        pl.BlockSpec((tile, features), lambda i: (i, 0)),
        shaped((hidden, features), low),
        scratch=[
            pltpu.VMEM((count * tokens, features), low),
            pltpu.VMEM((groups * size, tile), low),
        ],
        cost=(6 * count * tokens * features * hidden, 12 * features * hidden),
    )(*flows, *hiddens)


def join_blocks(blocks):
    def body(*refs):
        for i in range(len(blocks)):
            refs[len(blocks) + i][...] = refs[i][...]

    return plain_call(body, [shaped(block.shape, block.dtype) for block in blocks])(*blocks)


def groups_of(blocks):
    return [blocks[i : i + 2] for i in range(0, len(blocks), 2)]


def return_sums(sums):
    return [sums[0]] + [fsdp_shift(sums[j], j) for j in range(1, len(sums))]


def adam_update(weight, first, second, gradient, rate, decay):
    first_new = beta_one * first + (1.0 - beta_one) * gradient
    second_new = beta_two * second + (1.0 - beta_two) * gradient * gradient
    first_hat = first_new / (1.0 - beta_one**STEP)
    second_hat = second_new / (1.0 - beta_two**STEP)
    weight_new = weight - rate * (first_hat / (jnp.sqrt(second_hat) + eps_adam) + decay * weight)
    return (first_new, second_new, weight_new)


def local(
    inputs,
    cotangent,
    mix_weight,
    mix_first,
    mix_second,
    feed_weight,
    feed_first,
    feed_second,
    down_weight,
    down_first,
    down_second,
    gain_weight,
    gain_first,
    gain_second,
    tap_weight,
    tap_first,
    tap_second,
):
    sequences, length, features = inputs.shape
    seqs, rings = lax.axis_size("seq"), lax.axis_size("fsdp")
    rows = mix_weight.shape[1]
    chunk = features // seqs
    wide = -(-chunk // 128) * 128
    cotangent = cotangent.reshape(-1, features)
    Order.mark = jnp.zeros(mark_shape.shape, mark_shape.dtype)

    feed_swaps, mixes, feeds = [None] * LAYERS, [None] * LAYERS, [None] * LAYERS
    feed_swaps[0] = swap_feed(pack_feed(feed_weight, 0))
    mix_packed = pack_mix(mix_weight, 0, wide)
    mix_swap = swap_mix(mix_packed)
    down_rows = gather_rows(pack_down(down_weight, 0))
    vector_blocks = vectors_start(gain_weight, tap_weight)
    mix_pieces = gather_fsdp(join_mix(mix_swap, mix_packed))
    feeds[0] = (gather_rows(assemble_feed(feed_swaps[0])), down_rows)
    both, vector_blocks = vectors_middle(vector_blocks, mix_pieces[1:2])
    gain_rows, tap_rows = vectors_end(both, vector_blocks)
    stream, normed = first_norm(
        inputs.reshape(-1, features), gain_rows[0, 0], mix_pieces[2:-1]
    )
    blocks = send_seq(normed)
    later_packed = pack_mix(mix_weight, 1, wide)
    blocks = stack_pairs(blocks)
    mixes[0] = assemble_mix(mix_pieces, wide, features)

    kept = []
    for layer in range(LAYERS):
        last = layer + 1 == LAYERS
        gathered = blocks
        projected, even, odd = mixer_forward(blocks, *mixes[layer], tap_rows[layer])
        odd = seq_swap(odd, 1)
        if last:
            flow_blocks = gather_fsdp(cotangent)
        sums = pair_sum(even, odd)
        if last:
            flow_low = join_blocks(flow_blocks)
        else:
            feed_swaps[1] = swap_feed(pack_feed(feed_weight, 1))
        middle, normed_two = finish(stream, sums, gain_rows[layer, 1])
        two_blocks = gather_fsdp(normed_two)
        if not last:
            later_mix = join_mix(swap_mix(later_packed), later_packed)
            later_mix = lax.all_gather(later_mix, "fsdp", axis=0)
            feeds[1] = (
                gather_rows(assemble_feed(feed_swaps[1])),
                gather_rows(pack_down(down_weight, 1)),
            )
        sums, values = [], []
        for number, group in enumerate(groups_of(two_blocks)):
            outs, saved = feed_forward(group, *feeds[layer], number == 0)
            sums += outs
            values.append(saved)
        kept.append((stream, middle, gathered, projected, two_blocks, values))
        sums = return_sums(sums)
        if not last:
            stream, normed = finish(middle, sums, gain_rows[layer + 1, 0])
            blocks = stack_pairs(send_seq(normed))
            mixes[1] = assemble_mix(later_mix, wide, features)

    states = (
        (mix_weight, mix_first, mix_second),
        (feed_weight, feed_first, feed_second),
        (down_weight, down_first, down_second),
    )
    new = [None] * 3
    gain_grads, tap_grads = [None] * LAYERS, [None] * LAYERS
    flow = cotangent
    for layer in reversed(range(LAYERS)):
        last = layer + 1 == LAYERS
        stream, middle, gathered, projected, two_blocks, values = kept[layer]
        back_sums, gate_flows, up_flows = [], [], []
        for number, group in enumerate(groups_of(flow_low)):
            gates, ups, _ = values[number]
            outs, (gate_flow, up_flow) = feed_backward(
                group, gates, ups, *feeds[layer], number == 0
            )
            back_sums += outs
            gate_flows.append(gate_flow)
            up_flows.append(up_flow)
        if last:
            outputs = finish(middle, sums, None).reshape(inputs.shape)
        back_sums = return_sums(back_sums)
        down_part = down_grads([value[2] for value in values], flow_low)
        middle_flow, middle_low, gain_two, down_part = finish_back(
            flow, back_sums, middle, gain_rows[layer, 1], [down_part]
        )
        down_part = scatter_rows(down_part)
        blocks = send_seq(middle_low)
        feed_part = feed_grads(two_blocks, gate_flows, up_flows)
        even, odd, feed_part = stack_pairs(
            blocks, () if last else later_mix[1::2], [feed_part]
        )
        feed_part = scatter_rows(feed_part)
        blocks = even, odd
        even, odd, flows, mixed, tap_grads[layer] = mixer_backward(
            blocks, projected, *mixes[layer], tap_rows[layer]
        )
        sums = pair_sum(even, seq_swap(odd, 1))
        mix_part = return_sums(mixer_grads(gathered, flows, mixed, blocks, rows))
        if not last:
            later_mix = mix_reduce(later_mix)
        flow, low_flow, gain_one = finish_back(middle_flow, sums, stream, gain_rows[layer, 0])
        gain_grads[layer] = jnp.concatenate([gain_one, gain_two])
        if last:
            flow_low = gather_fsdp(low_flow)
            later_mix, later_feed, later_down = mix_part, feed_part, down_part
    later_feed = split_feed(later_feed, rows)
    new[2] = down_adam(later_down, states[2], 1, new[2])
    new[0] = mix_adam(later_mix, states[0], 1, new[0], wide)
    gain_grad, tap_grad = vector_gradients(
        jnp.stack(gain_grads), jnp.stack(tap_grads), gain_weight.shape[-1]
    )
    new[1] = feed_adam(later_feed, states[1], 1, new[1])
    mix_part = mix_reduce(mix_part)
    new[2] = down_adam(down_part, states[2], 0, new[2])
    feed_part = split_feed(feed_part, rows)
    new[0] = mix_adam(mix_part, states[0], 0, new[0], wide)
    new[1] = feed_adam(feed_part, states[1], 0, new[1])
    input_grad = flow.reshape(sequences, length, features)
    gain_new = adam_update(gain_weight, gain_first, gain_second, gain_grad, rate_vector, 0.0)
    tap_new = adam_update(tap_weight, tap_first, tap_second, tap_grad, rate_vector, 0.0)
    matrices = [(part[1], part[2], part[0]) for part in new]
    return (outputs, input_grad, *sum(matrices, ()), *gain_new, *tap_new)


def solution(mesh):
    tokens = P("fsdp", "seq", None)
    rows = P(None, ("seq", "fsdp"), None)
    last = P(None, None, ("seq", "fsdp"))
    return jax.shard_map(
        local,
        mesh=mesh,
        in_specs=(tokens,) * 2 + (rows,) * 9 + (last,) * 6,
        out_specs=(tokens,) * 2 + (rows,) * 9 + (last,) * 6,
        check_vma=False,
    )
```

time: 4460 us -> 1110 us (0.25)
  waiting for transfers between devices: 3520 us -> 509 us
  Pallas kernels: 0 us -> 361 us
  blocking collectives: 329 us -> 0 us
  matrix products: 307 us -> 0.4 us
  starting transfers between devices: 6.79 us -> 146 us
  local copies, waits for them, and re-layouts: 168 us -> 57.6 us
  other arithmetic: 104 us -> 4.17 us
    reduce_scatter x6 -> x4, waiting for transfers between devices: 2910 us -> 0.04 us  [scatter_rows(): return lax.psum_scatter(grad, 'seq', scatter_dimension=0, tiled=True)]
    ppermute x4 -> x119, waiting for transfers between devices: 1.76 us -> 508 us  [the longest x51 391 us: fsdp_shift(): lax.ppermute(array, 'fsdp', [(i, (i + by) % count) for i in range(count)])]
    all_gather x6 -> x5, waiting for transfers between devices: 480 us -> 0.01 us  [the longest x4 0.01 us: gather_rows(): lax.all_gather(part.reshape(-1, part.shape[-1]), 'seq', axis=0, tiled=True)]
    pallas_call x0 -> x59, Pallas kernels: none -> 361 us  [ordered_call(): pl.pallas_call(marked, in_specs=list(in_specs) + [anywhere], out_specs=li...]
    all_gather x4 -> x0, blocking collectives: 329 us -> none  [the longest x2 165 us: gather_forward(): lax.all_gather(gain_part, ('seq', 'fsdp'), axis=1, tiled=True)]
    dot_general x24 -> x2, matrix products: 307 us -> 0.4 us  [the longest x1 0.21 us: vector_gradients(): jnp.einsum('jo,koc->jkc', pick, both, precision=lax.Precision.HIGHEST)]
    slice x13 -> x14, local copies, waits for them, and re-layouts: 148 us -> 9.5 us  [the longest x2 3.97 us: down_adam(): part = part[:state[0].shape[1]]]
    ppermute x4 -> x119, starting transfers between devices: 6.14 us -> 136 us  [the longest x51 69.5 us: fsdp_shift(): lax.ppermute(array, 'fsdp', [(i, (i + by) % count) for i in range(count)])]
  transfers between devices with their start and end apart: 20 -> 128, of which waited for: 14 -> 49; matrix products, arithmetic and copies ran while one was open for 11% -> 2% of each run, Pallas kernels for 0% -> 32%
where the time goes in v1:
time: 1110 us; the launch traced here: 1090 us
  waiting for transfers between devices  509 us (46%)
  Pallas kernels  361 us (33%)
  starting transfers between devices  146 us (13%)
  local copies, waits for them, and re-layouts  57.6 us (5%)
  between operations  15.5 us (1%)
    ppermute x51, waiting for transfers between devices, fsdp_shift(): lax.ppermute(array, 'fsdp', [(i, (i + by) % count) for i in range(count)])  391 us
    pallas_call x59, Pallas kernels, ordered_call(): pl.pallas_call(marked, in_specs=list(in_specs) + [anywhere], out_specs=li...  361 us
    ppermute x68, waiting for transfers between devices, seq_swap(): return lax.ppermute(array, 'seq', [(i, i ^ by) for i in range(count)])  117 us
    ppermute x51, starting transfers between devices, fsdp_shift(): lax.ppermute(array, 'fsdp', [(i, (i + by) % count) for i in range(count)])  69.5 us
    ppermute x68, starting transfers between devices, seq_swap(): return lax.ppermute(array, 'seq', [(i, i ^ by) for i in range(count)])  66.4 us
    unnamed x293, local copies, waits for them, and re-layouts  39.8 us
  transfers between devices with their start and end apart: 128, of which 49 were waited for; matrix products, arithmetic and copies ran while one was open for 2% of the time, Pallas kernels for 32%

profile of v1, /device:TPU:8, one launch (start us, length us, event | category | flops | bytes accessed | tf_op | source)
XLA Modules:
  0.0 1093.2 jit_solution(3335693619081679320)
XLA Ops:
  64.1 42.9 %collective-permute-done.refs_2_ = bf16[10,48]{1,0:T(8,128)(2,1)S(1)} collective-permute-done((bf16[10,48]{1,0:T(8,128)(2,1)S(1)}, bf16[10,48]{1,0:T(8,128)(2,1)S(1)}, u32[]{:S(2)}, u32[]{:S(2)}) %collective-permute-start) | collective-permute-done | bytes 992 | tf_op jit(solution)/shard_map/ppermute | solution.py:46
  152.9 17.2 %collective-permute-done.23.refs_5_ = bf16[10,48,768]{2,1,0:T(8,128)(2,1)S(1)} collective-permute-done((bf16[10,48,768]{2,1,0:T(8,128)(2,1)S(1)}, bf16[10,48,768]{2,1,0:T(8,128)(2,1)S(1)}, u32[]{:S(2)}, u32[]{:S(2)}) %collective-permute-start.23) | collective-permute-done | bytes 737312 | tf_op jit(solution)/shard_map/ppermute | solution.py:46
  199.8 15.4 %collective-permute-done.33.refs_2_ = bf16[1,48,768]{2,1,0:T(8,128)(2,1)S(1)} collective-permute-done((bf16[1,48,768]{2,1,0:T(8,128)(2,1)S(1)}, bf16[1,48,768]{2,1,0:T(8,128)(2,1)S(1)}, u32[]{:S(2)}, u32[]{:S(2)}) %collective-permute-start.33) | collective-permute-done | bytes 73760 | tf_op jit(solution)/shard_map/ppermute | solution.py:37
  239.6 10.9 collective-permute-done.29.refs_2_
  250.6 39.4 %collective-permute-done.30.refs_3_ = bf16[1,48,3584]{2,1,0:T(8,128)(2,1)S(1)} collective-permute-done((bf16[1,48,3584]{2,1,0:T(8,128)(2,1)S(1)}, bf16[1,48,3584]{2,1,0:T(8,128)(2,1)S(1)}, u32[]{:S(2)}, u32[]{:S(2)}) %collective-permute-start.30) | collective-permute-done | bytes 344096 | tf_op jit(solution)/shard_map/ppermute | solution.py:46
  290.0 15.2 %collective-permute-done.31.refs_4_ = bf16[1,48,3584]{2,1,0:T(8,128)(2,1)S(1)} collective-permute-done((bf16[1,48,3584]{2,1,0:T(8,128)(2,1)S(1)}, bf16[1,48,3584]{2,1,0:T(8,128)(2,1)S(1)}, u32[]{:S(2)}, u32[]{:S(2)}) %collective-permute-start.31) | collective-permute-done | bytes 344096 | tf_op jit(solution)/shard_map/ppermute | solution.py:46
  310.8 40.4 %collective-permute-done.28.refs_1_ = bf16[128,1536]{1,0:T(8,128)(2,1)S(1)} collective-permute-done((bf16[128,1536]{1,0:T(8,128)(2,1)S(1)}, bf16[128,1536]{1,0:T(8,128)(2,1)S(1)}, u32[]{:S(2)}, u32[]{:S(2)}) %collective-permute-start.28) | collective-permute-done | bytes 393248 | tf_op jit(solution)/shard_map/ppermute | solution.py:46
  351.9 13.2 %shard_map.322 = (f32[128,1536]{1,0:T(8,128)}, bf16[128,1536]{1,0:T(8,128)(2,1)}, f32[256,1792]{1,0:T(8,128)}, f32[256,1792]{1,0:T(8,128)}, bf16[256,1792]{1,0:T(8,128)(2,1)}, /*index=5*/f32[8,128]{1,0:T(8,128)}) custom-call(bf16[128,1536]{1,0:T(8,128)(2,1)} %get-tuple-element.300.refs_0_, bf16[128,1536]{1,0:T(8,128)(2,1)} %copy-done.70, ...), custom_call_target="tpu_custom_call" | custom-call | tf_op jit(solution)/shard_map/pallas_call | solution.py:111
  366.0 12.8 %shard_map.323 = (bf16[128,1536]{1,0:T(8,128)(2,1)}, bf16[128,1536]{1,0:T(8,128)(2,1)}, f32[256,1792]{1,0:T(8,128)}, f32[256,1792]{1,0:T(8,128)}, bf16[256,1792]{1,0:T(8,128)(2,1)}, /*index=5*/f32[8,128]{1,0:T(8,128)}) custom-call(bf16[128,1536]{1,0:T(8,128)(2,1)} %copy-done.71, bf16[128,1536]{1,0:T(8,128)(2,1)} %copy-done.72, ...), custom_call_target="tpu_custom_call" | custom-call | tf_op jit(solution)/shard_map/pallas_call | solution.py:111
  381.6 20.7 %collective-permute-done.42.refs_3_ = bf16[128,1536]{1,0:T(8,128)(2,1)S(1)} collective-permute-done((bf16[128,1536]{1,0:T(8,128)(2,1)}, bf16[128,1536]{1,0:T(8,128)(2,1)S(1)}, u32[]{:S(2)}, u32[]{:S(2)}) %collective-permute-start.42) | collective-permute-done | bytes 393248 | tf_op jit(solution)/shard_map/ppermute | solution.py:46
  412.5 14.0 %collective-permute-done.44.refs_1_ = bf16[128,1536]{1,0:T(8,128)(2,1)S(1)} collective-permute-done((bf16[128,1536]{1,0:T(8,128)(2,1)}, bf16[128,1536]{1,0:T(8,128)(2,1)S(1)}, u32[]{:S(2)}, u32[]{:S(2)}) %collective-permute-start.44) | collective-permute-done | bytes 393248 | tf_op jit(solution)/shard_map/ppermute | solution.py:37
  468.1 15.2 %collective-permute-done.53.refs_2_ = bf16[128,1536]{1,0:T(8,128)(2,1)S(1)} collective-permute-done((bf16[128,1536]{1,0:T(8,128)(2,1)S(1)}, bf16[128,1536]{1,0:T(8,128)(2,1)S(1)}, u32[]{:S(2)}, u32[]{:S(2)}) %collective-permute-start.53) | collective-permute-done | bytes 393248 | tf_op jit(solution)/shard_map/ppermute | solution.py:46
  502.2 34.0 %collective-permute-done.55.refs_1_ = bf16[128,1536]{1,0:T(8,128)(2,1)S(1)} collective-permute-done((bf16[128,1536]{1,0:T(8,128)(2,1)}, bf16[128,1536]{1,0:T(8,128)(2,1)S(1)}, u32[]{:S(2)}, u32[]{:S(2)}) %collective-permute-start.55) | collective-permute-done | bytes 393248 | tf_op jit(solution)/shard_map/ppermute | solution.py:46
  537.0 12.9 %shard_map.331 = (f32[128,1536]{1,0:T(8,128)}, bf16[128,1536]{1,0:T(8,128)(2,1)}, f32[256,1792]{1,0:T(8,128)}, f32[256,1792]{1,0:T(8,128)}, bf16[256,1792]{1,0:T(8,128)(2,1)}, /*index=5*/f32[8,128]{1,0:T(8,128)}) custom-call(bf16[128,1536]{1,0:T(8,128)(2,1)} %get-tuple-element.332.refs_0_, bf16[128,1536]{1,0:T(8,128)(2,1)} %copy-done.73, ...), custom_call_target="tpu_custom_call" | custom-call | tf_op jit(solution)/shard_map/pallas_call | solution.py:111
  550.8 12.8 %shard_map.332 = (bf16[128,1536]{1,0:T(8,128)(2,1)}, bf16[128,1536]{1,0:T(8,128)(2,1)}, f32[256,1792]{1,0:T(8,128)}, f32[256,1792]{1,0:T(8,128)}, bf16[256,1792]{1,0:T(8,128)(2,1)}, /*index=5*/f32[8,128]{1,0:T(8,128)}) custom-call(bf16[128,1536]{1,0:T(8,128)(2,1)} %copy-done.74, bf16[128,1536]{1,0:T(8,128)(2,1)} %copy-done.75, ...), custom_call_target="tpu_custom_call" | custom-call | tf_op jit(solution)/shard_map/pallas_call | solution.py:111
  565.7 14.7 %shard_map.333 = (f32[128,1536]{1,0:T(8,128)}, bf16[128,1536]{1,0:T(8,128)(2,1)}, bf16[256,1792]{1,0:T(8,128)(2,1)}, bf16[256,1792]{1,0:T(8,128)(2,1)}, f32[8,128]{1,0:T(8,128)}) custom-call(bf16[128,1536]{1,0:T(8,128)(2,1)} %get-tuple-element.344.refs_0_, bf16[128,1536]{1,0:T(8,128)(2,1)} %get-tuple-element.345.refs_1_, ...), custom_call_target="tpu_custom_call" | custom-call | tf_op jit(solution)/shard_map/pallas_call | solution.py:111
  581.8 14.5 %shard_map.334 = (bf16[128,1536]{1,0:T(8,128)(2,1)}, bf16[128,1536]{1,0:T(8,128)(2,1)}, bf16[256,1792]{1,0:T(8,128)(2,1)}, bf16[256,1792]{1,0:T(8,128)(2,1)}, f32[8,128]{1,0:T(8,128)}) custom-call(bf16[128,1536]{1,0:T(8,128)(2,1)} %get-tuple-element.340.refs_0_.refs_2_, bf16[128,1536]{1,0:T(8,128)(2,1)} %get-tuple-element.341.refs_1_.refs_3_, ...), custom_call_target="tpu_custom_call" | custom-call | tf_op jit(solution)/shard_map/pallas_call | solution.py:111
  624.2 15.7 %shard_map.338 = (bf16[1536,3584]{1,0:T(8,128)(2,1)}, f32[8,128]{1,0:T(8,128)}) custom-call(bf16[128,1536]{1,0:T(8,128)(2,1)} %get-tuple-element.332.refs_0_, bf16[128,1536]{1,0:T(8,128)(2,1)} %copy-done.73, bf16[128,1536]{1,0:T(8,128)(2,1)} %copy-done.74, bf16[128,1536]{1,0:T(8,128)(2,1)} %copy-done.75, bf16[256,1792]{1,0:T(8,128)(2,1)} %get-tuple-element.363.refs_4_, ...), custom_call_target="tpu_custom_call" | custom-call | flops 16911433728 | bytes 66060288 | tf_op jit(solution)/shard_map/pallas_call | solution.py:111
  644.2 9.5 reduce-scatter.11.cloned.1.call-start
  660.2 10.4 shard_map.340
  682.6 8.8 shard_map.342
  701.1 14.7 %collective-permute-done.71.refs_6_ = bf16[128,1536]{1,0:T(8,128)(2,1)S(1)} collective-permute-done((bf16[128,1536]{1,0:T(8,128)(2,1)}, bf16[128,1536]{1,0:T(8,128)(2,1)S(1)}, u32[]{:S(2)}, u32[]{:S(2)}) %collective-permute-start.71) | collective-permute-done | bytes 393248 | tf_op jit(solution)/shard_map/ppermute | solution.py:37
  725.5 23.8 %collective-permute-done.72.refs_1_ = bf16[128,1536]{1,0:T(8,128)(2,1)S(1)} collective-permute-done((bf16[128,1536]{1,0:T(8,128)(2,1)}, bf16[128,1536]{1,0:T(8,128)(2,1)S(1)}, u32[]{:S(2)}, u32[]{:S(2)}) %collective-permute-start.72) | collective-permute-done | bytes 393248 | tf_op jit(solution)/shard_map/ppermute | solution.py:46
  750.0 15.5 %shard_map.344 = (f32[128,1536]{1,0:T(8,128)}, bf16[128,1536]{1,0:T(8,128)(2,1)}, bf16[256,1792]{1,0:T(8,128)(2,1)}, bf16[256,1792]{1,0:T(8,128)(2,1)}, f32[8,128]{1,0:T(8,128)}) custom-call(bf16[128,1536]{1,0:T(8,128)(2,1)} %get-tuple-element.385.refs_0_, bf16[128,1536]{1,0:T(8,128)(2,1)} %copy-done.26, f32[256,1792]{1,0:T(8,128)} %get-tuple-element.386.refs_2_, ...), custom_call_target="tpu_custom_call" | custom-call | tf_op jit(solution)/shard_map/pallas_call | solution.py:111
  766.5 15.0 %shard_map.345 = (bf16[128,1536]{1,0:T(8,128)(2,1)}, bf16[128,1536]{1,0:T(8,128)(2,1)}, bf16[256,1792]{1,0:T(8,128)(2,1)}, bf16[256,1792]{1,0:T(8,128)(2,1)}, f32[8,128]{1,0:T(8,128)}) custom-call(bf16[128,1536]{1,0:T(8,128)(2,1)} %copy-done.27, bf16[128,1536]{1,0:T(8,128)(2,1)} %copy-done.28, f32[256,1792]{1,0:T(8,128)} %get-tuple-element.391.refs_2_, ...), custom_call_target="tpu_custom_call" | custom-call | tf_op jit(solution)/shard_map/pallas_call | solution.py:111
  792.0 9.5 collective-permute-done.76.refs_5_
  814.8 16.3 %shard_map.348 = (bf16[1536,3584]{1,0:T(8,128)(2,1)}, f32[8,128]{1,0:T(8,128)}) custom-call(bf16[128,1536]{1,0:T(8,128)(2,1)} %get-tuple-element.300.refs_0_, bf16[128,1536]{1,0:T(8,128)(2,1)} %copy-done.70, bf16[128,1536]{1,0:T(8,128)(2,1)} %copy-done.71, bf16[128,1536]{1,0:T(8,128)(2,1)} %copy-done.72, bf16[256,1792]{1,0:T(8,128)(2,1)} %get-tuple-element.405.refs_4_, ...), custom_call_target="tpu_custom_call" | custom-call | flops 16911433728 | bytes 66060288 | tf_op jit(solution)/shard_map/pallas_call | solution.py:111
  847.4 10.1 shard_map.350
  879.4 11.8 %collective-permute-done.88.refs_3_ = bf16[10,48,768]{2,1,0:T(8,128)(2,1)S(1)} collective-permute-done((bf16[10,48,768]{2,1,0:T(8,128)(2,1)S(1)}, bf16[10,48,768]{2,1,0:T(8,128)(2,1)S(1)}, u32[]{:S(2)}, u32[]{:S(2)}) %collective-permute-start.88) | collective-permute-done | bytes 737312 | tf_op jit(solution)/shard_map/ppermute | solution.py:46
  944.4 63.3 %collective-permute-done.93.refs_3_ = bf16[48,3584]{1,0:T(8,128)(2,1)S(1)} collective-permute-done((bf16[48,3584]{1,0:T(8,128)(2,1)}, bf16[48,3584]{1,0:T(8,128)(2,1)S(1)}, u32[]{:S(2)}, u32[]{:S(2)}) %collective-permute-start.93) | collective-permute-done | bytes 344096 | tf_op jit(solution)/shard_map/ppermute | solution.py:46
  1013.3 9.2 shard_map.358
  1077.0 9.2 shard_map.363
  (635 shorter events, 488.7 us)
Async XLA Ops:
  7.2 343.9 %all-gather.9.cloned.1.call-start = ((), (), s32[]{:S(2)}) async-start(), calls=%async_computation.5 | async-start | bytes 6193152 | tf_op jit(solution)/shard_map/all_gather | solution.py:312
  11.0 340.1 %all-gather.7.cloned.1.call-start = ((), (), s32[]{:S(2)}) async-start(), calls=%async_computation.4 | async-start | bytes 12386304 | tf_op jit(solution)/shard_map/all_gather | solution.py:312
  56.6 383.0 %all-gather.15.cloned.1.call-start = ((), (), s32[]{:S(2)}) async-start(), calls=%async_computation.12 | async-start | bytes 3686400 | tf_op jit(solution)/shard_map/all_gather | solution.py:1056
  56.7 50.3 %collective-permute-start.10 = (bf16[10,48,768]{2,1,0:T(8,128)(2,1)S(1)}, bf16[10,48,768]{2,1,0:T(8,128)(2,1)S(1)}, u32[]{:S(2)}, u32[]{:S(2)}) collective-permute-start(bf16[10,48,768]{2,1,0:T(8,128)(2,1)S(1)} %copy-done.18), channel_id=1, source_target_pairs={{0,3},{1,0},{2,1},{3,2},{4,7},{5,4},{6,5},{7,6},{8,11},{9,8},{10,9... | collective-permute-start | bytes 2211848 | tf_op jit(solution)/shard_map/ppermute | solution.py:46
  58.1 66.7 %collective-permute-start.18 = (bf16[10,48,768]{2,1,0:T(8,128)(2,1)S(1)}, bf16[10,48,768]{2,1,0:T(8,128)(2,1)S(1)}, u32[]{:S(2)}, u32[]{:S(2)}) collective-permute-start(bf16[10,48,768]{2,1,0:T(8,128)(2,1)S(1)} %copy-done.18), channel_id=1, source_target_pairs={{0,2},{1,3},{2,0},{3,1},{4,6},{5,7},{6,4},{7,5},{8,10},{9,11},{10,... | collective-permute-start | bytes 2211848 | tf_op jit(solution)/shard_map/ppermute | solution.py:46
  58.2 48.8 %collective-permute-start = (bf16[10,48]{1,0:T(8,128)(2,1)S(1)}, bf16[10,48]{1,0:T(8,128)(2,1)S(1)}, u32[]{:S(2)}, u32[]{:S(2)}) collective-permute-start(bf16[10,48]{1,0:T(8,128)(2,1)S(1)} %pad_maximum_fusion.2.refs_1_), channel_id=1, source_target_pairs={{0,3},{1,0},{2,1},{3,2},{4,7},{5,4},{6,5},{7,6},{8,11},{9,8},{10,9... | collective-permute-start | bytes 2888 | tf_op jit(solution)/shard_map/ppermute | solution.py:46
  60.4 46.6 %collective-permute-start.1 = (bf16[10,48]{1,0:T(8,128)(2,1)S(1)}, bf16[10,48]{1,0:T(8,128)(2,1)S(1)}, u32[]{:S(2)}, u32[]{:S(2)}) collective-permute-start(bf16[10,48]{1,0:T(8,128)(2,1)S(1)} %pad_maximum_fusion.2.refs_1_), channel_id=1, source_target_pairs={{0,2},{1,3},{2,0},{3,1},{4,6},{5,7},{6,4},{7,5},{8,10},{9,11},{10,... | collective-permute-start | bytes 2888 | tf_op jit(solution)/shard_map/ppermute | solution.py:46
  62.4 44.6 %collective-permute-start.2 = (bf16[10,48]{1,0:T(8,128)(2,1)S(1)}, bf16[10,48]{1,0:T(8,128)(2,1)S(1)}, u32[]{:S(2)}, u32[]{:S(2)}) collective-permute-start(bf16[10,48]{1,0:T(8,128)(2,1)S(1)} %pad_maximum_fusion.2.refs_1_), channel_id=1, source_target_pairs={{0,1},{1,2},{2,3},{3,0},{4,5},{5,6},{6,7},{7,4},{8,9},{9,10},{10,1... | collective-permute-start | bytes 2888 | tf_op jit(solution)/shard_map/ppermute | solution.py:46
  232.0 270.2 %all-gather.13.cloned.1.call-start = ((), (), s32[]{:S(2)}) async-start(), calls=%async_computation.7 | async-start | bytes 6193152 | tf_op jit(solution)/shard_map/all_gather | solution.py:312
  233.0 269.2 %all-gather.11.cloned.1.call-start = ((), (), s32[]{:S(2)}) async-start(), calls=%async_computation.6 | async-start | bytes 12386304 | tf_op jit(solution)/shard_map/all_gather | solution.py:312
  234.9 55.0 %collective-permute-start.30 = (bf16[1,48,3584]{2,1,0:T(8,128)(2,1)S(1)}, bf16[1,48,3584]{2,1,0:T(8,128)(2,1)S(1)}, u32[]{:S(2)}, u32[]{:S(2)}) collective-permute-start(bf16[1,48,3584]{2,1,0:T(8,128)(2,1)S(1)} %get-tuple-element.524), channel_id=1, source_target_pairs={{0,2},{1,3},{2,0},{3,1},{4,6},{5,7},{6,4},{7,5},{8,10},{9,11},{10,... | collective-permute-start | bytes 1032200 | tf_op jit(solution)/shard_map/ppermute | solution.py:46
  239.6 65.5 %collective-permute-start.31 = (bf16[1,48,3584]{2,1,0:T(8,128)(2,1)S(1)}, bf16[1,48,3584]{2,1,0:T(8,128)(2,1)S(1)}, u32[]{:S(2)}, u32[]{:S(2)}) collective-permute-start(bf16[1,48,3584]{2,1,0:T(8,128)(2,1)S(1)} %get-tuple-element.523), channel_id=1, source_target_pairs={{0,3},{1,0},{2,1},{3,2},{4,7},{5,4},{6,5},{7,6},{8,11},{9,8},{10,9... | collective-permute-start | bytes 1032200 | tf_op jit(solution)/shard_map/ppermute | solution.py:46
  308.3 597.1 %reduce-scatter.5.cloned.1.call-start = ((), (), s32[]{:S(2)}) async-start(), calls=%async_computation.8 | async-start | bytes 12386304 | tf_op jit(solution)/shard_map/reduce_scatter | solution.py:415
  308.4 42.7 %collective-permute-start.28 = (bf16[128,1536]{1,0:T(8,128)(2,1)S(1)}, bf16[128,1536]{1,0:T(8,128)(2,1)S(1)}, u32[]{:S(2)}, u32[]{:S(2)}) collective-permute-start(bf16[128,1536]{1,0:T(8,128)(2,1)S(1)} %copy-done.69), channel_id=1, source_target_pairs={{0,3},{1,0},{2,1},{3,2},{4,7},{5,4},{6,5},{7,6},{8,11},{9,8},{10,9... | collective-permute-start | bytes 1179656 | tf_op jit(solution)/shard_map/ppermute | solution.py:46
  308.5 56.6 %collective-permute-start.40 = (bf16[128,1536]{1,0:T(8,128)(2,1)S(1)}, bf16[128,1536]{1,0:T(8,128)(2,1)S(1)}, u32[]{:S(2)}, u32[]{:S(2)}) collective-permute-start(bf16[128,1536]{1,0:T(8,128)(2,1)S(1)} %copy-done.69), channel_id=1, source_target_pairs={{0,2},{1,3},{2,0},{3,1},{4,6},{5,7},{6,4},{7,5},{8,10},{9,11},{10,... | collective-permute-start | bytes 1179656 | tf_op jit(solution)/shard_map/ppermute | solution.py:46
  309.1 56.0 %collective-permute-start.41 = (bf16[128,1536]{1,0:T(8,128)(2,1)S(1)}, bf16[128,1536]{1,0:T(8,128)(2,1)S(1)}, u32[]{:S(2)}, u32[]{:S(2)}) collective-permute-start(bf16[128,1536]{1,0:T(8,128)(2,1)S(1)} %copy-done.69), channel_id=1, source_target_pairs={{0,1},{1,2},{2,3},{3,0},{4,5},{5,6},{6,7},{7,4},{8,9},{9,10},{10,1... | collective-permute-start | bytes 1179656 | tf_op jit(solution)/shard_map/ppermute | solution.py:46
  498.2 38.0 %collective-permute-start.55 = (bf16[128,1536]{1,0:T(8,128)(2,1)}, bf16[128,1536]{1,0:T(8,128)(2,1)S(1)}, u32[]{:S(2)}, u32[]{:S(2)}) collective-permute-start(bf16[128,1536]{1,0:T(8,128)(2,1)} %get-tuple-element.332.refs_0_), channel_id=1, source_target_pairs={{0,3},{1,0},{2,1},{3,2},{4,7},{5,4},{6,5},{7,6},{8,11},{9,8},{10,9... | collective-permute-start | bytes 1179656 | tf_op jit(solution)/shard_map/ppermute | solution.py:46
  499.6 50.3 %collective-permute-start.57 = (bf16[128,1536]{1,0:T(8,128)(2,1)}, bf16[128,1536]{1,0:T(8,128)(2,1)S(1)}, u32[]{:S(2)}, u32[]{:S(2)}) collective-permute-start(bf16[128,1536]{1,0:T(8,128)(2,1)} %get-tuple-element.332.refs_0_), channel_id=1, source_target_pairs={{0,2},{1,3},{2,0},{3,1},{4,6},{5,7},{6,4},{7,5},{8,10},{9,11},{10,... | collective-permute-start | bytes 1179656 | tf_op jit(solution)/shard_map/ppermute | solution.py:46
  502.2 47.7 %collective-permute-start.58 = (bf16[128,1536]{1,0:T(8,128)(2,1)}, bf16[128,1536]{1,0:T(8,128)(2,1)S(1)}, u32[]{:S(2)}, u32[]{:S(2)}) collective-permute-start(bf16[128,1536]{1,0:T(8,128)(2,1)} %get-tuple-element.332.refs_0_), channel_id=1, source_target_pairs={{0,1},{1,2},{2,3},{3,0},{4,5},{5,6},{6,7},{7,4},{8,9},{9,10},{10,1... | collective-permute-start | bytes 1179656 | tf_op jit(solution)/shard_map/ppermute | solution.py:46
  549.9 49.7 %collective-permute-start.56 = (bf16[128,1536]{1,0:T(8,128)(2,1)}, bf16[128,1536]{1,0:T(8,128)(2,1)S(1)}, u32[]{:S(2)}, u32[]{:S(2)}) collective-permute-start(bf16[128,1536]{1,0:T(8,128)(2,1)} %get-tuple-element.336), channel_id=1, source_target_pairs={{0,1},{1,2},{2,3},{3,0},{4,5},{5,6},{6,7},{7,4},{8,9},{9,10},{10,1... | collective-permute-start | bytes 1179656 | tf_op jit(solution)/shard_map/ppermute | solution.py:46
  563.6 36.2 %collective-permute-start.59 = (bf16[128,1536]{1,0:T(8,128)(2,1)}, bf16[128,1536]{1,0:T(8,128)(2,1)S(1)}, u32[]{:S(2)}, u32[]{:S(2)}) collective-permute-start(bf16[128,1536]{1,0:T(8,128)(2,1)} %get-tuple-element.338), channel_id=1, source_target_pairs={{0,2},{1,3},{2,0},{3,1},{4,6},{5,7},{6,4},{7,5},{8,10},{9,11},{10,... | collective-permute-start | bytes 1179656 | tf_op jit(solution)/shard_map/ppermute | solution.py:46
  563.6 36.2 %collective-permute-start.60 = (bf16[128,1536]{1,0:T(8,128)(2,1)}, bf16[128,1536]{1,0:T(8,128)(2,1)S(1)}, u32[]{:S(2)}, u32[]{:S(2)}) collective-permute-start(bf16[128,1536]{1,0:T(8,128)(2,1)} %get-tuple-element.339), channel_id=1, source_target_pairs={{0,3},{1,0},{2,1},{3,2},{4,7},{5,4},{6,5},{7,6},{8,11},{9,8},{10,9... | collective-permute-start | bytes 1179656 | tf_op jit(solution)/shard_map/ppermute | solution.py:46
  643.5 278.8 %reduce-scatter.7.cloned.1.call-start = ((), (), s32[]{:S(2)}) async-start(), calls=%async_computation.9 | async-start | bytes 6193152 | tf_op jit(solution)/shard_map/reduce_scatter | solution.py:415
  644.2 386.9 %reduce-scatter.11.cloned.1.call-start = ((), (), s32[]{:S(2)}) async-start(), calls=%async_computation.11 | async-start | bytes 6193152 | tf_op jit(solution)/shard_map/reduce_scatter | solution.py:415
  720.2 45.4 %collective-permute-start.74 = (bf16[128,1536]{1,0:T(8,128)(2,1)}, bf16[128,1536]{1,0:T(8,128)(2,1)S(1)}, u32[]{:S(2)}, u32[]{:S(2)}) collective-permute-start(bf16[128,1536]{1,0:T(8,128)(2,1)} %get-tuple-element.385.refs_0_), channel_id=1, source_target_pairs={{0,2},{1,3},{2,0},{3,1},{4,6},{5,7},{6,4},{7,5},{8,10},{9,11},{10,... | collective-permute-start | bytes 1179656 | tf_op jit(solution)/shard_map/ppermute | solution.py:46
  722.6 43.0 %collective-permute-start.75 = (bf16[128,1536]{1,0:T(8,128)(2,1)}, bf16[128,1536]{1,0:T(8,128)(2,1)S(1)}, u32[]{:S(2)}, u32[]{:S(2)}) collective-permute-start(bf16[128,1536]{1,0:T(8,128)(2,1)} %get-tuple-element.385.refs_0_), channel_id=1, source_target_pairs={{0,1},{1,2},{2,3},{3,0},{4,5},{5,6},{6,7},{7,4},{8,9},{9,10},{10,1... | collective-permute-start | bytes 1179656 | tf_op jit(solution)/shard_map/ppermute | solution.py:46
  808.0 231.7 %reduce-scatter.9.cloned.1.call-start = ((), (), s32[]{:S(2)}) async-start(), calls=%async_computation.10 | async-start | bytes 12386304 | tf_op jit(solution)/shard_map/reduce_scatter | solution.py:415
  914.0 108.4 %collective-permute-start.89 = (bf16[10,48,768]{2,1,0:T(8,128)(2,1)}, bf16[10,48,768]{2,1,0:T(8,128)(2,1)S(1)}, u32[]{:S(2)}, u32[]{:S(2)}) collective-permute-start(bf16[10,48,768]{2,1,0:T(8,128)(2,1)} %get-tuple-element.431), channel_id=1, source_target_pairs={{0,1},{1,2},{2,3},{3,0},{4,5},{5,6},{6,7},{7,4},{8,9},{9,10},{10,1... | collective-permute-start | bytes 2211848 | tf_op jit(solution)/shard_map/ppermute | solution.py:46
  916.8 106.4 %collective-permute-start.90 = (bf16[10,48,768]{2,1,0:T(8,128)(2,1)}, bf16[10,48,768]{2,1,0:T(8,128)(2,1)S(1)}, u32[]{:S(2)}, u32[]{:S(2)}) collective-permute-start(bf16[10,48,768]{2,1,0:T(8,128)(2,1)} %get-tuple-element.432), channel_id=1, source_target_pairs={{0,2},{1,3},{2,0},{3,1},{4,6},{5,7},{6,4},{7,5},{8,10},{9,11},{10,... | collective-permute-start | bytes 2211848 | tf_op jit(solution)/shard_map/ppermute | solution.py:46
  919.6 103.6 %collective-permute-start.91 = (bf16[10,48,768]{2,1,0:T(8,128)(2,1)}, bf16[10,48,768]{2,1,0:T(8,128)(2,1)S(1)}, u32[]{:S(2)}, u32[]{:S(2)}) collective-permute-start(bf16[10,48,768]{2,1,0:T(8,128)(2,1)} %get-tuple-element.433), channel_id=1, source_target_pairs={{0,3},{1,0},{2,1},{3,2},{4,7},{5,4},{6,5},{7,6},{8,11},{9,8},{10,9... | collective-permute-start | bytes 2211848 | tf_op jit(solution)/shard_map/ppermute | solution.py:46
  931.2 76.6 %collective-permute-start.93 = (bf16[48,3584]{1,0:T(8,128)(2,1)}, bf16[48,3584]{1,0:T(8,128)(2,1)S(1)}, u32[]{:S(2)}, u32[]{:S(2)}) collective-permute-start(bf16[48,3584]{1,0:T(8,128)(2,1)} %get-tuple-element.438), channel_id=1, source_target_pairs={{0,2},{1,3},{2,0},{3,1},{4,6},{5,7},{6,4},{7,5},{8,10},{9,11},{10,... | collective-permute-start | bytes 1032200 | tf_op jit(solution)/shard_map/ppermute | solution.py:46
  932.9 79.7 %collective-permute-start.94 = (bf16[48,3584]{1,0:T(8,128)(2,1)}, bf16[48,3584]{1,0:T(8,128)(2,1)S(1)}, u32[]{:S(2)}, u32[]{:S(2)}) collective-permute-start(bf16[48,3584]{1,0:T(8,128)(2,1)} %get-tuple-element.439), channel_id=1, source_target_pairs={{0,3},{1,0},{2,1},{3,2},{4,7},{5,4},{6,5},{7,6},{8,11},{9,8},{10,9... | collective-permute-start | bytes 1032200 | tf_op jit(solution)/shard_map/ppermute | solution.py:46
  (238 other events, 2690.7 us)
Sparse Core Ops, SparseCore 0:
  11.1 48.1 all-gather.8
  61.7 65.3 all-gather.6
  232.1 105.4 all-gather.14
  339.4 50.9 all-gather.12
  392.1 86.6 all-gather.10
  643.6 101.1 reduce-scatter.4
  748.2 57.8 reduce-scatter.6
  809.9 57.8 reduce-scatter.10
  871.3 90.5 reduce-scatter.8

commit v2 on v1

--- a/solution.py
+++ b/solution.py
@@ -1,3 +1,5 @@
+import math
+
 import jax
 import jax.numpy as jnp
 from jax import lax
@@ -41,14 +43,14 @@
     return [array] + [seq_swap(array, by) for by in range(2, lax.axis_size("seq"), 2)]
 
 
-def fsdp_shift(array, by):
+def fsdp_swap(array, by):
     count = lax.axis_size("fsdp")
-    return lax.ppermute(array, "fsdp", [(i, (i + by) % count) for i in range(count)])
+    return lax.ppermute(array, "fsdp", [(i, i ^ by) for i in range(count)])
 
 
 def gather_fsdp(array):
     count = lax.axis_size("fsdp")
-    return [array] + [fsdp_shift(array, -by) for by in range(1, count)]
+    return [array] + [fsdp_swap(array, by) for by in range(1, count)]
 
 
 def small_scatter_seq(parts):
@@ -62,7 +64,7 @@
 def small_scatter_fsdp(parts):
     total = parts[0]
     for by in range(1, parts.shape[0]):
-        total = total + fsdp_shift(parts[by], by)
+        total = total + fsdp_swap(parts[by], by)
     return total
 
 
@@ -100,6 +102,24 @@
 
 mark_shape = jax.ShapeDtypeStruct((8, 128), jnp.float32)
 anywhere = pl.BlockSpec(memory_space=pl.ANY)
+
+
+def bytes_of(shape, kind):
+    return math.prod(shape) * jnp.dtype(kind).itemsize
+
+
+def vmem_of(operands, in_specs, out_shape, out_specs, scratch, grid):
+    total = 0
+    for array, spec in [*zip(operands, in_specs), *zip(out_shape, out_specs)]:
+        if spec is anywhere or spec is scalar:
+            continue
+        if grid:
+            total += 2 * bytes_of(spec.block_shape, array.dtype)
+        else:
+            total += bytes_of(array.shape, array.dtype)
+    for array in scratch:
+        total += bytes_of(array.shape, array.dtype)
+    return total + total // 2 + 4 * 1024 * 1024
 
 
 def ordered_call(body, operands, in_specs, out_specs, out_shape, aliases, scratch, grid, cost):
@@ -115,7 +135,11 @@
         out_shape=list(out_shape) + [mark_shape],
         scratch_shapes=list(scratch),
         input_output_aliases=aliases,
-        compiler_params=pltpu.CompilerParams(vmem_limit_bytes=56 * 1024 * 1024),
+        compiler_params=pltpu.CompilerParams(
+            vmem_limit_bytes=min(
+                vmem_of(operands, in_specs, out_shape, out_specs, scratch, grid), 60 << 20
+            )
+        ),
         cost_estimate=pl.CostEstimate(
             flops=cost[0], bytes_accessed=cost[1], transcendentals=0
         ),
@@ -177,14 +201,15 @@
     return pl.BlockSpec(shape, lambda i: (0,) * len(shape))
 
 
-def pack_mix(mix_weight, layer, wide):
+def pack_mix(mix_weight, layer, wide, earlier=()):
     seqs = lax.axis_size("seq")
     rows, columns = mix_weight.shape[1:]
     features = columns // 4
     chunk = features // seqs
     outer = features // (3 * wide)
 
-    def body(place, weight, out):
+    def body(place, weight, *refs):
+        out = refs[-1]
         for s in range(seqs):
             slot = lax.bitwise_xor(place[0], jnp.int32(s))
             for g in range(3):
@@ -201,10 +226,11 @@
     return kernel_call(
         body,
         (1,),
-        [scalar, pl.BlockSpec((1, rows, columns), lambda i: (layer, 0, 0))],
+        [scalar, pl.BlockSpec((1, rows, columns), lambda i: (layer, 0, 0))]
+        + [anywhere] * len(earlier),
         whole(shape),
         jax.ShapeDtypeStruct(shape, low),
-    )(place_of("seq"), mix_weight)
+    )(place_of("seq"), mix_weight, *earlier)
 
 
 def assemble_mix(pieces, wide, features):
@@ -218,7 +244,7 @@
         inner_out, outer_out = refs[-2:]
         refs = refs if rotated else [refs[0].at[j] for j in range(rings)]
         for j in range(rings):
-            f = lax.rem(place_fsdp[0] + j, rings) if rotated else j
+            f = lax.bitwise_xor(place_fsdp[0], jnp.int32(j)) if rotated else j
             for s in range(seqs):
                 inner_out[lax.bitwise_xor(place_seq[0], jnp.int32(s)), f] = refs[j][s]
             for i in range(outer):
@@ -237,7 +263,7 @@
     return [packed[:1]] + [seq_swap(packed[by : by + 1], by) for by in range(1, seqs)]
 
 
-def join_mix(parts, packed):
+def join_mix(parts, packed, earlier=()):
     seqs = len(parts)
 
     def body(*refs):
@@ -246,7 +272,7 @@
             out[s] = refs[s][0]
         out[seqs:] = refs[seqs][seqs:]
 
-    return plain_call(body, [shaped(packed.shape, low)])(*parts, packed)[0]
+    return plain_call(body, [shaped(packed.shape, low)], earlier=earlier)(*parts, packed)[0]
 
 
 def tall_of(block):
@@ -263,7 +289,7 @@
 
     def body(place, weight, out):
         for f in range(rings):
-            slot = lax.rem(f - place[0] + rings, rings)
+            slot = lax.bitwise_xor(place[0], jnp.int32(f))
             for g in range(2):
                 for s in range(seqs):
                     start = g * half + (s * rings + f) * block
@@ -291,7 +317,7 @@
     def body(place, *refs):
         out = refs[rings]
         for j in range(rings):
-            out[lax.rem(place[0] - j + rings, rings)] = refs[j][0]
+            out[lax.bitwise_xor(place[0], jnp.int32(j))] = refs[j][0]
 
     shape = (rings,) + pieces[0].shape[1:]
     return kernel_call(
@@ -305,7 +331,7 @@
 
 def swap_feed(packed):
     rings = lax.axis_size("fsdp")
-    return [packed[:1]] + [fsdp_shift(packed[by : by + 1], by) for by in range(1, rings)]
+    return [packed[:1]] + [fsdp_swap(packed[by : by + 1], by) for by in range(1, rings)]
 
 
 def gather_rows(part):
@@ -317,14 +343,17 @@
     return jnp.pad(down_weight[layer].astype(low), ((0, tall_of(block) - block), (0, 0)))
 
 
-def adam_kernel(load, scalars, grads, state, layer, previous, scratch=()):
+def adam_kernel(load, scalars, grads, state, layer, previous, scratch=(), earlier=()):
     weight = state[0]
     rows, columns = weight.shape[1:]
     tile = 16 if rows % 16 == 0 else rows
     width = 768
-    specs = [pl.BlockSpec((tile, grad.shape[-1]), lambda i: (i, 0)) for grad in grads]
+    specs = [
+        pl.BlockSpec(grad.shape if tile == rows else (tile, grad.shape[-1]), lambda i: (i, 0))
+        for grad in grads
+    ]
     part = pl.BlockSpec((1, tile, columns), lambda i: (layer, i, 0))
-    kept = 0 if previous is None else 3
+    kept = (0 if previous is None else 3) + len(earlier)
     before = len(scalars) + len(grads)
 
     def body(*refs):
@@ -353,10 +382,10 @@
         + [anywhere] * kept,
         [part] * 3,
         [shaped(weight.shape)] * 3,
-        aliases={before + 3 + i: i for i in range(kept)},
+        aliases={before + 3 + i: i for i in range(kept - len(earlier))},
         scratch=[pltpu.VMEM((tile, columns), jnp.float32), *(make(tile) for make in scratch)],
         cost=(0, 26 * rows * columns),
-    )(*scalars, *grads, *state, *(previous or ()))
+    )(*scalars, *grads, *state, *(previous or ()), *earlier)
 
 
 def mix_reduce(pieces):
@@ -421,7 +450,7 @@
 
     def body(place, part, *outs):
         for j in range(rings):
-            outs[j][...] = part[lax.rem(place[0] + j, rings)]
+            outs[j][...] = part[lax.bitwise_xor(place[0], jnp.int32(j))]
 
     pieces = plain_call(body, [shaped(part.shape[1:], low)] * rings, scalars=1)(
         place_of("fsdp"), part
@@ -437,7 +466,7 @@
 
     def load(scalars, grads, scratch, total):
         for j in range(rings):
-            scratch[0][lax.rem(scalars[0][0] - j + rings, rings)] = grads[j][...]
+            scratch[0][lax.bitwise_xor(scalars[0][0], jnp.int32(j))] = grads[j][...]
         for f in range(rings):
             for g in range(2):
                 for s in range(seqs):
@@ -457,13 +486,28 @@
     )
 
 
-def down_adam(part, state, layer, previous):
-    part = part[: state[0].shape[1]]
-
+def down_adam(parts, state, layer, previous, earlier):
     def load(scalars, grads, scratch, total):
-        total[...] = grads[0][...].astype(jnp.float32)
-
-    return adam_kernel(load, [], [part], state, layer, previous)
+        sums = grads[0][...].astype(jnp.float32)
+        for grad in grads[1:]:
+            sums = sums + grad[...].astype(jnp.float32)
+        total[...] = sums[: total.shape[0]]
+
+    return adam_kernel(load, [], parts, state, layer, previous, earlier=earlier)
+
+
+def split_down(part):
+    seqs = lax.axis_size("seq")
+    part = part.reshape(seqs, -1, part.shape[-1])
+
+    def body(place, part, even, odd):
+        for i in range(seqs):
+            owner = lax.bitwise_xor(place[0], jnp.int32(i))
+            (even, odd)[i % 2][i // 2] = part[owner]
+
+    return plain_call(
+        body, [shaped((seqs // 2,) + part.shape[1:], part.dtype)] * 2, scalars=1
+    )(place_of("seq"), part)
 
 
 def place_blocks(blocks, owners, place, earlier=()):
@@ -489,20 +533,19 @@
     return gather_fsdp(jnp.concatenate([gains, taps], axis=0).astype(low))
 
 
-def vectors_middle(blocks, earlier):
+def vectors_middle(blocks):
     rings = lax.axis_size("fsdp")
     both = place_blocks(
         blocks,
-        lambda place: [lax.rem(place + j, rings) for j in range(rings)],
+        lambda place: [lax.bitwise_xor(place, jnp.int32(j)) for j in range(rings)],
         place_of("fsdp"),
-        earlier,
     )
     return both, send_seq(both)
 
 
 def vectors_end(both, blocks):
     spread = place_blocks(
-        stack_pairs(blocks),
+        blocks,
         lambda place: [lax.bitwise_xor(place, jnp.int32(i)) for i in seq_order()],
         place_of("seq"),
     )
@@ -521,7 +564,7 @@
     gains = small_scatter_seq(gains)
     taps = tap_grads.reshape(3 * LAYERS, -1)[:, : rings * short]
     both = jnp.concatenate([gains, taps], axis=0).reshape(5 * LAYERS, rings, short)
-    owner = (place_fsdp + jnp.arange(rings)) % rings
+    owner = place_fsdp ^ jnp.arange(rings)
     pick = (owner[:, None] == jnp.arange(rings)[None, :]).astype(jnp.float32)
     both = jnp.einsum("jo,koc->jkc", pick, both, precision=lax.Precision.HIGHEST)
     both = small_scatter_fsdp(both)
@@ -547,7 +590,7 @@
     )(inputs, gain)
 
 
-def finish(base, sums, gain):
+def finish(base, sums, gain, earlier=(), carried=()):
     def body(*refs):
         total = refs[0][...]
         for part in refs[1 : 1 + len(sums)]:
@@ -560,10 +603,15 @@
 
     if gain is None:
         return plain_call(body, [shaped(base.shape, low)])(base, *sums)[0]
-    return plain_call(body, [shaped(base.shape), shaped(base.shape, low)])(base, *sums, gain)
-
-
-def finish_back(flow, sums, stream, gain, carried=()):
+    return plain_call(
+        body,
+        [shaped(base.shape), shaped(base.shape, low)],
+        earlier=earlier,
+        carried=carried,
+    )(base, *sums, gain)
+
+
+def finish_back(flow, sums, stream, gain, carried=(), earlier=()):
     def body(flow, stream, gain, *refs):
         total = refs[0][...].astype(jnp.float32)
         for part in refs[1 : len(sums)]:
@@ -580,10 +628,11 @@
         body,
         [shaped(flow.shape), shaped(flow.shape, low), shaped((1, flow.shape[1]))],
         carried=carried,
+        earlier=earlier,
     )(flow, stream, gain, *sums)
 
 
-def pair_sum(even, received):
+def pair_sum(even, received, earlier=()):
     half, tokens, features = even.shape
 
     def body(even, received, *outs):
@@ -594,6 +643,7 @@
     outs = plain_call(
         body,
         [shaped((tokens, features))] + [shaped((tokens, features), low)] * (half - 1),
+        earlier=earlier,
     )(even, received)
     return [outs[0]] + [seq_swap(outs[i], 2 * i) for i in range(1, half)]
 
@@ -752,7 +802,7 @@
         for f in range(rings):
             outer[f] = part[f * rows : (f + 1) * rows]
         for j in range(rings):
-            f = lax.rem(place[0] + j, rings)
+            f = lax.bitwise_xor(place[0], jnp.int32(j))
             for s in range(seqs):
                 outs[j][s] = inner[s, f]
             for i in range(count):
@@ -891,7 +941,9 @@
 def feed_grads(normed, gate_flows, up_flows):
     count, groups = len(normed), len(gate_flows)
     tokens, features = normed[0].shape
-    size, hidden = gate_flows[0].shape
+    hidden = gate_flows[0].shape[1]
+    sizes = [flow.shape[0] for flow in gate_flows]
+    starts = [sum(sizes[:i]) for i in range(groups)]
     tile = hidden_tile(hidden)
     steps = hidden // tile
 
@@ -910,23 +962,26 @@
             @pl.when(lax.div(step, steps) == half)
             def _():
                 for i in range(groups):
-                    columns[i * size : (i + 1) * size] = flows[half * groups + i][...]
+                    at = slice(starts[i], starts[i] + sizes[i])
+                    columns[at] = flows[half * groups + i][...]
 
         out[...] = dot(rows[...], columns[...], tn).astype(low)
 
-    gate_spec = pl.BlockSpec((size, tile), lambda i: (0, jnp.minimum(i, steps - 1)))
-    up_spec = pl.BlockSpec((size, tile), lambda i: (0, jnp.maximum(i - steps, 0)))
+    gate_specs = [
+        pl.BlockSpec((size, tile), lambda i: (0, jnp.minimum(i, steps - 1))) for size in sizes
+    ]
+    up_specs = [
+        pl.BlockSpec((size, tile), lambda i: (0, jnp.maximum(i - steps, 0))) for size in sizes
+    ]
     return kernel_call(
         body,
         (2 * steps,),
-        [whole((tokens, features))] * count
-        + [gate_spec] * groups
-        + [up_spec] * groups,
+        [whole((tokens, features))] * count + gate_specs + up_specs,
         pl.BlockSpec((features, tile), lambda i: (0, i)),
         shaped((features, 2 * hidden), low),
         scratch=[
             pltpu.VMEM((count * tokens, features), low),
-            pltpu.VMEM((groups * size, tile), low),
+            pltpu.VMEM((count * tokens, tile), low),
         ],
         cost=(12 * count * tokens * features * hidden, 24 * features * hidden),
     )(*normed, *gate_flows, *up_flows)
@@ -935,7 +990,9 @@
 def down_grads(hiddens, flows):
     count, groups = len(flows), len(hiddens)
     tokens, features = flows[0].shape
-    size, hidden = hiddens[0].shape
+    hidden = hiddens[0].shape[1]
+    sizes = [values.shape[0] for values in hiddens]
+    starts = [sum(sizes[:i]) for i in range(groups)]
     tile = hidden_tile(hidden)
 
     def body(*refs):
@@ -948,19 +1005,19 @@
                 rows[i * tokens : (i + 1) * tokens] = refs[i][...]
 
         for i in range(groups):
-            columns[i * size : (i + 1) * size] = hiddens[i][...]
+            columns[starts[i] : starts[i] + sizes[i]] = hiddens[i][...]
         out[...] = dot(columns[...], rows[...], tn).astype(low)
 
     return kernel_call(
         body,
         (hidden // tile,),
         [whole((tokens, features))] * count
-        + [pl.BlockSpec((size, tile), lambda i: (0, i))] * groups,
+        + [pl.BlockSpec((size, tile), lambda i: (0, i)) for size in sizes],
         pl.BlockSpec((tile, features), lambda i: (i, 0)),
         shaped((hidden, features), low),
         scratch=[
             pltpu.VMEM((count * tokens, features), low),
-            pltpu.VMEM((groups * size, tile), low),
+            pltpu.VMEM((count * tokens, tile), low),
         ],
         cost=(6 * count * tokens * features * hidden, 12 * features * hidden),
     )(*flows, *hiddens)
@@ -975,11 +1032,11 @@
 
 
 def groups_of(blocks):
-    return [blocks[i : i + 2] for i in range(0, len(blocks), 2)]
+    return [blocks[:2]] + [[block] for block in blocks[2:]]
 
 
 def return_sums(sums):
-    return [sums[0]] + [fsdp_shift(sums[j], j) for j in range(1, len(sums))]
+    return [sums[0]] + [fsdp_swap(sums[j], j) for j in range(1, len(sums))]
 
 
 def adam_update(weight, first, second, gradient, rate, decay):
@@ -1018,23 +1075,30 @@
     cotangent = cotangent.reshape(-1, features)
     Order.mark = jnp.zeros(mark_shape.shape, mark_shape.dtype)
 
-    feed_swaps, mixes, feeds = [None] * LAYERS, [None] * LAYERS, [None] * LAYERS
-    feed_swaps[0] = swap_feed(pack_feed(feed_weight, 0))
-    mix_packed = pack_mix(mix_weight, 0, wide)
+    mixes, feeds = [None] * LAYERS, [None] * LAYERS
+    vector_blocks = vectors_start(gain_weight, tap_weight)
+    feed_swap = swap_feed(pack_feed(feed_weight, 0))
+    mix_packed = pack_mix(mix_weight, 0, wide, vector_blocks[1:])
     mix_swap = swap_mix(mix_packed)
     down_rows = gather_rows(pack_down(down_weight, 0))
-    vector_blocks = vectors_start(gain_weight, tap_weight)
+    both, vector_blocks = vectors_middle(vector_blocks)
     mix_pieces = gather_fsdp(join_mix(mix_swap, mix_packed))
-    feeds[0] = (gather_rows(assemble_feed(feed_swaps[0])), down_rows)
-    both, vector_blocks = vectors_middle(vector_blocks, mix_pieces[1:2])
+    feed_part = assemble_feed(feed_swap)
+    later_packed = pack_mix(mix_weight, 1, wide)
+    later_swap = swap_mix(later_packed)
+    vector_blocks = stack_pairs(vector_blocks)
+    later_piece = join_mix(later_swap, later_packed, mix_pieces[1:2])
     gain_rows, tap_rows = vectors_end(both, vector_blocks)
     stream, normed = first_norm(
-        inputs.reshape(-1, features), gain_rows[0, 0], mix_pieces[2:-1]
+        inputs.reshape(-1, features), gain_rows[0, 0], mix_pieces[2:3]
     )
     blocks = send_seq(normed)
-    later_packed = pack_mix(mix_weight, 1, wide)
-    blocks = stack_pairs(blocks)
+    later_feed = pack_feed(feed_weight, 1)
+    *blocks, feed_part = stack_pairs(blocks, mix_pieces[3:], [feed_part])
+    feeds[0] = (gather_rows(feed_part), down_rows)
     mixes[0] = assemble_mix(mix_pieces, wide, features)
+    later_mix = [None, None, fsdp_swap(later_piece, 2)] if rings > 2 else [None, None]
+    later_feed = swap_feed(later_feed)
 
     kept = []
     for layer in range(LAYERS):
@@ -1047,17 +1111,20 @@
         sums = pair_sum(even, odd)
         if last:
             flow_low = join_blocks(flow_blocks)
+            middle, normed_two = finish(stream, sums, gain_rows[layer, 1])
         else:
-            feed_swaps[1] = swap_feed(pack_feed(feed_weight, 1))
-        middle, normed_two = finish(stream, sums, gain_rows[layer, 1])
+            middle, normed_two, later_piece, down_packed = finish(
+                stream,
+                sums,
+                gain_rows[layer, 1],
+                (*later_mix[2:], *later_feed[1:]),
+                (later_piece, pack_down(down_weight, 1)),
+            )
         two_blocks = gather_fsdp(normed_two)
         if not last:
-            later_mix = join_mix(swap_mix(later_packed), later_packed)
-            later_mix = lax.all_gather(later_mix, "fsdp", axis=0)
-            feeds[1] = (
-                gather_rows(assemble_feed(feed_swaps[1])),
-                gather_rows(pack_down(down_weight, 1)),
-            )
+            later_mix[0] = later_piece
+            later_mix[1] = fsdp_swap(later_piece, 1)
+            feeds[1] = (gather_rows(assemble_feed(later_feed)), gather_rows(down_packed))
         sums, values = [], []
         for number, group in enumerate(groups_of(two_blocks)):
             outs, saved = feed_forward(group, *feeds[layer], number == 0)
@@ -1066,8 +1133,12 @@
         kept.append((stream, middle, gathered, projected, two_blocks, values))
         sums = return_sums(sums)
         if not last:
-            stream, normed = finish(middle, sums, gain_rows[layer + 1, 0])
-            blocks = stack_pairs(send_seq(normed))
+            stream, normed, later_piece = finish(
+                middle, sums, gain_rows[layer + 1, 0], later_mix[1:2], [later_piece]
+            )
+            blocks = send_seq(normed)
+            later_mix += [fsdp_swap(later_piece, by) for by in range(3, rings)]
+            blocks = stack_pairs(blocks)
             mixes[1] = assemble_mix(later_mix, wide, features)
 
     states = (
@@ -1078,6 +1149,7 @@
     new = [None] * 3
     gain_grads, tap_grads = [None] * LAYERS, [None] * LAYERS
     flow = cotangent
+    later_mix = ()
     for layer in reversed(range(LAYERS)):
         last = layer + 1 == LAYERS
         stream, middle, gathered, projected, two_blocks, values = kept[layer]
@@ -1094,41 +1166,50 @@
             outputs = finish(middle, sums, None).reshape(inputs.shape)
         back_sums = return_sums(back_sums)
         down_part = down_grads([value[2] for value in values], flow_low)
-        middle_flow, middle_low, gain_two, down_part = finish_back(
-            flow, back_sums, middle, gain_rows[layer, 1], [down_part]
+        middle_flow, middle_low, gain_two, down_part, *later_mix = finish_back(
+            flow, back_sums, middle, gain_rows[layer, 1], [down_part, *later_mix]
         )
-        down_part = scatter_rows(down_part)
+        later_mix = return_sums(later_mix) if later_mix else later_mix
+        if last:
+            down_part = [scatter_rows(down_part)]
         blocks = send_seq(middle_low)
         feed_part = feed_grads(two_blocks, gate_flows, up_flows)
+        if not last:
+            later_feed = split_feed(later_feed, rows)
         even, odd, feed_part = stack_pairs(
-            blocks, () if last else later_mix[1::2], [feed_part]
+            blocks, () if last else later_mix[2:3], [feed_part]
         )
         feed_part = scatter_rows(feed_part)
         blocks = even, odd
         even, odd, flows, mixed, tap_grads[layer] = mixer_backward(
             blocks, projected, *mixes[layer], tap_rows[layer]
         )
-        sums = pair_sum(even, seq_swap(odd, 1))
-        mix_part = return_sums(mixer_grads(gathered, flows, mixed, blocks, rows))
+        sums = pair_sum(even, seq_swap(odd, 1), () if last else later_mix[3:])
+        mix_part = mixer_grads(gathered, flows, mixed, blocks, rows)
+        flow, low_flow, gain_one, *mix_part = finish_back(
+            middle_flow, sums, stream, gain_rows[layer, 0], mix_part, () if last else later_feed[1:]
+        )
         if not last:
-            later_mix = mix_reduce(later_mix)
-        flow, low_flow, gain_one = finish_back(middle_flow, sums, stream, gain_rows[layer, 0])
+            mix_part = return_sums(mix_part)
         gain_grads[layer] = jnp.concatenate([gain_one, gain_two])
         if last:
             flow_low = gather_fsdp(low_flow)
             later_mix, later_feed, later_down = mix_part, feed_part, down_part
-    later_feed = split_feed(later_feed, rows)
-    new[2] = down_adam(later_down, states[2], 1, new[2])
-    new[0] = mix_adam(later_mix, states[0], 1, new[0], wide)
+    later_mix = mix_reduce(later_mix)
+    new[1] = feed_adam(later_feed, states[1], 1, new[1])
+    even, odd = split_down(down_part)
+    odd = seq_swap(odd, 1)
+    new[2] = down_adam(later_down, states[2], 1, new[2], mix_part[2:3])
+    down_part = pair_sum(even, odd)
     gain_grad, tap_grad = vector_gradients(
         jnp.stack(gain_grads), jnp.stack(tap_grads), gain_weight.shape[-1]
     )
-    new[1] = feed_adam(later_feed, states[1], 1, new[1])
+    new[0] = mix_adam(later_mix, states[0], 1, new[0], wide)
+    feed_part = split_feed(feed_part, rows)
     mix_part = mix_reduce(mix_part)
-    new[2] = down_adam(down_part, states[2], 0, new[2])
-    feed_part = split_feed(feed_part, rows)
+    new[2] = down_adam(down_part, states[2], 0, new[2], ())
+    new[1] = feed_adam(feed_part, states[1], 0, new[1])
     new[0] = mix_adam(mix_part, states[0], 0, new[0], wide)
-    new[1] = feed_adam(feed_part, states[1], 0, new[1])
     input_grad = flow.reshape(sequences, length, features)
     gain_new = adam_update(gain_weight, gain_first, gain_second, gain_grad, rate_vector, 0.0)
     tap_new = adam_update(tap_weight, tap_first, tap_second, tap_grad, rate_vector, 0.0)

time: 1110 us -> 1020 us (0.919)
  Pallas kernels: 361 us -> 223 us
  local copies, waits for them, and re-layouts: 57.6 us -> 126 us
  waiting for transfers between devices: 509 us -> 495 us
    pallas_call x59 -> x65, Pallas kernels: 361 us -> 223 us  [ordered_call(): pl.pallas_call(marked, in_specs=list(in_specs) + [anywhere], out_specs=li...]
    unnamed x293 -> x400, local copies, waits for them, and re-layouts: 39.8 us -> 119 us
    ppermute x68 -> x72, starting transfers between devices: 66.4 us -> 75.7 us  [seq_swap(): return lax.ppermute(array, 'seq', [(i, i ^ by) for i in range(count)])]
    ppermute x68 -> x72, waiting for transfers between devices: 117 us -> 108 us  [seq_swap(): return lax.ppermute(array, 'seq', [(i, i ^ by) for i in range(count)])]
    ppermute x51 -> x54, waiting for transfers between devices: 391 us -> 386 us  [fsdp_swap(): return lax.ppermute(array, 'fsdp', [(i, i ^ by) for i in range(count)])]
    ppermute x51 -> x54, starting transfers between devices: 69.5 us -> 69 us  [fsdp_swap(): return lax.ppermute(array, 'fsdp', [(i, i ^ by) for i in range(count)])]
  transfers between devices with their start and end apart: 128 -> 133, of which waited for: 49 -> 61; matrix products, arithmetic and copies ran while one was open for 2% -> 1% of each run, Pallas kernels for 32% -> 22%
where the time goes in v2:
time: 1020 us; the launch traced here: 1010 us
  waiting for transfers between devices  495 us (49%)
  Pallas kernels  223 us (22%)
  starting transfers between devices  145 us (14%)
  local copies, waits for them, and re-layouts  126 us (12%)
  between operations  16.6 us (2%)
    ppermute x54, waiting for transfers between devices, fsdp_swap(): return lax.ppermute(array, 'fsdp', [(i, i ^ by) for i in range(count)])  386 us
    pallas_call x65, Pallas kernels, ordered_call(): pl.pallas_call(marked, in_specs=list(in_specs) + [anywhere], out_specs=li...  223 us
    unnamed x400, local copies, waits for them, and re-layouts  119 us
    ppermute x72, waiting for transfers between devices, seq_swap(): return lax.ppermute(array, 'seq', [(i, i ^ by) for i in range(count)])  108 us
    ppermute x72, starting transfers between devices, seq_swap(): return lax.ppermute(array, 'seq', [(i, i ^ by) for i in range(count)])  75.7 us
    ppermute x54, starting transfers between devices, fsdp_swap(): return lax.ppermute(array, 'fsdp', [(i, i ^ by) for i in range(count)])  69 us
  transfers between devices with their start and end apart: 133, of which 61 were waited for; matrix products, arithmetic and copies ran while one was open for 1% of the time, Pallas kernels for 22%

profile of v2, /device:TPU:8, one launch (start us, length us, event | category | flops | bytes accessed | tf_op | source)
XLA Modules:
  0.0 1010.7 jit_solution(13317360490571312706)
XLA Ops:
  46.7 10.3 %collective-permute-done.7.refs_3_ = bf16[1,48,3584]{2,1,0:T(8,128)(2,1)S(1)} collective-permute-done((bf16[1,48,3584]{2,1,0:T(8,128)(2,1)S(1)}, bf16[1,48,3584]{2,1,0:T(8,128)(2,1)S(1)}, u32[]{:S(2)}, u32[]{:S(2)}) %collective-permute-start.7) | collective-permute-done | bytes 344096 | tf_op jit(solution)/shard_map/ppermute | solution.py:48
  92.5 42.2 %collective-permute-done.25.refs_2_.refs_4_ = bf16[10,48,768]{2,1,0:T(8,128)(2,1)S(1)} collective-permute-done((bf16[10,48,768]{2,1,0:T(8,128)(2,1)}, bf16[10,48,768]{2,1,0:T(8,128)(2,1)S(1)}, u32[]{:S(2)}, u32[]{:S(2)}) %collective-permute-start.25) | collective-permute-done | bytes 737312 | tf_op jit(solution)/shard_map/ppermute | solution.py:48
  177.9 19.4 %collective-permute-done.36.refs_7_.refs_2_ = bf16[1,48,3584]{2,1,0:T(8,128)(2,1)S(1)} collective-permute-done((bf16[1,48,3584]{2,1,0:T(8,128)(2,1)S(1)}, bf16[1,48,3584]{2,1,0:T(8,128)(2,1)S(1)}, u32[]{:S(2)}, u32[]{:S(2)}) %collective-permute-start.36) | collective-permute-done | bytes 344096 | tf_op jit(solution)/shard_map/ppermute | solution.py:48
  198.5 20.7 %collective-permute-done.37.refs_8_.refs_3_ = bf16[1,48,3584]{2,1,0:T(8,128)(2,1)S(1)} collective-permute-done((bf16[1,48,3584]{2,1,0:T(8,128)(2,1)S(1)}, bf16[1,48,3584]{2,1,0:T(8,128)(2,1)S(1)}, u32[]{:S(2)}, u32[]{:S(2)}) %collective-permute-start.37) | collective-permute-done | bytes 344096 | tf_op jit(solution)/shard_map/ppermute | solution.py:48
  220.5 16.0 %collective-permute-done.38.refs_9_.refs_4_ = bf16[1,48,3584]{2,1,0:T(8,128)(2,1)S(1)} collective-permute-done((bf16[1,48,3584]{2,1,0:T(8,128)(2,1)S(1)}, bf16[1,48,3584]{2,1,0:T(8,128)(2,1)S(1)}, u32[]{:S(2)}, u32[]{:S(2)}) %collective-permute-start.38) | collective-permute-done | bytes 344096 | tf_op jit(solution)/shard_map/ppermute | solution.py:48
  246.9 12.2 %collective-permute-done.39.refs_1_ = bf16[128,1536]{1,0:T(8,128)(2,1)S(1)} collective-permute-done((bf16[128,1536]{1,0:T(8,128)(2,1)}, bf16[128,1536]{1,0:T(8,128)(2,1)S(1)}, u32[]{:S(2)}, u32[]{:S(2)}) %collective-permute-start.39) | collective-permute-done | bytes 393248 | tf_op jit(solution)/shard_map/ppermute | solution.py:48
  299.1 11.3 %collective-permute-done.42.refs_3_ = bf16[128,1536]{1,0:T(8,128)(2,1)S(1)} collective-permute-done((bf16[128,1536]{1,0:T(8,128)(2,1)S(1)}, bf16[128,1536]{1,0:T(8,128)(2,1)S(1)}, u32[]{:S(2)}, u32[]{:S(2)}) %collective-permute-start.42) | collective-permute-done | bytes 393248 | tf_op jit(solution)/shard_map/ppermute | solution.py:48
  310.4 8.8 collective-permute-done.44.refs_4_
  324.0 16.9 %collective-permute-done.46.refs_1_ = bf16[128,1536]{1,0:T(8,128)(2,1)S(1)} collective-permute-done((bf16[128,1536]{1,0:T(8,128)(2,1)S(1)}, bf16[128,1536]{1,0:T(8,128)(2,1)S(1)}, u32[]{:S(2)}, u32[]{:S(2)}) %collective-permute-start.46) | collective-permute-done | bytes 393248 | tf_op jit(solution)/shard_map/ppermute | solution.py:39
  341.9 13.7 %collective-permute-done.48.refs_3_ = bf16[128,1536]{1,0:T(8,128)(2,1)S(1)} collective-permute-done((bf16[128,1536]{1,0:T(8,128)(2,1)S(1)}, bf16[128,1536]{1,0:T(8,128)(2,1)S(1)}, u32[]{:S(2)}, u32[]{:S(2)}) %collective-permute-start.48) | collective-permute-done | bytes 393248 | tf_op jit(solution)/shard_map/ppermute | solution.py:39
  358.1 24.9 %collective-permute-done.50.refs_5_ = bf16[10,48,768]{2,1,0:T(8,128)(2,1)S(1)} collective-permute-done((bf16[10,48,768]{2,1,0:T(8,128)(2,1)S(1)}, bf16[10,48,768]{2,1,0:T(8,128)(2,1)S(1)}, u32[]{:S(2)}, u32[]{:S(2)}) %collective-permute-start.50) | collective-permute-done | bytes 737312 | tf_op jit(solution)/shard_map/ppermute | solution.py:48
  400.9 8.8 collective-permute-done.55.refs_1_
  412.2 9.2 collective-permute-done.56.refs_2_
  421.4 10.0 collective-permute-done.57.refs_3_
  439.4 11.7 %collective-permute-done.58.refs_1_ = bf16[128,1536]{1,0:T(8,128)(2,1)} collective-permute-done((bf16[128,1536]{1,0:T(8,128)(2,1)}, bf16[128,1536]{1,0:T(8,128)(2,1)}, u32[]{:S(2)}, u32[]{:S(2)}) %collective-permute-start.58) | collective-permute-done | bytes 393248 | tf_op jit(solution)/shard_map/ppermute | solution.py:48
  457.8 9.4 shard_map.332
  484.9 11.0 %shard_map.335 = (f32[128,1536]{1,0:T(8,128)S(1)}, bf16[128,1536]{1,0:T(8,128)(2,1)S(1)}, bf16[256,1792]{1,0:T(8,128)(2,1)S(1)}, bf16[256,1792]{1,0:T(8,128)(2,1)S(1)}, f32[8,128]{1,0:T(8,128)S(1)}) custom-call(bf16[128,1536]{1,0:T(8,128)(2,1)S(1)} %get-tuple-element.390.refs_0_, bf16[128,1536]{1,0:T(8,128)(2,1)S(1)} %copy-done.116, ...), custom_call_target="tpu_custom_call" | custom-call | tf_op jit(solution)/shard_map/pallas_call | solution.py:131
  498.8 10.2 %shard_map.336 = (bf16[128,1536]{1,0:T(8,128)(2,1)S(1)}, bf16[128,1792]{1,0:T(8,128)(2,1)S(1)}, bf16[128,1792]{1,0:T(8,128)(2,1)S(1)}, f32[8,128]{1,0:T(8,128)S(1)}) custom-call(bf16[128,1536]{1,0:T(8,128)(2,1)S(1)} %copy-done.118, f32[128,1792]{1,0:T(8,128)S(1)} %get-tuple-element.388.refs_1_, f32[128,1792]{1,0:T(8,128)S(1)} %get-tuple-element.389.refs_2_, ...), custom_call_target="tpu_custom_call" | custom-call | tf_op jit(solution)/shard_map/pallas_call | solution.py:131
  509.7 10.2 %shard_map.337 = (bf16[128,1536]{1,0:T(8,128)(2,1)S(1)}, bf16[128,1792]{1,0:T(8,128)(2,1)S(1)}, bf16[128,1792]{1,0:T(8,128)(2,1)S(1)}, f32[8,128]{1,0:T(8,128)S(1)}) custom-call(bf16[128,1536]{1,0:T(8,128)(2,1)S(1)} %copy-done.120, f32[128,1792]{1,0:T(8,128)S(1)} %get-tuple-element.385.refs_1_, f32[128,1792]{1,0:T(8,128)S(1)} %get-tuple-element.386.refs_2_, ...), custom_call_target="tpu_custom_call" | custom-call | tf_op jit(solution)/shard_map/pallas_call | solution.py:131
  527.1 9.9 collective-permute-done.65.refs_5_
  553.6 12.3 %shard_map.341 = (bf16[1536,3584]{1,0:T(8,128)(2,1)S(1)}, f32[8,128]{1,0:T(8,128)S(1)}) custom-call(bf16[128,1536]{1,0:T(8,128)(2,1)} %get-tuple-element.374.refs_0_, bf16[128,1536]{1,0:T(8,128)(2,1)} %collective-permute-done.58.refs_1_, bf16[128,1536]{1,0:T(8,128)(2,1)} %collective-permute-done.60.refs_0_.refs_2_, ...), custom_call_target="tpu_custom_call" | custom-call | flops 16911433728 | bytes 66060288 | tf_op jit(solution)/shard_map/pallas_call | solution.py:131
  606.3 9.1 collective-permute-done.73.refs_5_
  625.4 10.1 collective-permute-done.75.refs_1_
  635.5 10.8 %shard_map.347 = (f32[128,1536]{1,0:T(8,128)S(1)}, bf16[128,1536]{1,0:T(8,128)(2,1)S(1)}, bf16[256,1792]{1,0:T(8,128)(2,1)S(1)}, bf16[256,1792]{1,0:T(8,128)(2,1)S(1)}, f32[8,128]{1,0:T(8,128)S(1)}) custom-call(bf16[128,1536]{1,0:T(8,128)(2,1)S(1)} %get-tuple-element.439.refs_0_, bf16[128,1536]{1,0:T(8,128)(2,1)S(1)} %collective-permute-done.75.refs_1_, ...), custom_call_target="tpu_custom_call" | custom-call | tf_op jit(solution)/shard_map/pallas_call | solution.py:131
  651.7 10.3 %shard_map.348 = (bf16[128,1536]{1,0:T(8,128)(2,1)S(1)}, bf16[128,1792]{1,0:T(8,128)(2,1)S(1)}, bf16[128,1792]{1,0:T(8,128)(2,1)S(1)}, f32[8,128]{1,0:T(8,128)S(1)}) custom-call(bf16[128,1536]{1,0:T(8,128)(2,1)S(1)} %collective-permute-done.77.refs_0_.refs_2_, f32[128,1792]{1,0:T(8,128)S(1)} %copy-done.101, f32[128,1792]{1,0:T(8,128)S(1)} %copy-done.103, ...), custom_call_target="tpu_custom_call" | custom-call | tf_op jit(solution)/shard_map/pallas_call | solution.py:131
  665.4 10.3 %shard_map.349 = (bf16[128,1536]{1,0:T(8,128)(2,1)S(1)}, bf16[128,1792]{1,0:T(8,128)(2,1)S(1)}, bf16[128,1792]{1,0:T(8,128)(2,1)S(1)}, f32[8,128]{1,0:T(8,128)S(1)}) custom-call(bf16[128,1536]{1,0:T(8,128)(2,1)S(1)} %collective-permute-done.79.refs_0_.refs_3_, f32[128,1792]{1,0:T(8,128)S(1)} %copy-done.97, f32[128,1792]{1,0:T(8,128)S(1)} %copy-done.99, ...), custom_call_target="tpu_custom_call" | custom-call | tf_op jit(solution)/shard_map/pallas_call | solution.py:131
  703.0 12.0 %shard_map.352 = (bf16[1536,3584]{1,0:T(8,128)(2,1)S(1)}, f32[8,128]{1,0:T(8,128)S(1)}) custom-call(bf16[128,1536]{1,0:T(8,128)(2,1)} %get-tuple-element.343.refs_0_, bf16[128,1536]{1,0:T(8,128)(2,1)S(1)} %copy-done.127, bf16[128,1536]{1,0:T(8,128)(2,1)S(1)} %copy-done.123, bf16[128,1536]{1,0:T(8,128)(2,1)S(1)} %copy-done.125, ...), custom_call_target="tpu_custom_call" | custom-call | flops 16911433728 | bytes 66060288 | tf_op jit(solution)/shard_map/pallas_call | solution.py:131
  763.8 26.9 %collective-permute-done.87.refs_2_.refs_4_ = bf16[10,48,768]{2,1,0:T(8,128)(2,1)S(1)} collective-permute-done((bf16[10,48,768]{2,1,0:T(8,128)(2,1)S(1)}, bf16[10,48,768]{2,1,0:T(8,128)(2,1)S(1)}, u32[]{:S(2)}, u32[]{:S(2)}) %collective-permute-start.87) | collective-permute-done | bytes 737312 | tf_op jit(solution)/shard_map/ppermute | solution.py:48
  794.6 14.6 %collective-permute-done.92.refs_8_.refs_3_ = bf16[48,3584]{1,0:T(8,128)(2,1)S(1)} collective-permute-done((bf16[48,3584]{1,0:T(8,128)(2,1)S(1)}, bf16[48,3584]{1,0:T(8,128)(2,1)S(1)}, u32[]{:S(2)}, u32[]{:S(2)}) %collective-permute-start.92) | collective-permute-done | bytes 344096 | tf_op jit(solution)/shard_map/ppermute | solution.py:48
  814.7 10.3 %collective-permute-done.93.refs_9_.refs_4_ = bf16[48,3584]{1,0:T(8,128)(2,1)S(1)} collective-permute-done((bf16[48,3584]{1,0:T(8,128)(2,1)S(1)}, bf16[48,3584]{1,0:T(8,128)(2,1)S(1)}, u32[]{:S(2)}, u32[]{:S(2)}) %collective-permute-start.93) | collective-permute-done | bytes 344096 | tf_op jit(solution)/shard_map/ppermute | solution.py:48
  852.4 21.1 %collective-permute-done.95.refs_4_.refs_3_ = bf16[10,48,768]{2,1,0:T(8,128)(2,1)} collective-permute-done((bf16[10,48,768]{2,1,0:T(8,128)(2,1)}, bf16[10,48,768]{2,1,0:T(8,128)(2,1)}, u32[]{:S(2)}, u32[]{:S(2)}) %collective-permute-start.95) | collective-permute-done | bytes 737312 | tf_op jit(solution)/shard_map/ppermute | solution.py:48
  889.3 17.6 %collective-permute-done.125 = f32[10,48]{1,0:T(8,128)S(1)} collective-permute-done((f32[10,48]{1,0:T(8,128)S(1)}, f32[10,48]{1,0:T(8,128)S(1)}, u32[]{:S(2)}, u32[]{:S(2)}) %collective-permute-start.125) | collective-permute-done | bytes 1952 | tf_op jit(solution)/shard_map/ppermute | solution.py:48
  (761 shorter events, 542.0 us)
Async XLA Ops:
  7.2 251.9 %all-gather.7.cloned.1.call-start = ((), (), s32[]{:S(2)}) async-start(), calls=%async_computation.4 | async-start | bytes 6193152 | tf_op jit(solution)/shard_map/all_gather | solution.py:338
  11.0 248.0 %all-gather.5.cloned.1.call-start = ((), (), s32[]{:S(2)}) async-start(), calls=%async_computation.3 | async-start | bytes 12386304 | tf_op jit(solution)/shard_map/all_gather | solution.py:338
  37.9 53.5 %collective-permute-start.24 = (bf16[10,48,768]{2,1,0:T(8,128)(2,1)}, bf16[10,48,768]{2,1,0:T(8,128)(2,1)S(1)}, u32[]{:S(2)}, u32[]{:S(2)}) collective-permute-start(bf16[10,48,768]{2,1,0:T(8,128)(2,1)} %get-tuple-element.317.refs_2_), channel_id=1, source_target_pairs={{0,1},{1,0},{2,3},{3,2},{4,5},{5,4},{6,7},{7,6},{8,9},{9,8},{10,11... | collective-permute-start | bytes 2211848 | tf_op jit(solution)/shard_map/ppermute | solution.py:48
  86.0 48.7 %collective-permute-start.25 = (bf16[10,48,768]{2,1,0:T(8,128)(2,1)}, bf16[10,48,768]{2,1,0:T(8,128)(2,1)S(1)}, u32[]{:S(2)}, u32[]{:S(2)}) collective-permute-start(bf16[10,48,768]{2,1,0:T(8,128)(2,1)} %get-tuple-element.317.refs_2_), channel_id=1, source_target_pairs={{0,2},{1,3},{2,0},{3,1},{4,6},{5,7},{6,4},{7,5},{8,10},{9,11},{10,... | collective-permute-start | bytes 2211848 | tf_op jit(solution)/shard_map/ppermute | solution.py:48
  89.9 62.1 %collective-permute-start.29 = (bf16[10,48,768]{2,1,0:T(8,128)(2,1)}, bf16[10,48,768]{2,1,0:T(8,128)(2,1)S(1)}, u32[]{:S(2)}, u32[]{:S(2)}) collective-permute-start(bf16[10,48,768]{2,1,0:T(8,128)(2,1)} %get-tuple-element.317.refs_2_), channel_id=1, source_target_pairs={{0,3},{1,2},{2,1},{3,0},{4,7},{5,6},{6,5},{7,4},{8,11},{9,10},{10,... | collective-permute-start | bytes 2211848 | tf_op jit(solution)/shard_map/ppermute | solution.py:48
  157.4 281.9 %all-gather.11.cloned.1.call-start = ((), (), s32[]{:S(2)}) async-start(), calls=%async_computation.6 | async-start | bytes 6193152 | tf_op jit(solution)/shard_map/all_gather | solution.py:338
  169.2 67.3 %collective-permute-start.35 = (bf16[10,48,768]{2,1,0:T(8,128)(2,1)S(1)}, bf16[10,48,768]{2,1,0:T(8,128)(2,1)S(1)}, u32[]{:S(2)}, u32[]{:S(2)}) collective-permute-start(bf16[10,48,768]{2,1,0:T(8,128)(2,1)S(1)} %get-tuple-element.339.refs_10_), channel_id=1, source_target_pairs={{0,2},{1,3},{2,0},{3,1},{4,6},{5,7},{6,4},{7,5},{8,10},{9,11},{10,... | collective-permute-start | bytes 2211848 | tf_op jit(solution)/shard_map/ppermute | solution.py:48
  172.8 46.3 %collective-permute-start.37 = (bf16[1,48,3584]{2,1,0:T(8,128)(2,1)S(1)}, bf16[1,48,3584]{2,1,0:T(8,128)(2,1)S(1)}, u32[]{:S(2)}, u32[]{:S(2)}) collective-permute-start(bf16[1,48,3584]{2,1,0:T(8,128)(2,1)S(1)} %get-tuple-element.584), channel_id=1, source_target_pairs={{0,2},{1,3},{2,0},{3,1},{4,6},{5,7},{6,4},{7,5},{8,10},{9,11},{10,... | collective-permute-start | bytes 1032200 | tf_op jit(solution)/shard_map/ppermute | solution.py:48
  176.1 60.4 %collective-permute-start.32 = (bf16[128,1536]{1,0:T(8,128)(2,1)S(1)}, bf16[128,1536]{1,0:T(8,128)(2,1)S(1)}, u32[]{:S(2)}, u32[]{:S(2)}) collective-permute-start(bf16[128,1536]{1,0:T(8,128)(2,1)S(1)} %get-tuple-element.336), channel_id=1, source_target_pairs={{0,8},{4,12},{8,0},{12,4},{16,24},{20,28},{24,16},{28,20},{1,9},{5... | collective-permute-start | bytes 1179656 | tf_op jit(solution)/shard_map/ppermute | solution.py:39
  176.6 59.9 %collective-permute-start.33 = (bf16[128,1536]{1,0:T(8,128)(2,1)S(1)}, bf16[128,1536]{1,0:T(8,128)(2,1)S(1)}, u32[]{:S(2)}, u32[]{:S(2)}) collective-permute-start(bf16[128,1536]{1,0:T(8,128)(2,1)S(1)} %get-tuple-element.337), channel_id=1, source_target_pairs={{0,16},{4,20},{8,24},{12,28},{16,0},{20,4},{24,8},{28,12},{1,17},{... | collective-permute-start | bytes 1179656 | tf_op jit(solution)/shard_map/ppermute | solution.py:39
  197.3 39.2 %collective-permute-start.34 = (bf16[128,1536]{1,0:T(8,128)(2,1)S(1)}, bf16[128,1536]{1,0:T(8,128)(2,1)S(1)}, u32[]{:S(2)}, u32[]{:S(2)}) collective-permute-start(bf16[128,1536]{1,0:T(8,128)(2,1)S(1)} %get-tuple-element.338), channel_id=1, source_target_pairs={{0,24},{4,28},{8,16},{12,20},{16,8},{20,12},{24,0},{28,4},{1,25},{... | collective-permute-start | bytes 1179656 | tf_op jit(solution)/shard_map/ppermute | solution.py:39
  237.7 201.7 %all-gather.9.cloned.1.call-start = ((), (), s32[]{:S(2)}) async-start(), calls=%async_computation.5 | async-start | bytes 12386304 | tf_op jit(solution)/shard_map/all_gather | solution.py:338
  242.1 477.0 %reduce-scatter.4.cloned.1.call-start = ((), (), s32[]{:S(2)}) async-start(), calls=%async_computation.7 | async-start | bytes 12386304 | tf_op jit(solution)/shard_map/reduce_scatter | solution.py:444
  244.4 42.1 %collective-permute-start.43 = (bf16[128,1536]{1,0:T(8,128)(2,1)}, bf16[128,1536]{1,0:T(8,128)(2,1)S(1)}, u32[]{:S(2)}, u32[]{:S(2)}) collective-permute-start(bf16[128,1536]{1,0:T(8,128)(2,1)} %get-tuple-element.343.refs_0_), channel_id=1, source_target_pairs={{0,3},{1,2},{2,1},{3,0},{4,7},{5,6},{6,5},{7,4},{8,11},{9,10},{10,... | collective-permute-start | bytes 1179656 | tf_op jit(solution)/shard_map/ppermute | solution.py:48
  245.9 47.6 %collective-permute-start.45 = (bf16[10,48,768]{2,1,0:T(8,128)(2,1)S(1)}, bf16[10,48,768]{2,1,0:T(8,128)(2,1)S(1)}, u32[]{:S(2)}, u32[]{:S(2)}) collective-permute-start(bf16[10,48,768]{2,1,0:T(8,128)(2,1)S(1)} %get-tuple-element.353.refs_2_), channel_id=1, source_target_pairs={{0,1},{1,0},{2,3},{3,2},{4,5},{5,4},{6,7},{7,6},{8,9},{9,8},{10,11... | collective-permute-start | bytes 2211848 | tf_op jit(solution)/shard_map/ppermute | solution.py:48
  395.2 36.2 %collective-permute-start.57 = (bf16[128,1536]{1,0:T(8,128)(2,1)S(1)}, bf16[128,1536]{1,0:T(8,128)(2,1)S(1)}, u32[]{:S(2)}, u32[]{:S(2)}) collective-permute-start(bf16[128,1536]{1,0:T(8,128)(2,1)S(1)} %bitcast.136), channel_id=1, source_target_pairs={{0,3},{1,2},{2,1},{3,0},{4,7},{5,6},{6,5},{7,4},{8,11},{9,10},{10,... | collective-permute-start | bytes 1179656 | tf_op jit(solution)/shard_map/ppermute | solution.py:48
  397.3 36.5 %collective-permute-start.52 = (bf16[128,1536]{1,0:T(8,128)(2,1)S(1)}, bf16[128,1536]{1,0:T(8,128)(2,1)S(1)}, u32[]{:S(2)}, u32[]{:S(2)}) collective-permute-start(bf16[128,1536]{1,0:T(8,128)(2,1)S(1)} %get-tuple-element.368), channel_id=1, source_target_pairs={{0,8},{4,12},{8,0},{12,4},{16,24},{20,28},{24,16},{28,20},{1,9},{5... | collective-permute-start | bytes 1179656 | tf_op jit(solution)/shard_map/ppermute | solution.py:39
  437.6 39.9 %collective-permute-start.62 = (bf16[128,1536]{1,0:T(8,128)(2,1)}, bf16[128,1536]{1,0:T(8,128)(2,1)}, u32[]{:S(2)}, u32[]{:S(2)}) collective-permute-start(bf16[128,1536]{1,0:T(8,128)(2,1)} %get-tuple-element.374.refs_0_), channel_id=1, source_target_pairs={{0,3},{1,2},{2,1},{3,0},{4,7},{5,6},{6,5},{7,4},{8,11},{9,10},{10,... | collective-permute-start | bytes 1179656 | tf_op jit(solution)/shard_map/ppermute | solution.py:48
  468.2 51.8 %collective-permute-start.59 = (bf16[128,1536]{1,0:T(8,128)(2,1)}, bf16[128,1536]{1,0:T(8,128)(2,1)S(1)}, u32[]{:S(2)}, u32[]{:S(2)}) collective-permute-start(bf16[128,1536]{1,0:T(8,128)(2,1)} %get-tuple-element.379), channel_id=1, source_target_pairs={{0,1},{1,0},{2,3},{3,2},{4,5},{5,4},{6,7},{7,6},{8,9},{9,8},{10,11... | collective-permute-start | bytes 1179656 | tf_op jit(solution)/shard_map/ppermute | solution.py:48
  477.0 44.1 %collective-permute-start.61 = (bf16[128,1536]{1,0:T(8,128)(2,1)S(1)}, bf16[128,1536]{1,0:T(8,128)(2,1)S(1)}, u32[]{:S(2)}, u32[]{:S(2)}) collective-permute-start(bf16[128,1536]{1,0:T(8,128)(2,1)S(1)} %get-tuple-element.381), channel_id=1, source_target_pairs={{0,2},{1,3},{2,0},{3,1},{4,6},{5,7},{6,4},{7,5},{8,10},{9,11},{10,... | collective-permute-start | bytes 1179656 | tf_op jit(solution)/shard_map/ppermute | solution.py:48
  483.8 37.9 %collective-permute-start.63 = (bf16[128,1536]{1,0:T(8,128)(2,1)S(1)}, bf16[128,1536]{1,0:T(8,128)(2,1)S(1)}, u32[]{:S(2)}, u32[]{:S(2)}) collective-permute-start(bf16[128,1536]{1,0:T(8,128)(2,1)S(1)} %get-tuple-element.383), channel_id=1, source_target_pairs={{0,3},{1,2},{2,1},{3,0},{4,7},{5,6},{6,5},{7,4},{8,11},{9,10},{10,... | collective-permute-start | bytes 1179656 | tf_op jit(solution)/shard_map/ppermute | solution.py:48
  574.8 277.7 %reduce-scatter.8.cloned.1.call-start = ((), (), s32[]{:S(2)}) async-start(), calls=%async_computation.9 | async-start | bytes 6193152 | tf_op jit(solution)/shard_map/reduce_scatter | solution.py:444
  575.4 372.9 %reduce-scatter.6.cloned.1.call-start = ((), (), s32[]{:S(2)}) async-start(), calls=%async_computation.8 | async-start | bytes 12386304 | tf_op jit(solution)/shard_map/reduce_scatter | solution.py:444
  625.3 40.1 %collective-permute-start.79 = (bf16[128,1536]{1,0:T(8,128)(2,1)S(1)}, bf16[128,1536]{1,0:T(8,128)(2,1)S(1)}, u32[]{:S(2)}, u32[]{:S(2)}) collective-permute-start(bf16[128,1536]{1,0:T(8,128)(2,1)S(1)} %get-tuple-element.439.refs_0_), channel_id=1, source_target_pairs={{0,3},{1,2},{2,1},{3,0},{4,7},{5,6},{6,5},{7,4},{8,11},{9,10},{10,... | collective-permute-start | bytes 1179656 | tf_op jit(solution)/shard_map/ppermute | solution.py:48
  760.7 66.0 %collective-permute-start.97 = (bf16[10,48,768]{2,1,0:T(8,128)(2,1)S(1)}, bf16[10,48,768]{2,1,0:T(8,128)(2,1)S(1)}, u32[]{:S(2)}, u32[]{:S(2)}) collective-permute-start(bf16[10,48,768]{2,1,0:T(8,128)(2,1)S(1)} %copy-done.57), channel_id=1, source_target_pairs={{0,1},{1,0},{2,3},{3,2},{4,5},{5,4},{6,7},{7,6},{8,9},{9,8},{10,11... | collective-permute-start | bytes 2211848 | tf_op jit(solution)/shard_map/ppermute | solution.py:48
  760.7 48.5 %collective-permute-start.92 = (bf16[48,3584]{1,0:T(8,128)(2,1)S(1)}, bf16[48,3584]{1,0:T(8,128)(2,1)S(1)}, u32[]{:S(2)}, u32[]{:S(2)}) collective-permute-start(bf16[48,3584]{1,0:T(8,128)(2,1)S(1)} %copy-done.159), channel_id=1, source_target_pairs={{0,2},{1,3},{2,0},{3,1},{4,6},{5,7},{6,4},{7,5},{8,10},{9,11},{10,... | collective-permute-start | bytes 1032200 | tf_op jit(solution)/shard_map/ppermute | solution.py:48
  838.4 42.3 %collective-permute-start.105 = (bf16[4,224,1536]{2,1,0:T(8,128)(2,1)}, bf16[4,224,1536]{2,1,0:T(8,128)(2,1)}, u32[]{:S(2)}, u32[]{:S(2)}) collective-permute-start(bf16[4,224,1536]{2,1,0:T(8,128)(2,1)} %get-tuple-element.515), channel_id=1, source_target_pairs={{0,4},{4,0},{8,12},{12,8},{16,20},{20,16},{24,28},{28,24},{1,5},{5... | collective-permute-start | bytes 8257544 | tf_op jit(solution)/shard_map/ppermute | solution.py:39
  849.0 100.7 %collective-permute-start.94 = (bf16[10,48,768]{2,1,0:T(8,128)(2,1)}, bf16[10,48,768]{2,1,0:T(8,128)(2,1)}, u32[]{:S(2)}, u32[]{:S(2)}) collective-permute-start(bf16[10,48,768]{2,1,0:T(8,128)(2,1)} %copy-done.108), channel_id=1, source_target_pairs={{0,1},{1,0},{2,3},{3,2},{4,5},{5,4},{6,7},{7,6},{8,9},{9,8},{10,11... | collective-permute-start | bytes 2211848 | tf_op jit(solution)/shard_map/ppermute | solution.py:48
  849.2 100.7 %collective-permute-start.96 = (bf16[10,48,768]{2,1,0:T(8,128)(2,1)}, bf16[10,48,768]{2,1,0:T(8,128)(2,1)}, u32[]{:S(2)}, u32[]{:S(2)}) collective-permute-start(bf16[10,48,768]{2,1,0:T(8,128)(2,1)} %copy-done.110), channel_id=1, source_target_pairs={{0,3},{1,2},{2,1},{3,0},{4,7},{5,6},{6,5},{7,4},{8,11},{9,10},{10,... | collective-permute-start | bytes 2211848 | tf_op jit(solution)/shard_map/ppermute | solution.py:48
  850.8 66.0 %collective-permute-start.98 = (bf16[48,768]{1,0:T(8,128)(2,1)}, bf16[48,768]{1,0:T(8,128)(2,1)S(1)}, u32[]{:S(2)}, u32[]{:S(2)}) collective-permute-start(bf16[48,768]{1,0:T(8,128)(2,1)} %get-tuple-element.622), channel_id=1, source_target_pairs={{0,4},{4,0},{8,12},{12,8},{16,20},{20,16},{24,28},{28,24},{1,5},{5... | collective-permute-start | bytes 221192 | tf_op jit(solution)/shard_map/ppermute | solution.py:39
  885.6 66.7 %collective-permute-start.116 = (bf16[224,1536]{1,0:T(8,128)(2,1)}, bf16[224,1536]{1,0:T(8,128)(2,1)}, u32[]{:S(2)}, u32[]{:S(2)}) collective-permute-start(bf16[224,1536]{1,0:T(8,128)(2,1)} %get-tuple-element.535), channel_id=1, source_target_pairs={{0,8},{4,12},{8,0},{12,4},{16,24},{20,28},{24,16},{28,20},{1,9},{5... | collective-permute-start | bytes 2064392 | tf_op jit(solution)/shard_map/ppermute | solution.py:39
  964.5 36.2 %collective-permute-start.108 = (bf16[48,768]{1,0:T(8,128)(2,1)S(1)}, bf16[48,768]{1,0:T(8,128)(2,1)S(1)}, u32[]{:S(2)}, u32[]{:S(2)}) collective-permute-start(bf16[48,768]{1,0:T(8,128)(2,1)S(1)} %get-tuple-element.612), channel_id=1, source_target_pairs={{0,12},{4,8},{8,4},{12,0},{16,28},{20,24},{24,20},{28,16},{1,13},{... | collective-permute-start | bytes 221192 | tf_op jit(solution)/shard_map/ppermute | solution.py:39
  (296 other events, 4249.8 us)
Sparse Core Ops, SparseCore 0:
  11.1 49.6 all-gather.6
  157.6 82.2 all-gather.4
  241.8 40.4 all-gather.10
  284.6 82.3 all-gather.8
  574.9 93.0 reduce-scatter.3
  671.3 68.6 reduce-scatter.7
  744.0 102.3 reduce-scatter.5

commit v3 on v2

--- a/solution.py
+++ b/solution.py
@@ -136,9 +136,9 @@
         scratch_shapes=list(scratch),
         input_output_aliases=aliases,
         compiler_params=pltpu.CompilerParams(
-            vmem_limit_bytes=min(
-                vmem_of(operands, in_specs, out_shape, out_specs, scratch, grid), 60 << 20
-            )
+            vmem_limit_bytes=56 << 20
+            if cost[0]
+            else min(vmem_of(operands, in_specs, out_shape, out_specs, scratch, grid), 60 << 20)
         ),
         cost_estimate=pl.CostEstimate(
             flops=cost[0], bytes_accessed=cost[1], transcendentals=0
@@ -201,28 +201,22 @@
     return pl.BlockSpec(shape, lambda i: (0,) * len(shape))
 
 
-def pack_mix(mix_weight, layer, wide, earlier=()):
+def pack_mix(mix_weight, layer, earlier=()):
     seqs = lax.axis_size("seq")
     rows, columns = mix_weight.shape[1:]
     features = columns // 4
     chunk = features // seqs
-    outer = features // (3 * wide)
 
     def body(place, weight, *refs):
         out = refs[-1]
         for s in range(seqs):
             slot = lax.bitwise_xor(place[0], jnp.int32(s))
-            for g in range(3):
+            for g in range(4):
                 start = g * features + s * chunk
                 piece = weight[0, :, start : start + chunk].astype(low)
-                if wide > chunk:
-                    piece = jnp.concatenate([piece, jnp.zeros((rows, wide - chunk), low)], axis=1)
-                out[slot, :, g * wide : (g + 1) * wide] = piece
-        for i in range(outer):
-            start = 3 * features + i * 3 * wide
-            out[seqs + i] = weight[0, :, start : start + 3 * wide].astype(low)
-
-    shape = (seqs + outer, rows, 3 * wide)
+                out[slot if g < 3 else s, :, g * chunk : (g + 1) * chunk] = piece
+
+    shape = (seqs, rows, 4 * chunk)
     return kernel_call(
         body,
         (1,),
@@ -233,22 +227,25 @@
     )(place_of("seq"), mix_weight, *earlier)
 
 
-def assemble_mix(pieces, wide, features):
-    seqs, rings = lax.axis_size("seq"), lax.axis_size("fsdp")
-    outer, rows, _ = pieces[0].shape
-    outer = outer - seqs
-    rotated = isinstance(pieces, list)
-    pieces = pieces if rotated else [pieces]
+def assemble_mix(pieces, wide):
+    rings = len(pieces)
+    seqs, rows, width = pieces[0].shape
+    chunk = width // 4
+    features = seqs * chunk
 
     def body(place_seq, place_fsdp, *refs):
-        inner_out, outer_out = refs[-2:]
-        refs = refs if rotated else [refs[0].at[j] for j in range(rings)]
+        inner_out, outer_out = refs[rings:]
         for j in range(rings):
-            f = lax.bitwise_xor(place_fsdp[0], jnp.int32(j)) if rotated else j
+            f = lax.bitwise_xor(place_fsdp[0], jnp.int32(j))
             for s in range(seqs):
-                inner_out[lax.bitwise_xor(place_seq[0], jnp.int32(s)), f] = refs[j][s]
-            for i in range(outer):
-                outer_out[f, :, i * 3 * wide : (i + 1) * 3 * wide] = refs[j][seqs + i]
+                owner = lax.bitwise_xor(place_seq[0], jnp.int32(s))
+                for g in range(3):
+                    piece = refs[j][s, :, g * chunk : (g + 1) * chunk]
+                    if wide > chunk:
+                        gap = jnp.zeros((rows, wide - chunk), low)
+                        piece = jnp.concatenate([piece, gap], axis=1)
+                    inner_out[owner, f, :, g * wide : (g + 1) * wide] = piece
+                outer_out[f, :, s * chunk : (s + 1) * chunk] = refs[j][s, :, 3 * chunk :]
 
     inner_shape = (seqs, rings, rows, 3 * wide)
     outer_shape = (rings, rows, features)
@@ -268,9 +265,10 @@
 
     def body(*refs):
         out = refs[-1]
+        split = out.shape[-1] // 4 * 3
         for s in range(seqs):
-            out[s] = refs[s][0]
-        out[seqs:] = refs[seqs][seqs:]
+            out[s, :, :split] = refs[s][0, :, :split]
+            out[s, :, split:] = refs[seqs][s, :, split:]
 
     return plain_call(body, [shaped(packed.shape, low)], earlier=earlier)(*parts, packed)[0]
 
@@ -348,11 +346,21 @@
     rows, columns = weight.shape[1:]
     tile = 16 if rows % 16 == 0 else rows
     width = 768
-    specs = [
-        pl.BlockSpec(grad.shape if tile == rows else (tile, grad.shape[-1]), lambda i: (i, 0))
-        for grad in grads
-    ]
-    part = pl.BlockSpec((1, tile, columns), lambda i: (layer, i, 0))
+    steps = rows // tile
+    if layer is None:
+        each = steps
+        where = lambda i: (lax.div(i, each), lax.rem(i, each), 0)
+        specs = [pl.BlockSpec((1, tile, grad.shape[-1]), where) for grad in grads]
+        steps = LAYERS * each
+    else:
+        where = lambda i: (layer, i, 0)
+        specs = [
+            pl.BlockSpec(
+                grad.shape if tile == rows else (tile, grad.shape[-1]), lambda i: (i, 0)
+            )
+            for grad in grads
+        ]
+    part = pl.BlockSpec((1, tile, columns), where)
     kept = (0 if previous is None else 3) + len(earlier)
     before = len(scalars) + len(grads)
 
@@ -375,7 +383,7 @@
 
     return kernel_call(
         body,
-        (rows // tile,),
+        (steps,),
         [scalar] * len(scalars)
         + specs
         + [part] * 3
@@ -388,55 +396,53 @@
     )(*scalars, *grads, *state, *(previous or ()), *earlier)
 
 
-def mix_reduce(pieces):
-    seqs, rings = lax.axis_size("seq"), lax.axis_size("fsdp")
-    count, rows, width = pieces[0].shape
-    outer = count - seqs
+def mix_reduce(layers):
+    seqs, rows, width = layers[0][0].shape
+    count, rings = len(layers), len(layers[0])
+    chunk = width // 4
 
     def body(place, *refs):
-        inner_out, outer_out = refs[rings:]
-        for s in range(seqs):
-            total = refs[0][s].astype(jnp.float32)
-            for j in range(1, rings):
-                total = total + refs[j][s].astype(jnp.float32)
-            inner_out[lax.bitwise_xor(place[0], jnp.int32(s))] = total.astype(low)
-        for i in range(outer):
-            total = refs[0][seqs + i].astype(jnp.float32)
-            for j in range(1, rings):
-                total = total + refs[j][seqs + i].astype(jnp.float32)
-            outer_out[:, i * width : (i + 1) * width] = total
+        inner_out, outer_out = refs[count * rings :]
+        for layer in range(count):
+            parts = refs[layer * rings : (layer + 1) * rings]
+            for s in range(seqs):
+                total = parts[0][s].astype(jnp.float32)
+                for part in parts[1:]:
+                    total = total + part[s].astype(jnp.float32)
+                inner_out[lax.bitwise_xor(place[0], jnp.int32(s)), layer] = total.astype(low)
+                outer_out[layer, :, s * chunk : (s + 1) * chunk] = total[:, 3 * chunk :]
 
     inner, last = plain_call(
         body,
-        [shaped((seqs, rows, width), low), shaped((rows, outer * width))],
+        [shaped((seqs, count, rows, width), low), shaped((count, rows, seqs * chunk))],
         scalars=1,
-    )(place_of("seq"), *pieces)
+    )(place_of("seq"), *sum((list(pieces) for pieces in layers), []))
     return [inner[0]] + [seq_swap(inner[j], j) for j in range(1, seqs)] + [last]
 
 
-def mix_adam(grads, state, layer, previous, wide):
+def mix_adam(grads, state):
     seqs = lax.axis_size("seq")
     features = state[0].shape[2] // 4
     chunk = features // seqs
 
     def load(scalars, grads, scratch, total):
         for s in range(seqs):
-            scratch[0][lax.bitwise_xor(scalars[0][0], jnp.int32(s))] = grads[s][...]
+            scratch[0][lax.bitwise_xor(scalars[0][0], jnp.int32(s))] = grads[s][0]
         for s in range(seqs):
             for g in range(3):
                 start = g * features + s * chunk
-                piece = scratch[0][s, :, g * wide : g * wide + chunk]
+                piece = scratch[0][s, :, g * chunk : (g + 1) * chunk]
                 total[:, start : start + chunk] = piece.astype(jnp.float32)
-        total[:, 3 * features :] = grads[seqs][...]
+        total[:, 3 * features :] = grads[seqs][0]
 
     return adam_kernel(
         load,
         [place_of("seq")],
         grads,
         state,
-        layer,
-        previous,
-        [lambda tile: pltpu.VMEM((seqs, tile, 3 * wide), low)],
+        None,
+        None,
+        [lambda tile: pltpu.VMEM((seqs, tile, 4 * chunk), low)],
     )
 
 
@@ -486,17 +492,17 @@
     )
 
 
-def down_adam(parts, state, layer, previous, earlier):
+def down_adam(parts, state, layer, previous):
     def load(scalars, grads, scratch, total):
         sums = grads[0][...].astype(jnp.float32)
         for grad in grads[1:]:
             sums = sums + grad[...].astype(jnp.float32)
         total[...] = sums[: total.shape[0]]
 
-    return adam_kernel(load, [], parts, state, layer, previous, earlier=earlier)
-
-
-def split_down(part):
+    return adam_kernel(load, [], parts, state, layer, previous)
+
+
+def split_down(part, earlier):
     seqs = lax.axis_size("seq")
     part = part.reshape(seqs, -1, part.shape[-1])
 
@@ -506,7 +512,10 @@
             (even, odd)[i % 2][i // 2] = part[owner]
 
     return plain_call(
-        body, [shaped((seqs // 2,) + part.shape[1:], part.dtype)] * 2, scalars=1
+        body,
+        [shaped((seqs // 2,) + part.shape[1:], part.dtype)] * 2,
+        scalars=1,
+        earlier=earlier,
     )(place_of("seq"), part)
 
 
@@ -632,7 +641,7 @@
     )(flow, stream, gain, *sums)
 
 
-def pair_sum(even, received, earlier=()):
+def pair_sum(even, received, earlier=(), carried=()):
     half, tokens, features = even.shape
 
     def body(even, received, *outs):
@@ -644,8 +653,9 @@
         body,
         [shaped((tokens, features))] + [shaped((tokens, features), low)] * (half - 1),
         earlier=earlier,
+        carried=carried,
     )(even, received)
-    return [outs[0]] + [seq_swap(outs[i], 2 * i) for i in range(1, half)]
+    return [outs[0]] + [seq_swap(outs[i], 2 * i) for i in range(1, half)], *outs[half:]
 
 
 def block_neighbour(place, i, count, step):
@@ -784,7 +794,7 @@
     features, width = normed[0].shape[-1], flows.shape[-1]
     half = normed[0].shape[0]
     wide = width // 3
-    count = features // width
+    chunk = mixed.shape[-1]
 
     def body(place, normed_even, normed_odd, flows, mixed, low_even, low_odd, *refs):
         outs, inner, outer = refs[:rings], refs[rings], refs[rings + 1]
@@ -804,13 +814,14 @@
         for j in range(rings):
             f = lax.bitwise_xor(place[0], jnp.int32(j))
             for s in range(seqs):
-                outs[j][s] = inner[s, f]
-            for i in range(count):
-                outs[j][seqs + i] = outer[f, :, i * width : (i + 1) * width]
+                for g in range(3):
+                    piece = inner[s, f, :, g * wide : g * wide + chunk]
+                    outs[j][s, :, g * chunk : (g + 1) * chunk] = piece
+                outs[j][s, :, 3 * chunk :] = outer[f, :, s * chunk : (s + 1) * chunk]
 
     return plain_call(
         body,
-        [shaped((seqs + count, rows, width), low)] * rings,
+        [shaped((seqs, rows, 4 * chunk), low)] * rings,
         scalars=1,
         scratch=[
             pltpu.VMEM((seqs, rings, rows, width), low),
@@ -1078,25 +1089,23 @@
     mixes, feeds = [None] * LAYERS, [None] * LAYERS
     vector_blocks = vectors_start(gain_weight, tap_weight)
     feed_swap = swap_feed(pack_feed(feed_weight, 0))
-    mix_packed = pack_mix(mix_weight, 0, wide, vector_blocks[1:])
+    mix_packed = pack_mix(mix_weight, 0, vector_blocks[1:])
     mix_swap = swap_mix(mix_packed)
     down_rows = gather_rows(pack_down(down_weight, 0))
     both, vector_blocks = vectors_middle(vector_blocks)
     mix_pieces = gather_fsdp(join_mix(mix_swap, mix_packed))
     feed_part = assemble_feed(feed_swap)
-    later_packed = pack_mix(mix_weight, 1, wide)
+    later_packed = pack_mix(mix_weight, 1)
     later_swap = swap_mix(later_packed)
     vector_blocks = stack_pairs(vector_blocks)
     later_piece = join_mix(later_swap, later_packed, mix_pieces[1:2])
     gain_rows, tap_rows = vectors_end(both, vector_blocks)
-    stream, normed = first_norm(
-        inputs.reshape(-1, features), gain_rows[0, 0], mix_pieces[2:3]
-    )
+    stream, normed = first_norm(inputs.reshape(-1, features), gain_rows[0, 0], ())
     blocks = send_seq(normed)
     later_feed = pack_feed(feed_weight, 1)
-    *blocks, feed_part = stack_pairs(blocks, mix_pieces[3:], [feed_part])
+    *blocks, feed_part = stack_pairs(blocks, mix_pieces[2:], [feed_part])
     feeds[0] = (gather_rows(feed_part), down_rows)
-    mixes[0] = assemble_mix(mix_pieces, wide, features)
+    mixes[0] = assemble_mix(mix_pieces, wide)
     later_mix = [None, None, fsdp_swap(later_piece, 2)] if rings > 2 else [None, None]
     later_feed = swap_feed(later_feed)
 
@@ -1107,17 +1116,17 @@
         projected, even, odd = mixer_forward(blocks, *mixes[layer], tap_rows[layer])
         odd = seq_swap(odd, 1)
         if last:
-            flow_blocks = gather_fsdp(cotangent)
-        sums = pair_sum(even, odd)
-        if last:
-            flow_low = join_blocks(flow_blocks)
+            sums, flow_low = pair_sum(even, odd, (), [cotangent])
+            flow_low = gather_fsdp(flow_low)
             middle, normed_two = finish(stream, sums, gain_rows[layer, 1])
+            flow_low = join_blocks(flow_low)
         else:
+            (sums,) = pair_sum(even, odd, later_feed[1:])
             middle, normed_two, later_piece, down_packed = finish(
                 stream,
                 sums,
                 gain_rows[layer, 1],
-                (*later_mix[2:], *later_feed[1:]),
+                later_mix[2:],
                 (later_piece, pack_down(down_weight, 1)),
             )
         two_blocks = gather_fsdp(normed_two)
@@ -1139,7 +1148,7 @@
             blocks = send_seq(normed)
             later_mix += [fsdp_swap(later_piece, by) for by in range(3, rings)]
             blocks = stack_pairs(blocks)
-            mixes[1] = assemble_mix(later_mix, wide, features)
+            mixes[1] = assemble_mix(later_mix, wide)
 
     states = (
         (mix_weight, mix_first, mix_second),
@@ -1184,10 +1193,15 @@
         even, odd, flows, mixed, tap_grads[layer] = mixer_backward(
             blocks, projected, *mixes[layer], tap_rows[layer]
         )
-        sums = pair_sum(even, seq_swap(odd, 1), () if last else later_mix[3:])
+        (sums,) = pair_sum(even, seq_swap(odd, 1), () if last else later_feed[1:])
         mix_part = mixer_grads(gathered, flows, mixed, blocks, rows)
         flow, low_flow, gain_one, *mix_part = finish_back(
-            middle_flow, sums, stream, gain_rows[layer, 0], mix_part, () if last else later_feed[1:]
+            middle_flow,
+            sums,
+            stream,
+            gain_rows[layer, 0],
+            mix_part,
+            () if last else (later_mix[1], *later_mix[3:]),
         )
         if not last:
             mix_part = return_sums(mix_part)
@@ -1195,21 +1209,19 @@
         if last:
             flow_low = gather_fsdp(low_flow)
             later_mix, later_feed, later_down = mix_part, feed_part, down_part
-    later_mix = mix_reduce(later_mix)
     new[1] = feed_adam(later_feed, states[1], 1, new[1])
-    even, odd = split_down(down_part)
+    even, odd = split_down(down_part, mix_part[1:3])
     odd = seq_swap(odd, 1)
-    new[2] = down_adam(later_down, states[2], 1, new[2], mix_part[2:3])
-    down_part = pair_sum(even, odd)
+    new[2] = down_adam(later_down, states[2], 1, new[2])
+    (down_part,) = pair_sum(even, odd, mix_part[3:])
     gain_grad, tap_grad = vector_gradients(
         jnp.stack(gain_grads), jnp.stack(tap_grads), gain_weight.shape[-1]
     )
-    new[0] = mix_adam(later_mix, states[0], 1, new[0], wide)
+    mix_part = mix_reduce([mix_part, later_mix])
     feed_part = split_feed(feed_part, rows)
-    mix_part = mix_reduce(mix_part)
-    new[2] = down_adam(down_part, states[2], 0, new[2], ())
+    new[2] = down_adam(down_part, states[2], 0, new[2])
+    new[0] = mix_adam(mix_part, states[0])
     new[1] = feed_adam(feed_part, states[1], 0, new[1])
-    new[0] = mix_adam(mix_part, states[0], 0, new[0], wide)
     input_grad = flow.reshape(sequences, length, features)
     gain_new = adam_update(gain_weight, gain_first, gain_second, gain_grad, rate_vector, 0.0)
     tap_new = adam_update(tap_weight, tap_first, tap_second, tap_grad, rate_vector, 0.0)

time: 1020 us -> 1010 us (level)
  waiting for transfers between devices: 495 us -> 441 us
  Pallas kernels: 223 us -> 253 us
  local copies, waits for them, and re-layouts: 126 us -> 148 us
  starting transfers between devices: 145 us -> 132 us
    ppermute x54, waiting for transfers between devices: 386 us -> 302 us  [fsdp_swap(): return lax.ppermute(array, 'fsdp', [(i, i ^ by) for i in range(count)])]
    ppermute x72 -> x65, waiting for transfers between devices: 108 us -> 139 us  [seq_swap(): return lax.ppermute(array, 'seq', [(i, i ^ by) for i in range(count)])]
    pallas_call x65 -> x63, Pallas kernels: 223 us -> 253 us  [ordered_call(): pl.pallas_call(marked, in_specs=list(in_specs) + [anywhere], out_specs=li...]
    unnamed x400 -> x491, local copies, waits for them, and re-layouts: 119 us -> 144 us
    ppermute x72 -> x65, starting transfers between devices: 75.7 us -> 63.7 us  [seq_swap(): return lax.ppermute(array, 'seq', [(i, i ^ by) for i in range(count)])]
  transfers between devices with their start and end apart: 133 -> 126, of which waited for: 61 -> 62; matrix products, arithmetic and copies ran while one was open for 1% -> 1% of each run, Pallas kernels for 22% -> 25%
where the time goes in v3:
time: 1010 us; the launch traced here: 994 us
  waiting for transfers between devices  441 us (44%)
  Pallas kernels  253 us (25%)
  local copies, waits for them, and re-layouts  148 us (15%)
  starting transfers between devices  132 us (13%)
  between operations  16.7 us (2%)
    ppermute x54, waiting for transfers between devices, fsdp_swap(): return lax.ppermute(array, 'fsdp', [(i, i ^ by) for i in range(count)])  302 us
    pallas_call x63, Pallas kernels, ordered_call(): pl.pallas_call(marked, in_specs=list(in_specs) + [anywhere], out_specs=li...  253 us
    unnamed x491, local copies, waits for them, and re-layouts  144 us
    ppermute x65, waiting for transfers between devices, seq_swap(): return lax.ppermute(array, 'seq', [(i, i ^ by) for i in range(count)])  139 us
    ppermute x54, starting transfers between devices, fsdp_swap(): return lax.ppermute(array, 'fsdp', [(i, i ^ by) for i in range(count)])  67.5 us
    ppermute x65, starting transfers between devices, seq_swap(): return lax.ppermute(array, 'seq', [(i, i ^ by) for i in range(count)])  63.7 us
  transfers between devices with their start and end apart: 126, of which 62 were waited for; matrix products, arithmetic and copies ran while one was open for 1% of the time, Pallas kernels for 25%

profile of v3, /device:TPU:8, one launch (start us, length us, event | category | flops | bytes accessed | tf_op | source)
XLA Modules:
  0.0 994.3 jit_solution(5058316299463276392)
XLA Ops:
  43.7 10.8 %collective-permute-done.7.refs_3_ = bf16[1,48,3584]{2,1,0:T(8,128)(2,1)S(1)} collective-permute-done((bf16[1,48,3584]{2,1,0:T(8,128)(2,1)S(1)}, bf16[1,48,3584]{2,1,0:T(8,128)(2,1)S(1)}, u32[]{:S(2)}, u32[]{:S(2)}) %collective-permute-start.7) | collective-permute-done | bytes 344096 | tf_op jit(solution)/shard_map/ppermute | solution.py:48
  101.5 22.6 %collective-permute-done.28.refs_4_ = bf16[8,48,768]{2,1,0:T(8,128)(2,1)S(1)} collective-permute-done((bf16[8,48,768]{2,1,0:T(8,128)(2,1)S(1)}, bf16[8,48,768]{2,1,0:T(8,128)(2,1)S(1)}, u32[]{:S(2)}, u32[]{:S(2)}) %collective-permute-start.28) | collective-permute-done | bytes 589856 | tf_op jit(solution)/shard_map/ppermute | solution.py:48
  124.2 14.9 %collective-permute-done.29.refs_5_ = bf16[8,48,768]{2,1,0:T(8,128)(2,1)S(1)} collective-permute-done((bf16[8,48,768]{2,1,0:T(8,128)(2,1)S(1)}, bf16[8,48,768]{2,1,0:T(8,128)(2,1)S(1)}, u32[]{:S(2)}, u32[]{:S(2)}) %collective-permute-start.29) | collective-permute-done | bytes 589856 | tf_op jit(solution)/shard_map/ppermute | solution.py:48
  153.6 8.6 collective-permute-done.32.refs_2_
  162.2 23.7 %collective-permute-done.33.refs_3_ = bf16[1,48,3584]{2,1,0:T(8,128)(2,1)S(1)} collective-permute-done((bf16[1,48,3584]{2,1,0:T(8,128)(2,1)S(1)}, bf16[1,48,3584]{2,1,0:T(8,128)(2,1)S(1)}, u32[]{:S(2)}, u32[]{:S(2)}) %collective-permute-start.33) | collective-permute-done | bytes 344096 | tf_op jit(solution)/shard_map/ppermute | solution.py:48
  185.9 10.5 %collective-permute-done.34.refs_4_ = bf16[1,48,3584]{2,1,0:T(8,128)(2,1)S(1)} collective-permute-done((bf16[1,48,3584]{2,1,0:T(8,128)(2,1)S(1)}, bf16[1,48,3584]{2,1,0:T(8,128)(2,1)S(1)}, u32[]{:S(2)}, u32[]{:S(2)}) %collective-permute-start.34) | collective-permute-done | bytes 344096 | tf_op jit(solution)/shard_map/ppermute | solution.py:48
  227.3 12.4 %collective-permute-done.39.refs_1_ = bf16[128,1536]{1,0:T(8,128)(2,1)S(1)} collective-permute-done((bf16[128,1536]{1,0:T(8,128)(2,1)S(1)}, bf16[128,1536]{1,0:T(8,128)(2,1)S(1)}, u32[]{:S(2)}, u32[]{:S(2)}) %collective-permute-start.39) | collective-permute-done | bytes 393248 | tf_op jit(solution)/shard_map/ppermute | solution.py:48
  274.9 16.7 %collective-permute-done.42.refs_3_ = bf16[128,1536]{1,0:T(8,128)(2,1)S(1)} collective-permute-done((bf16[128,1536]{1,0:T(8,128)(2,1)S(1)}, bf16[128,1536]{1,0:T(8,128)(2,1)S(1)}, u32[]{:S(2)}, u32[]{:S(2)}) %collective-permute-start.42) | collective-permute-done | bytes 393248 | tf_op jit(solution)/shard_map/ppermute | solution.py:48
  303.5 16.8 %collective-permute-done.46.refs_1_ = bf16[128,1536]{1,0:T(8,128)(2,1)S(1)} collective-permute-done((bf16[128,1536]{1,0:T(8,128)(2,1)S(1)}, bf16[128,1536]{1,0:T(8,128)(2,1)S(1)}, u32[]{:S(2)}, u32[]{:S(2)}) %collective-permute-start.46) | collective-permute-done | bytes 393248 | tf_op jit(solution)/shard_map/ppermute | solution.py:39
  322.1 9.7 collective-permute-done.48.refs_3_
  333.7 20.9 %collective-permute-done.50.refs_5_ = bf16[8,48,768]{2,1,0:T(8,128)(2,1)S(1)} collective-permute-done((bf16[8,48,768]{2,1,0:T(8,128)(2,1)S(1)}, bf16[8,48,768]{2,1,0:T(8,128)(2,1)S(1)}, u32[]{:S(2)}, u32[]{:S(2)}) %collective-permute-start.50) | collective-permute-done | bytes 589856 | tf_op jit(solution)/shard_map/ppermute | solution.py:48
  401.1 26.7 %collective-permute-done.58.refs_3_ = bf16[128,1536]{1,0:T(8,128)(2,1)S(1)} collective-permute-done((bf16[128,1536]{1,0:T(8,128)(2,1)S(1)}, bf16[128,1536]{1,0:T(8,128)(2,1)S(1)}, u32[]{:S(2)}, u32[]{:S(2)}) %collective-permute-start.58) | collective-permute-done | bytes 393248 | tf_op jit(solution)/shard_map/ppermute | solution.py:48
  437.7 9.5 shard_map.332
  464.5 11.8 %shard_map.335 = (f32[128,1536]{1,0:T(8,128)S(1)}, bf16[128,1536]{1,0:T(8,128)(2,1)}, bf16[256,1792]{1,0:T(8,128)(2,1)S(1)}, bf16[256,1792]{1,0:T(8,128)(2,1)S(1)}, f32[8,128]{1,0:T(8,128)S(1)}) custom-call(bf16[128,1536]{1,0:T(8,128)(2,1)S(1)} %copy-done.152, bf16[128,1536]{1,0:T(8,128)(2,1)S(1)} %copy-done.154, f32[256,1792]{1,0:T(8,128)S(1)} %copy-done.97, ...), custom_call_target="tpu_custom_call" | custom-call | tf_op jit(solution)/shard_map/pallas_call | solution.py:131
  477.5 11.1 %shard_map.336 = (bf16[128,1536]{1,0:T(8,128)(2,1)}, bf16[128,1792]{1,0:T(8,128)(2,1)S(1)}, bf16[128,1792]{1,0:T(8,128)(2,1)S(1)}, f32[8,128]{1,0:T(8,128)S(1)}) custom-call(bf16[128,1536]{1,0:T(8,128)(2,1)S(1)} %copy-done.156, f32[128,1792]{1,0:T(8,128)S(1)} %get-tuple-element.383.refs_1_, f32[128,1792]{1,0:T(8,128)S(1)} %get-tuple-element.384.refs_2_, ...), custom_call_target="tpu_custom_call" | custom-call | tf_op jit(solution)/shard_map/pallas_call | solution.py:131
  491.4 11.1 %shard_map.337 = (bf16[128,1536]{1,0:T(8,128)(2,1)}, bf16[128,1792]{1,0:T(8,128)(2,1)S(1)}, bf16[128,1792]{1,0:T(8,128)(2,1)S(1)}, f32[8,128]{1,0:T(8,128)S(1)}) custom-call(bf16[128,1536]{1,0:T(8,128)(2,1)S(1)} %copy-done.158, f32[128,1792]{1,0:T(8,128)S(1)} %get-tuple-element.380.refs_1_, f32[128,1792]{1,0:T(8,128)S(1)} %get-tuple-element.381.refs_2_, ...), custom_call_target="tpu_custom_call" | custom-call | tf_op jit(solution)/shard_map/pallas_call | solution.py:131
  505.1 8.7 shard_map.339
  532.8 15.5 %shard_map.341 = (bf16[1536,3584]{1,0:T(8,128)(2,1)}, f32[8,128]{1,0:T(8,128)}) custom-call(bf16[128,1536]{1,0:T(8,128)(2,1)} %get-tuple-element.367.refs_0_, bf16[128,1536]{1,0:T(8,128)(2,1)} %collective-permute-done.55.refs_1_, bf16[128,1536]{1,0:T(8,128)(2,1)} %collective-permute-done.60.refs_0_.refs_2_, ...), custom_call_target="tpu_custom_call" | custom-call | flops 16911433728 | bytes 66060288 | tf_op jit(solution)/shard_map/pallas_call | solution.py:131
  597.8 14.5 %collective-permute-done.74.refs_6_ = bf16[128,1536]{1,0:T(8,128)(2,1)} collective-permute-done((bf16[128,1536]{1,0:T(8,128)(2,1)}, bf16[128,1536]{1,0:T(8,128)(2,1)}, u32[]{:S(2)}, u32[]{:S(2)}) %collective-permute-start.74) | collective-permute-done | bytes 393248 | tf_op jit(solution)/shard_map/ppermute | solution.py:39
  626.8 10.6 %collective-permute-done.75.refs_1_ = bf16[128,1536]{1,0:T(8,128)(2,1)S(1)} collective-permute-done((bf16[128,1536]{1,0:T(8,128)(2,1)S(1)}, bf16[128,1536]{1,0:T(8,128)(2,1)S(1)}, u32[]{:S(2)}, u32[]{:S(2)}) %collective-permute-start.75) | collective-permute-done | bytes 393248 | tf_op jit(solution)/shard_map/ppermute | solution.py:48
  641.8 11.6 %shard_map.347 = (f32[128,1536]{1,0:T(8,128)S(1)}, bf16[128,1536]{1,0:T(8,128)(2,1)}, bf16[256,1792]{1,0:T(8,128)(2,1)S(1)}, bf16[256,1792]{1,0:T(8,128)(2,1)S(1)}, f32[8,128]{1,0:T(8,128)S(1)}) custom-call(bf16[128,1536]{1,0:T(8,128)(2,1)S(1)} %get-tuple-element.434.refs_0_, bf16[128,1536]{1,0:T(8,128)(2,1)S(1)} %collective-permute-done.75.refs_1_, ...), custom_call_target="tpu_custom_call" | custom-call | tf_op jit(solution)/shard_map/pallas_call | solution.py:131
  655.9 11.0 %shard_map.348 = (bf16[128,1536]{1,0:T(8,128)(2,1)}, bf16[128,1792]{1,0:T(8,128)(2,1)S(1)}, bf16[128,1792]{1,0:T(8,128)(2,1)S(1)}, f32[8,128]{1,0:T(8,128)S(1)}) custom-call(bf16[128,1536]{1,0:T(8,128)(2,1)S(1)} %collective-permute-done.77.refs_0_.refs_2_, f32[128,1792]{1,0:T(8,128)S(1)} %copy-done.121, f32[128,1792]{1,0:T(8,128)S(1)} %copy-done.123, ...), custom_call_target="tpu_custom_call" | custom-call | tf_op jit(solution)/shard_map/pallas_call | solution.py:131
  668.9 11.0 %shard_map.349 = (bf16[128,1536]{1,0:T(8,128)(2,1)}, bf16[128,1792]{1,0:T(8,128)(2,1)S(1)}, bf16[128,1792]{1,0:T(8,128)(2,1)S(1)}, f32[8,128]{1,0:T(8,128)S(1)}) custom-call(bf16[128,1536]{1,0:T(8,128)(2,1)S(1)} %collective-permute-done.79.refs_0_.refs_3_, f32[128,1792]{1,0:T(8,128)S(1)} %copy-done.117, f32[128,1792]{1,0:T(8,128)S(1)} %copy-done.119, ...), custom_call_target="tpu_custom_call" | custom-call | tf_op jit(solution)/shard_map/pallas_call | solution.py:131
  682.7 8.9 shard_map.350
  714.5 15.7 %shard_map.352 = (bf16[1536,3584]{1,0:T(8,128)(2,1)}, f32[8,128]{1,0:T(8,128)}) custom-call(bf16[128,1536]{1,0:T(8,128)(2,1)} %copy-done.166, bf16[128,1536]{1,0:T(8,128)(2,1)} %copy-done.167, bf16[128,1536]{1,0:T(8,128)(2,1)} %copy-done.164, bf16[128,1536]{1,0:T(8,128)(2,1)} %copy-done.165, bf16[256,1792]{1,0:T(8,128)(2,1)} %copy-done.192, ...), custom_call_target="tpu_custom_call" | custom-call | flops 16911433728 | bytes 66060288 | tf_op jit(solution)/shard_map/pallas_call | solution.py:131
  771.0 9.7 collective-permute-done.87.refs_2_
  789.7 9.5 collective-permute-done.89.refs_4_
  804.8 8.5 shard_map.357
  814.7 9.3 collective-permute-done.94.refs_8_
  850.4 12.2 %collective-permute-done.95.refs_2_ = bf16[8,48,768]{2,1,0:T(8,128)(2,1)S(1)} collective-permute-done((bf16[8,48,768]{2,1,0:T(8,128)(2,1)}, bf16[8,48,768]{2,1,0:T(8,128)(2,1)S(1)}, u32[]{:S(2)}, u32[]{:S(2)}) %collective-permute-start.95) | collective-permute-done | bytes 589856 | tf_op jit(solution)/shard_map/ppermute | solution.py:48
  887.4 11.1 %collective-permute-done.97.refs_2_.refs_4_ = bf16[8,48,768]{2,1,0:T(8,128)(2,1)} collective-permute-done((bf16[8,48,768]{2,1,0:T(8,128)(2,1)}, bf16[8,48,768]{2,1,0:T(8,128)(2,1)}, u32[]{:S(2)}, u32[]{:S(2)}) %collective-permute-start.97) | collective-permute-done | bytes 589856 | tf_op jit(solution)/shard_map/ppermute | solution.py:48
  921.4 16.9 %collective-permute-done.100.refs_3_ = bf16[2,48,768]{2,1,0:T(8,128)(2,1)S(1)} collective-permute-done((bf16[2,48,768]{2,1,0:T(8,128)(2,1)S(1)}, bf16[2,48,768]{2,1,0:T(8,128)(2,1)S(1)}, u32[]{:S(2)}, u32[]{:S(2)}) %collective-permute-start.100) | collective-permute-done | bytes 147488 | tf_op jit(solution)/shard_map/ppermute | solution.py:39
  (834 shorter events, 554.9 us)
Async XLA Ops:
  7.2 233.3 %all-gather.7.cloned.1.call-start = ((), (), s32[]{:S(2)}) async-start(), calls=%async_computation.4 | async-start | bytes 6193152 | tf_op jit(solution)/shard_map/all_gather | solution.py:336
  11.0 229.5 %all-gather.5.cloned.1.call-start = ((), (), s32[]{:S(2)}) async-start(), calls=%async_computation.3 | async-start | bytes 12386304 | tf_op jit(solution)/shard_map/all_gather | solution.py:336
  39.5 48.3 %collective-permute-start.24 = (bf16[8,48,768]{2,1,0:T(8,128)(2,1)S(1)}, bf16[8,48,768]{2,1,0:T(8,128)(2,1)S(1)}, u32[]{:S(2)}, u32[]{:S(2)}) collective-permute-start(bf16[8,48,768]{2,1,0:T(8,128)(2,1)S(1)} %get-tuple-element.311.refs_2_), channel_id=1, source_target_pairs={{0,1},{1,0},{2,3},{3,2},{4,5},{5,4},{6,7},{7,6},{8,9},{9,8},{10,11... | collective-permute-start | bytes 1769480 | tf_op jit(solution)/shard_map/ppermute | solution.py:48
  85.2 39.0 %collective-permute-start.28 = (bf16[8,48,768]{2,1,0:T(8,128)(2,1)S(1)}, bf16[8,48,768]{2,1,0:T(8,128)(2,1)S(1)}, u32[]{:S(2)}, u32[]{:S(2)}) collective-permute-start(bf16[8,48,768]{2,1,0:T(8,128)(2,1)S(1)} %get-tuple-element.311.refs_2_), channel_id=1, source_target_pairs={{0,2},{1,3},{2,0},{3,1},{4,6},{5,7},{6,4},{7,5},{8,10},{9,11},{10,... | collective-permute-start | bytes 1769480 | tf_op jit(solution)/shard_map/ppermute | solution.py:48
  85.2 53.8 %collective-permute-start.29 = (bf16[8,48,768]{2,1,0:T(8,128)(2,1)S(1)}, bf16[8,48,768]{2,1,0:T(8,128)(2,1)S(1)}, u32[]{:S(2)}, u32[]{:S(2)}) collective-permute-start(bf16[8,48,768]{2,1,0:T(8,128)(2,1)S(1)} %get-tuple-element.311.refs_2_), channel_id=1, source_target_pairs={{0,3},{1,2},{2,1},{3,0},{4,7},{5,6},{6,5},{7,4},{8,11},{9,10},{10,... | collective-permute-start | bytes 1769480 | tf_op jit(solution)/shard_map/ppermute | solution.py:48
  90.7 48.3 %collective-permute-start.25 = (bf16[128,1536]{1,0:T(8,128)(2,1)S(1)}, bf16[128,1536]{1,0:T(8,128)(2,1)S(1)}, u32[]{:S(2)}, u32[]{:S(2)}) collective-permute-start(bf16[128,1536]{1,0:T(8,128)(2,1)S(1)} %get-tuple-element.317.refs_0_), channel_id=1, source_target_pairs={{0,8},{4,12},{8,0},{12,4},{16,24},{20,28},{24,16},{28,20},{1,9},{5... | collective-permute-start | bytes 1179656 | tf_op jit(solution)/shard_map/ppermute | solution.py:39
  93.1 45.9 %collective-permute-start.26 = (bf16[128,1536]{1,0:T(8,128)(2,1)S(1)}, bf16[128,1536]{1,0:T(8,128)(2,1)S(1)}, u32[]{:S(2)}, u32[]{:S(2)}) collective-permute-start(bf16[128,1536]{1,0:T(8,128)(2,1)S(1)} %get-tuple-element.317.refs_0_), channel_id=1, source_target_pairs={{0,16},{4,20},{8,24},{12,28},{16,0},{20,4},{24,8},{28,12},{1,17},{... | collective-permute-start | bytes 1179656 | tf_op jit(solution)/shard_map/ppermute | solution.py:39
  93.1 45.9 %collective-permute-start.27 = (bf16[128,1536]{1,0:T(8,128)(2,1)S(1)}, bf16[128,1536]{1,0:T(8,128)(2,1)S(1)}, u32[]{:S(2)}, u32[]{:S(2)}) collective-permute-start(bf16[128,1536]{1,0:T(8,128)(2,1)S(1)} %get-tuple-element.317.refs_0_), channel_id=1, source_target_pairs={{0,24},{4,28},{8,16},{12,20},{16,8},{20,12},{24,0},{28,4},{1,25},{... | collective-permute-start | bytes 1179656 | tf_op jit(solution)/shard_map/ppermute | solution.py:39
  139.9 291.1 %all-gather.11.cloned.1.call-start = ((), (), s32[]{:S(2)}) async-start(), calls=%async_computation.6 | async-start | bytes 6193152 | tf_op jit(solution)/shard_map/all_gather | solution.py:336
  148.4 47.9 %collective-permute-start.31 = (bf16[4,128,1536]{2,1,0:T(8,128)(2,1)S(1)}, bf16[4,128,1536]{2,1,0:T(8,128)(2,1)S(1)}, u32[]{:S(2)}, u32[]{:S(2)}) collective-permute-start(bf16[4,128,1536]{2,1,0:T(8,128)(2,1)S(1)} %get-tuple-element.327), channel_id=1, source_target_pairs={{0,4},{4,0},{8,12},{12,8},{16,20},{20,16},{24,28},{28,24},{1,5},{5... | collective-permute-start | bytes 4718600 | tf_op jit(solution)/shard_map/ppermute | solution.py:39
  150.2 46.2 %collective-permute-start.34 = (bf16[1,48,3584]{2,1,0:T(8,128)(2,1)S(1)}, bf16[1,48,3584]{2,1,0:T(8,128)(2,1)S(1)}, u32[]{:S(2)}, u32[]{:S(2)}) collective-permute-start(bf16[1,48,3584]{2,1,0:T(8,128)(2,1)S(1)} %get-tuple-element.571), channel_id=1, source_target_pairs={{0,3},{1,2},{2,1},{3,0},{4,7},{5,6},{6,5},{7,4},{8,11},{9,10},{10,... | collective-permute-start | bytes 1032200 | tf_op jit(solution)/shard_map/ppermute | solution.py:48
  152.7 52.2 %collective-permute-start.38 = (bf16[8,48,768]{2,1,0:T(8,128)(2,1)S(1)}, bf16[8,48,768]{2,1,0:T(8,128)(2,1)S(1)}, u32[]{:S(2)}, u32[]{:S(2)}) collective-permute-start(bf16[8,48,768]{2,1,0:T(8,128)(2,1)S(1)} %copy-done.40), channel_id=1, source_target_pairs={{0,2},{1,3},{2,0},{3,1},{4,6},{5,7},{6,4},{7,5},{8,10},{9,11},{10,... | collective-permute-start | bytes 1769480 | tf_op jit(solution)/shard_map/ppermute | solution.py:48
  220.8 210.2 %all-gather.9.cloned.1.call-start = ((), (), s32[]{:S(2)}) async-start(), calls=%async_computation.5 | async-start | bytes 12386304 | tf_op jit(solution)/shard_map/all_gather | solution.py:336
  222.0 508.2 %reduce-scatter.4.cloned.1.call-start = ((), (), s32[]{:S(2)}) async-start(), calls=%async_computation.7 | async-start | bytes 12386304 | tf_op jit(solution)/shard_map/reduce_scatter | solution.py:450
  225.3 40.8 %collective-permute-start.43 = (bf16[128,1536]{1,0:T(8,128)(2,1)S(1)}, bf16[128,1536]{1,0:T(8,128)(2,1)S(1)}, u32[]{:S(2)}, u32[]{:S(2)}) collective-permute-start(bf16[128,1536]{1,0:T(8,128)(2,1)S(1)} %get-tuple-element.337.refs_0_), channel_id=1, source_target_pairs={{0,3},{1,2},{2,1},{3,0},{4,7},{5,6},{6,5},{7,4},{8,11},{9,10},{10,... | collective-permute-start | bytes 1179656 | tf_op jit(solution)/shard_map/ppermute | solution.py:48
  225.9 47.3 %collective-permute-start.45 = (bf16[8,48,768]{2,1,0:T(8,128)(2,1)S(1)}, bf16[8,48,768]{2,1,0:T(8,128)(2,1)S(1)}, u32[]{:S(2)}, u32[]{:S(2)}) collective-permute-start(bf16[8,48,768]{2,1,0:T(8,128)(2,1)S(1)} %copy-done.42), channel_id=1, source_target_pairs={{0,1},{1,0},{2,3},{3,2},{4,5},{5,4},{6,7},{7,6},{8,9},{9,8},{10,11... | collective-permute-start | bytes 1769480 | tf_op jit(solution)/shard_map/ppermute | solution.py:48
  380.7 47.2 %collective-permute-start.58 = (bf16[128,1536]{1,0:T(8,128)(2,1)S(1)}, bf16[128,1536]{1,0:T(8,128)(2,1)S(1)}, u32[]{:S(2)}, u32[]{:S(2)}) collective-permute-start(bf16[128,1536]{1,0:T(8,128)(2,1)S(1)} %get-tuple-element.370.refs_0_), channel_id=1, source_target_pairs={{0,3},{1,2},{2,1},{3,0},{4,7},{5,6},{6,5},{7,4},{8,11},{9,10},{10,... | collective-permute-start | bytes 1179656 | tf_op jit(solution)/shard_map/ppermute | solution.py:48
  389.5 41.5 %collective-permute-start.55 = (bf16[128,1536]{1,0:T(8,128)(2,1)}, bf16[128,1536]{1,0:T(8,128)(2,1)}, u32[]{:S(2)}, u32[]{:S(2)}) collective-permute-start(bf16[128,1536]{1,0:T(8,128)(2,1)} %get-tuple-element.367.refs_0_), channel_id=1, source_target_pairs={{0,1},{1,0},{2,3},{3,2},{4,5},{5,4},{6,7},{7,6},{8,9},{9,8},{10,11... | collective-permute-start | bytes 1179656 | tf_op jit(solution)/shard_map/ppermute | solution.py:48
  389.5 57.8 %collective-permute-start.60 = (bf16[128,1536]{1,0:T(8,128)(2,1)}, bf16[128,1536]{1,0:T(8,128)(2,1)}, u32[]{:S(2)}, u32[]{:S(2)}) collective-permute-start(bf16[128,1536]{1,0:T(8,128)(2,1)} %get-tuple-element.367.refs_0_), channel_id=1, source_target_pairs={{0,2},{1,3},{2,0},{3,1},{4,6},{5,7},{6,4},{7,5},{8,10},{9,11},{10,... | collective-permute-start | bytes 1179656 | tf_op jit(solution)/shard_map/ppermute | solution.py:48
  392.4 63.7 %collective-permute-start.62 = (bf16[128,1536]{1,0:T(8,128)(2,1)}, bf16[128,1536]{1,0:T(8,128)(2,1)}, u32[]{:S(2)}, u32[]{:S(2)}) collective-permute-start(bf16[128,1536]{1,0:T(8,128)(2,1)} %get-tuple-element.367.refs_0_), channel_id=1, source_target_pairs={{0,3},{1,2},{2,1},{3,0},{4,7},{5,6},{6,5},{7,4},{8,11},{9,10},{10,... | collective-permute-start | bytes 1179656 | tf_op jit(solution)/shard_map/ppermute | solution.py:48
  447.2 55.3 %collective-permute-start.59 = (bf16[128,1536]{1,0:T(8,128)(2,1)}, bf16[128,1536]{1,0:T(8,128)(2,1)S(1)}, u32[]{:S(2)}, u32[]{:S(2)}) collective-permute-start(bf16[128,1536]{1,0:T(8,128)(2,1)} %get-tuple-element.374), channel_id=1, source_target_pairs={{0,1},{1,0},{2,3},{3,2},{4,5},{5,4},{6,7},{7,6},{8,9},{9,8},{10,11... | collective-permute-start | bytes 1179656 | tf_op jit(solution)/shard_map/ppermute | solution.py:48
  453.9 49.6 %collective-permute-start.61 = (bf16[128,1536]{1,0:T(8,128)(2,1)S(1)}, bf16[128,1536]{1,0:T(8,128)(2,1)S(1)}, u32[]{:S(2)}, u32[]{:S(2)}) collective-permute-start(bf16[128,1536]{1,0:T(8,128)(2,1)S(1)} %get-tuple-element.376), channel_id=1, source_target_pairs={{0,2},{1,3},{2,0},{3,1},{4,6},{5,7},{6,4},{7,5},{8,10},{9,11},{10,... | collective-permute-start | bytes 1179656 | tf_op jit(solution)/shard_map/ppermute | solution.py:48
  463.5 40.1 %collective-permute-start.63 = (bf16[128,1536]{1,0:T(8,128)(2,1)S(1)}, bf16[128,1536]{1,0:T(8,128)(2,1)S(1)}, u32[]{:S(2)}, u32[]{:S(2)}) collective-permute-start(bf16[128,1536]{1,0:T(8,128)(2,1)S(1)} %get-tuple-element.378), channel_id=1, source_target_pairs={{0,3},{1,2},{2,1},{3,0},{4,7},{5,6},{6,5},{7,4},{8,11},{9,10},{10,... | collective-permute-start | bytes 1179656 | tf_op jit(solution)/shard_map/ppermute | solution.py:48
  559.0 321.2 %reduce-scatter.6.cloned.1.call-start = ((), (), s32[]{:S(2)}) async-start(), calls=%async_computation.8 | async-start | bytes 6193152 | tf_op jit(solution)/shard_map/reduce_scatter | solution.py:450
  559.6 380.7 %reduce-scatter.8.cloned.1.call-start = ((), (), s32[]{:S(2)}) async-start(), calls=%async_computation.9 | async-start | bytes 12386304 | tf_op jit(solution)/shard_map/reduce_scatter | solution.py:450
  626.4 42.5 %collective-permute-start.79 = (bf16[128,1536]{1,0:T(8,128)(2,1)S(1)}, bf16[128,1536]{1,0:T(8,128)(2,1)S(1)}, u32[]{:S(2)}, u32[]{:S(2)}) collective-permute-start(bf16[128,1536]{1,0:T(8,128)(2,1)S(1)} %get-tuple-element.434.refs_0_), channel_id=1, source_target_pairs={{0,3},{1,2},{2,1},{3,0},{4,7},{5,6},{6,5},{7,4},{8,11},{9,10},{10,... | collective-permute-start | bytes 1179656 | tf_op jit(solution)/shard_map/ppermute | solution.py:48
  653.4 38.2 %collective-permute-start.76 = (bf16[128,1536]{1,0:T(8,128)(2,1)}, bf16[128,1536]{1,0:T(8,128)(2,1)}, u32[]{:S(2)}, u32[]{:S(2)}) collective-permute-start(bf16[128,1536]{1,0:T(8,128)(2,1)} %get-tuple-element.439), channel_id=1, source_target_pairs={{0,1},{1,0},{2,3},{3,2},{4,5},{5,4},{6,7},{7,6},{8,9},{9,8},{10,11... | collective-permute-start | bytes 1179656 | tf_op jit(solution)/shard_map/ppermute | solution.py:48
  768.2 46.5 %collective-permute-start.93 = (bf16[8,48,768]{2,1,0:T(8,128)(2,1)}, bf16[8,48,768]{2,1,0:T(8,128)(2,1)S(1)}, u32[]{:S(2)}, u32[]{:S(2)}) collective-permute-start(bf16[8,48,768]{2,1,0:T(8,128)(2,1)} %get-tuple-element.485), channel_id=1, source_target_pairs={{0,1},{1,0},{2,3},{3,2},{4,5},{5,4},{6,7},{7,6},{8,9},{9,8},{10,11... | collective-permute-start | bytes 1769480 | tf_op jit(solution)/shard_map/ppermute | solution.py:48
  780.7 43.3 %collective-permute-start.94 = (bf16[8,48,768]{2,1,0:T(8,128)(2,1)}, bf16[8,48,768]{2,1,0:T(8,128)(2,1)S(1)}, u32[]{:S(2)}, u32[]{:S(2)}) collective-permute-start(bf16[8,48,768]{2,1,0:T(8,128)(2,1)} %get-tuple-element.486), channel_id=1, source_target_pairs={{0,3},{1,2},{2,1},{3,0},{4,7},{5,6},{6,5},{7,4},{8,11},{9,10},{10,... | collective-permute-start | bytes 1769480 | tf_op jit(solution)/shard_map/ppermute | solution.py:48
  902.0 45.7 %collective-permute-start.106 = (bf16[224,1536]{1,0:T(8,128)(2,1)}, bf16[224,1536]{1,0:T(8,128)(2,1)}, u32[]{:S(2)}, u32[]{:S(2)}) collective-permute-start(bf16[224,1536]{1,0:T(8,128)(2,1)} %get-tuple-element.514), channel_id=1, source_target_pairs={{0,8},{4,12},{8,0},{12,4},{16,24},{20,28},{24,16},{28,20},{1,9},{5... | collective-permute-start | bytes 2064392 | tf_op jit(solution)/shard_map/ppermute | solution.py:39
  905.3 45.8 %collective-permute-start.107 = (bf16[224,1536]{1,0:T(8,128)(2,1)}, bf16[224,1536]{1,0:T(8,128)(2,1)S(1)}, u32[]{:S(2)}, u32[]{:S(2)}) collective-permute-start(bf16[224,1536]{1,0:T(8,128)(2,1)} %get-tuple-element.515), channel_id=1, source_target_pairs={{0,16},{4,20},{8,24},{12,28},{16,0},{20,4},{24,8},{28,12},{1,17},{... | collective-permute-start | bytes 2064392 | tf_op jit(solution)/shard_map/ppermute | solution.py:39
  905.6 45.5 %collective-permute-start.108 = (bf16[224,1536]{1,0:T(8,128)(2,1)}, bf16[224,1536]{1,0:T(8,128)(2,1)}, u32[]{:S(2)}, u32[]{:S(2)}) collective-permute-start(bf16[224,1536]{1,0:T(8,128)(2,1)} %get-tuple-element.516), channel_id=1, source_target_pairs={{0,24},{4,28},{8,16},{12,20},{16,8},{20,12},{24,0},{28,4},{1,25},{... | collective-permute-start | bytes 2064392 | tf_op jit(solution)/shard_map/ppermute | solution.py:39
  (334 other events, 3900.6 us)
Sparse Core Ops, SparseCore 0:
  11.1 46.5 all-gather.6
  139.3 67.2 all-gather.4
  220.9 44.5 all-gather.10
  267.8 80.6 all-gather.8
  559.1 96.2 reduce-scatter.3
  658.8 60.3 reduce-scatter.5
  748.8 101.3 reduce-scatter.7

commit v4 on v3

--- a/solution.py
+++ b/solution.py
@@ -101,7 +101,7 @@
 
 
 mark_shape = jax.ShapeDtypeStruct((8, 128), jnp.float32)
-anywhere = pl.BlockSpec(memory_space=pl.ANY)
+anywhere = pl.BlockSpec(memory_space=pltpu.HBM)
 
 
 def bytes_of(shape, kind):
@@ -228,24 +228,26 @@
 
 
 def assemble_mix(pieces, wide):
-    rings = len(pieces)
-    seqs, rows, width = pieces[0].shape
+    rings = lax.axis_size("fsdp")
+    rotated = len(pieces) == rings
+    seqs, rows, width = pieces[0].shape[-3:]
     chunk = width // 4
     features = seqs * chunk
 
     def body(place_seq, place_fsdp, *refs):
-        inner_out, outer_out = refs[rings:]
+        inner_out, outer_out = refs[-2:]
         for j in range(rings):
-            f = lax.bitwise_xor(place_fsdp[0], jnp.int32(j))
+            f = lax.bitwise_xor(place_fsdp[0], jnp.int32(j)) if rotated else j
+            part = refs[j] if rotated else refs[0].at[j]
             for s in range(seqs):
                 owner = lax.bitwise_xor(place_seq[0], jnp.int32(s))
                 for g in range(3):
-                    piece = refs[j][s, :, g * chunk : (g + 1) * chunk]
+                    piece = part[s, :, g * chunk : (g + 1) * chunk]
                     if wide > chunk:
                         gap = jnp.zeros((rows, wide - chunk), low)
                         piece = jnp.concatenate([piece, gap], axis=1)
                     inner_out[owner, f, :, g * wide : (g + 1) * wide] = piece
-                outer_out[f, :, s * chunk : (s + 1) * chunk] = refs[j][s, :, 3 * chunk :]
+                outer_out[f, :, s * chunk : (s + 1) * chunk] = part[s, :, 3 * chunk :]
 
     inner_shape = (seqs, rings, rows, 3 * wide)
     outer_shape = (rings, rows, features)
@@ -398,13 +400,14 @@
 
 def mix_reduce(layers):
     seqs, rows, width = layers[0][0].shape
-    count, rings = len(layers), len(layers[0])
+    count = len(layers)
     chunk = width // 4
+    starts = [sum(len(pieces) for pieces in layers[:i]) for i in range(count + 1)]
 
     def body(place, *refs):
-        inner_out, outer_out = refs[count * rings :]
+        inner_out, outer_out = refs[starts[-1] :]
         for layer in range(count):
-            parts = refs[layer * rings : (layer + 1) * rings]
+            parts = refs[starts[layer] : starts[layer + 1]]
             for s in range(seqs):
                 total = parts[0][s].astype(jnp.float32)
                 for part in parts[1:]:
@@ -789,7 +792,7 @@
     )(place_of("seq"), *blocks, projected, inner, outer, taps)
 
 
-def mixer_grads(normed, flows, mixed, lows, rows):
+def mixer_grads(normed, flows, mixed, lows, rows, rotated):
     seqs, rings = lax.axis_size("seq"), lax.axis_size("fsdp")
     features, width = normed[0].shape[-1], flows.shape[-1]
     half = normed[0].shape[0]
@@ -797,7 +800,8 @@
     chunk = mixed.shape[-1]
 
     def body(place, normed_even, normed_odd, flows, mixed, low_even, low_odd, *refs):
-        outs, inner, outer = refs[:rings], refs[rings], refs[rings + 1]
+        inner, outer = refs[-2:]
+        outs = refs[:rings] if rotated else [refs[0].at[j] for j in range(rings)]
         long = lambda array: array.reshape(-1, array.shape[-1])
         for g in range(3):
             at = slice(g * wide, (g + 1) * wide)
@@ -812,16 +816,17 @@
         for f in range(rings):
             outer[f] = part[f * rows : (f + 1) * rows]
         for j in range(rings):
-            f = lax.bitwise_xor(place[0], jnp.int32(j))
+            f = lax.bitwise_xor(place[0], jnp.int32(j)) if rotated else j
             for s in range(seqs):
                 for g in range(3):
                     piece = inner[s, f, :, g * wide : g * wide + chunk]
                     outs[j][s, :, g * chunk : (g + 1) * chunk] = piece
                 outs[j][s, :, 3 * chunk :] = outer[f, :, s * chunk : (s + 1) * chunk]
 
+    shape = (seqs, rows, 4 * chunk)
     return plain_call(
         body,
-        [shaped((seqs, rows, 4 * chunk), low)] * rings,
+        [shaped(shape, low)] * rings if rotated else [shaped((rings,) + shape, low)],
         scalars=1,
         scratch=[
             pltpu.VMEM((seqs, rings, rows, width), low),
@@ -1094,20 +1099,21 @@
     down_rows = gather_rows(pack_down(down_weight, 0))
     both, vector_blocks = vectors_middle(vector_blocks)
     mix_pieces = gather_fsdp(join_mix(mix_swap, mix_packed))
-    feed_part = assemble_feed(feed_swap)
+    feeds[0] = (gather_rows(assemble_feed(feed_swap)), down_rows)
     later_packed = pack_mix(mix_weight, 1)
     later_swap = swap_mix(later_packed)
     vector_blocks = stack_pairs(vector_blocks)
     later_piece = join_mix(later_swap, later_packed, mix_pieces[1:2])
+    later_mix = lax.all_gather(
+        later_piece.reshape(-1, later_piece.shape[-1]), "fsdp", axis=0, tiled=True
+    ).reshape((rings,) + later_piece.shape)
     gain_rows, tap_rows = vectors_end(both, vector_blocks)
     stream, normed = first_norm(inputs.reshape(-1, features), gain_rows[0, 0], ())
     blocks = send_seq(normed)
     later_feed = pack_feed(feed_weight, 1)
-    *blocks, feed_part = stack_pairs(blocks, mix_pieces[2:], [feed_part])
-    feeds[0] = (gather_rows(feed_part), down_rows)
+    *blocks, down_packed = stack_pairs(blocks, mix_pieces[2:], [pack_down(down_weight, 1)])
+    later_down = gather_rows(down_packed)
     mixes[0] = assemble_mix(mix_pieces, wide)
-    later_mix = [None, None, fsdp_swap(later_piece, 2)] if rings > 2 else [None, None]
-    later_feed = swap_feed(later_feed)
 
     kept = []
     for layer in range(LAYERS):
@@ -1116,24 +1122,17 @@
         projected, even, odd = mixer_forward(blocks, *mixes[layer], tap_rows[layer])
         odd = seq_swap(odd, 1)
         if last:
-            sums, flow_low = pair_sum(even, odd, (), [cotangent])
-            flow_low = gather_fsdp(flow_low)
-            middle, normed_two = finish(stream, sums, gain_rows[layer, 1])
-            flow_low = join_blocks(flow_low)
+            flow_low = join_blocks(gather_fsdp(flow_low))
+            (sums,) = pair_sum(even, odd)
         else:
-            (sums,) = pair_sum(even, odd, later_feed[1:])
-            middle, normed_two, later_piece, down_packed = finish(
-                stream,
-                sums,
-                gain_rows[layer, 1],
-                later_mix[2:],
-                (later_piece, pack_down(down_weight, 1)),
-            )
+            sums, later_feed = pair_sum(even, odd, (), [later_feed])
+            later_feed = swap_feed(later_feed)
+        middle, normed_two = finish(
+            stream, sums, gain_rows[layer, 1], feeds[layer] if last else ()
+        )
         two_blocks = gather_fsdp(normed_two)
         if not last:
-            later_mix[0] = later_piece
-            later_mix[1] = fsdp_swap(later_piece, 1)
-            feeds[1] = (gather_rows(assemble_feed(later_feed)), gather_rows(down_packed))
+            feeds[1] = (gather_rows(assemble_feed(later_feed)), later_down)
         sums, values = [], []
         for number, group in enumerate(groups_of(two_blocks)):
             outs, saved = feed_forward(group, *feeds[layer], number == 0)
@@ -1142,13 +1141,11 @@
         kept.append((stream, middle, gathered, projected, two_blocks, values))
         sums = return_sums(sums)
         if not last:
-            stream, normed, later_piece = finish(
-                middle, sums, gain_rows[layer + 1, 0], later_mix[1:2], [later_piece]
+            stream, normed, flow_low = finish(
+                middle, sums, gain_rows[layer + 1, 0], (), [cotangent]
             )
-            blocks = send_seq(normed)
-            later_mix += [fsdp_swap(later_piece, by) for by in range(3, rings)]
-            blocks = stack_pairs(blocks)
-            mixes[1] = assemble_mix(later_mix, wide)
+            blocks = stack_pairs(send_seq(normed))
+            mixes[1] = assemble_mix([later_mix], wide)
 
     states = (
         (mix_weight, mix_first, mix_second),
@@ -1158,11 +1155,13 @@
     new = [None] * 3
     gain_grads, tap_grads = [None] * LAYERS, [None] * LAYERS
     flow = cotangent
-    later_mix = ()
     for layer in reversed(range(LAYERS)):
         last = layer + 1 == LAYERS
         stream, middle, gathered, projected, two_blocks, values = kept[layer]
         back_sums, gate_flows, up_flows = [], [], []
+        if not last:
+            even, odd = split_down(later_down, ())
+            odd = seq_swap(odd, 1)
         for number, group in enumerate(groups_of(flow_low)):
             gates, ups, _ = values[number]
             outs, (gate_flow, up_flow) = feed_backward(
@@ -1171,44 +1170,47 @@
             back_sums += outs
             gate_flows.append(gate_flow)
             up_flows.append(up_flow)
+            if number == 0 and not last:
+                (later_down,) = pair_sum(even, odd)
         if last:
             outputs = finish(middle, sums, None).reshape(inputs.shape)
         back_sums = return_sums(back_sums)
         down_part = down_grads([value[2] for value in values], flow_low)
-        middle_flow, middle_low, gain_two, down_part, *later_mix = finish_back(
-            flow, back_sums, middle, gain_rows[layer, 1], [down_part, *later_mix]
+        middle_flow, middle_low, gain_two = finish_back(
+            flow, back_sums, middle, gain_rows[layer, 1]
         )
-        later_mix = return_sums(later_mix) if later_mix else later_mix
-        if last:
-            down_part = [scatter_rows(down_part)]
         blocks = send_seq(middle_low)
         feed_part = feed_grads(two_blocks, gate_flows, up_flows)
         if not last:
             later_feed = split_feed(later_feed, rows)
-        even, odd, feed_part = stack_pairs(
-            blocks, () if last else later_mix[2:3], [feed_part]
-        )
+        even, odd, feed_part = stack_pairs(blocks, (), [feed_part])
         feed_part = scatter_rows(feed_part)
         blocks = even, odd
         even, odd, flows, mixed, tap_grads[layer] = mixer_backward(
             blocks, projected, *mixes[layer], tap_rows[layer]
         )
-        (sums,) = pair_sum(even, seq_swap(odd, 1), () if last else later_feed[1:])
-        mix_part = mixer_grads(gathered, flows, mixed, blocks, rows)
+        (sums,) = pair_sum(even, seq_swap(odd, 1))
+        mix_part = mixer_grads(gathered, flows, mixed, blocks, rows, not last)
         flow, low_flow, gain_one, *mix_part = finish_back(
             middle_flow,
             sums,
             stream,
             gain_rows[layer, 0],
             mix_part,
-            () if last else (later_mix[1], *later_mix[3:]),
+            () if last else later_feed[1:],
         )
         if not last:
             mix_part = return_sums(mix_part)
         gain_grads[layer] = jnp.concatenate([gain_one, gain_two])
         if last:
             flow_low = gather_fsdp(low_flow)
-            later_mix, later_feed, later_down = mix_part, feed_part, down_part
+            later_mix = lax.psum_scatter(
+                mix_part[0].reshape(-1, mix_part[0].shape[-1]),
+                "fsdp",
+                scatter_dimension=0,
+                tiled=True,
+            ).reshape(mix_part[0].shape[1:])
+            later_feed, later_down = feed_part, down_part
     new[1] = feed_adam(later_feed, states[1], 1, new[1])
     even, odd = split_down(down_part, mix_part[1:3])
     odd = seq_swap(odd, 1)
@@ -1217,7 +1219,7 @@
     gain_grad, tap_grad = vector_gradients(
         jnp.stack(gain_grads), jnp.stack(tap_grads), gain_weight.shape[-1]
     )
-    mix_part = mix_reduce([mix_part, later_mix])
+    mix_part = mix_reduce([mix_part, [later_mix]])
     feed_part = split_feed(feed_part, rows)
     new[2] = down_adam(down_part, states[2], 0, new[2])
     new[0] = mix_adam(mix_part, states[0])

time: 1010 us -> 1050 us (1.040)
  waiting for transfers between devices: 441 us -> 482 us
    ppermute x65 -> x69, waiting for transfers between devices: 139 us -> 171 us  [seq_swap(): return lax.ppermute(array, 'seq', [(i, i ^ by) for i in range(count)])]
    ppermute x54 -> x48, starting transfers between devices: 67.5 us -> 54.4 us  [fsdp_swap(): return lax.ppermute(array, 'fsdp', [(i, i ^ by) for i in range(count)])]
    ppermute x54 -> x48, waiting for transfers between devices: 302 us -> 312 us  [fsdp_swap(): return lax.ppermute(array, 'fsdp', [(i, i ^ by) for i in range(count)])]
    unnamed x491 -> x446, local copies, waits for them, and re-layouts: 144 us -> 148 us
    ppermute x65 -> x69, starting transfers between devices: 63.7 us -> 68.4 us  [seq_swap(): return lax.ppermute(array, 'seq', [(i, i ^ by) for i in range(count)])]
    pallas_call x63 -> x65, Pallas kernels: 253 us -> 256 us  [ordered_call(): pl.pallas_call(marked, in_specs=list(in_specs) + [anywhere], out_specs=li...]
  transfers between devices with their start and end apart: 126 -> 125, of which waited for: 62 -> 63; matrix products, arithmetic and copies ran while one was open for 1% -> 1% of each run, Pallas kernels for 25% -> 24%
where the time goes in v4:
time: 1050 us; the launch traced here: 1040 us
  waiting for transfers between devices  482 us (46%)
  Pallas kernels  256 us (24%)
  local copies, waits for them, and re-layouts  155 us (15%)
  starting transfers between devices  124 us (12%)
  between operations  16.5 us (2%)
    ppermute x48, waiting for transfers between devices, fsdp_swap(): return lax.ppermute(array, 'fsdp', [(i, i ^ by) for i in range(count)])  312 us
    pallas_call x65, Pallas kernels, ordered_call(): pl.pallas_call(marked, in_specs=list(in_specs) + [anywhere], out_specs=li...  256 us
    ppermute x69, waiting for transfers between devices, seq_swap(): return lax.ppermute(array, 'seq', [(i, i ^ by) for i in range(count)])  171 us
    unnamed x446, local copies, waits for them, and re-layouts  148 us
    ppermute x69, starting transfers between devices, seq_swap(): return lax.ppermute(array, 'seq', [(i, i ^ by) for i in range(count)])  68.4 us
    ppermute x48, starting transfers between devices, fsdp_swap(): return lax.ppermute(array, 'fsdp', [(i, i ^ by) for i in range(count)])  54.4 us
  transfers between devices with their start and end apart: 125, of which 63 were waited for; matrix products, arithmetic and copies ran while one was open for 1% of the time, Pallas kernels for 24%

profile of v4, /device:TPU:8, one launch (start us, length us, event | category | flops | bytes accessed | tf_op | source)
XLA Modules:
  0.0 1036.5 jit_solution(6201668484085927664)
XLA Ops:
  102.6 24.2 %collective-permute-done.28.refs_4_ = bf16[8,48,768]{2,1,0:T(8,128)(2,1)S(1)} collective-permute-done((bf16[8,48,768]{2,1,0:T(8,128)(2,1)S(1)}, bf16[8,48,768]{2,1,0:T(8,128)(2,1)S(1)}, u32[]{:S(2)}, u32[]{:S(2)}) %collective-permute-start.28) | collective-permute-done | bytes 589856 | tf_op jit(solution)/shard_map/ppermute | solution.py:48
  126.8 13.9 %collective-permute-done.29.refs_5_ = bf16[8,48,768]{2,1,0:T(8,128)(2,1)S(1)} collective-permute-done((bf16[8,48,768]{2,1,0:T(8,128)(2,1)S(1)}, bf16[8,48,768]{2,1,0:T(8,128)(2,1)S(1)}, u32[]{:S(2)}, u32[]{:S(2)}) %collective-permute-start.29) | collective-permute-done | bytes 589856 | tf_op jit(solution)/shard_map/ppermute | solution.py:48
  176.2 12.3 %collective-permute-done.36.refs_2_ = bf16[1,48,3584]{2,1,0:T(8,128)(2,1)S(1)} collective-permute-done((bf16[1,48,3584]{2,1,0:T(8,128)(2,1)S(1)}, bf16[1,48,3584]{2,1,0:T(8,128)(2,1)S(1)}, u32[]{:S(2)}, u32[]{:S(2)}) %collective-permute-start.36) | collective-permute-done | bytes 344096 | tf_op jit(solution)/shard_map/ppermute | solution.py:48
  192.5 30.4 %collective-permute-done.38.refs_4_ = bf16[1,48,3584]{2,1,0:T(8,128)(2,1)S(1)} collective-permute-done((bf16[1,48,3584]{2,1,0:T(8,128)(2,1)S(1)}, bf16[1,48,3584]{2,1,0:T(8,128)(2,1)S(1)}, u32[]{:S(2)}, u32[]{:S(2)}) %collective-permute-start.38) | collective-permute-done | bytes 344096 | tf_op jit(solution)/shard_map/ppermute | solution.py:48
  227.9 11.1 %collective-permute-done.35.refs_1_ = bf16[128,1536]{1,0:T(8,128)(2,1)S(1)} collective-permute-done((bf16[128,1536]{1,0:T(8,128)(2,1)S(1)}, bf16[128,1536]{1,0:T(8,128)(2,1)S(1)}, u32[]{:S(2)}, u32[]{:S(2)}) %collective-permute-start.35) | collective-permute-done | bytes 393248 | tf_op jit(solution)/shard_map/ppermute | solution.py:48
  272.1 18.4 %collective-permute-done.41.refs_3_ = bf16[128,1536]{1,0:T(8,128)(2,1)S(1)} collective-permute-done((bf16[128,1536]{1,0:T(8,128)(2,1)S(1)}, bf16[128,1536]{1,0:T(8,128)(2,1)S(1)}, u32[]{:S(2)}, u32[]{:S(2)}) %collective-permute-start.41) | collective-permute-done | bytes 393248 | tf_op jit(solution)/shard_map/ppermute | solution.py:48
  290.4 8.9 collective-permute-done.43.refs_4_
  303.3 11.5 %collective-permute-done.44.refs_1_ = bf16[128,1536]{1,0:T(8,128)(2,1)S(1)} collective-permute-done((bf16[128,1536]{1,0:T(8,128)(2,1)S(1)}, bf16[128,1536]{1,0:T(8,128)(2,1)S(1)}, u32[]{:S(2)}, u32[]{:S(2)}) %collective-permute-start.44) | collective-permute-done | bytes 393248 | tf_op jit(solution)/shard_map/ppermute | solution.py:39
  319.7 10.2 collective-permute-done.46.refs_3_
  345.1 12.2 %collective-permute-done.49.refs_1_ = bf16[128,1536]{1,0:T(8,128)(2,1)S(1)} collective-permute-done((bf16[128,1536]{1,0:T(8,128)(2,1)S(1)}, bf16[128,1536]{1,0:T(8,128)(2,1)S(1)}, u32[]{:S(2)}, u32[]{:S(2)}) %collective-permute-start.49) | collective-permute-done | bytes 393248 | tf_op jit(solution)/shard_map/ppermute | solution.py:48
  357.3 12.2 %collective-permute-done.50.refs_2_ = bf16[128,1536]{1,0:T(8,128)(2,1)S(1)} collective-permute-done((bf16[128,1536]{1,0:T(8,128)(2,1)S(1)}, bf16[128,1536]{1,0:T(8,128)(2,1)S(1)}, u32[]{:S(2)}, u32[]{:S(2)}) %collective-permute-start.50) | collective-permute-done | bytes 393248 | tf_op jit(solution)/shard_map/ppermute | solution.py:48
  369.5 9.8 collective-permute-done.51.refs_3_
  419.7 9.0 collective-permute-done.55.refs_1_
  454.0 16.9 %collective-permute-done.59.refs_0_.refs_3_ = bf16[128,1536]{1,0:T(8,128)(2,1)S(1)} collective-permute-done((bf16[128,1536]{1,0:T(8,128)(2,1)S(1)}, bf16[128,1536]{1,0:T(8,128)(2,1)S(1)}, u32[]{:S(2)}, u32[]{:S(2)}) %collective-permute-start.59) | collective-permute-done | bytes 393248 | tf_op jit(solution)/shard_map/ppermute | solution.py:48
  478.3 11.7 %shard_map.335 = (f32[128,1536]{1,0:T(8,128)S(1)}, bf16[128,1536]{1,0:T(8,128)(2,1)}, bf16[256,1792]{1,0:T(8,128)(2,1)S(1)}, bf16[256,1792]{1,0:T(8,128)(2,1)S(1)}, f32[8,128]{1,0:T(8,128)S(1)}) custom-call(bf16[128,1536]{1,0:T(8,128)(2,1)S(1)} %copy-done.118, bf16[128,1536]{1,0:T(8,128)(2,1)S(1)} %copy-done.120, ...), custom_call_target="tpu_custom_call" | custom-call | tf_op jit(solution)/shard_map/pallas_call | solution.py:131
  490.1 11.0 %shard_map.336 = (bf16[128,1536]{1,0:T(8,128)(2,1)}, bf16[128,1792]{1,0:T(8,128)(2,1)S(1)}, bf16[128,1792]{1,0:T(8,128)(2,1)S(1)}, f32[8,128]{1,0:T(8,128)S(1)}) custom-call(bf16[128,1536]{1,0:T(8,128)(2,1)S(1)} %copy-done.122, f32[128,1792]{1,0:T(8,128)S(1)} %get-tuple-element.375.refs_1_, f32[128,1792]{1,0:T(8,128)S(1)} %get-tuple-element.376.refs_2_, ...), custom_call_target="tpu_custom_call" | custom-call | tf_op jit(solution)/shard_map/pallas_call | solution.py:131
  503.4 10.2 shard_map.337
  532.6 15.5 %shard_map.341 = (bf16[1536,3584]{1,0:T(8,128)(2,1)}, f32[8,128]{1,0:T(8,128)}) custom-call(bf16[128,1536]{1,0:T(8,128)(2,1)} %copy-done.135, bf16[128,1536]{1,0:T(8,128)(2,1)} %copy-done.136, bf16[128,1536]{1,0:T(8,128)(2,1)} %copy-done.131, bf16[128,1536]{1,0:T(8,128)(2,1)} %copy-done.132, bf16[256,1792]{1,0:T(8,128)(2,1)} %copy-done.174, ...), custom_call_target="tpu_custom_call" | custom-call | flops 16911433728 | bytes 66060288 | tf_op jit(solution)/shard_map/pallas_call | solution.py:131
  596.2 11.6 %collective-permute-done.71.refs_6_ = bf16[128,1536]{1,0:T(8,128)(2,1)S(1)} collective-permute-done((bf16[128,1536]{1,0:T(8,128)(2,1)S(1)}, bf16[128,1536]{1,0:T(8,128)(2,1)S(1)}, u32[]{:S(2)}, u32[]{:S(2)}) %collective-permute-start.71) | collective-permute-done | bytes 393248 | tf_op jit(solution)/shard_map/ppermute | solution.py:39
  624.0 10.6 %collective-permute-done.72.refs_1_ = bf16[128,1536]{1,0:T(8,128)(2,1)S(1)} collective-permute-done((bf16[128,1536]{1,0:T(8,128)(2,1)}, bf16[128,1536]{1,0:T(8,128)(2,1)S(1)}, u32[]{:S(2)}, u32[]{:S(2)}) %collective-permute-start.72) | collective-permute-done | bytes 393248 | tf_op jit(solution)/shard_map/ppermute | solution.py:48
  644.6 12.3 %shard_map.348 = (f32[128,1536]{1,0:T(8,128)S(1)}, bf16[128,1536]{1,0:T(8,128)(2,1)}, bf16[256,1792]{1,0:T(8,128)(2,1)S(1)}, bf16[256,1792]{1,0:T(8,128)(2,1)S(1)}, f32[8,128]{1,0:T(8,128)S(1)}) custom-call(bf16[128,1536]{1,0:T(8,128)(2,1)} %get-tuple-element.422.refs_0_, bf16[128,1536]{1,0:T(8,128)(2,1)S(1)} %collective-permute-done.72.refs_1_, ...), custom_call_target="tpu_custom_call" | custom-call | tf_op jit(solution)/shard_map/pallas_call | solution.py:131
  668.5 11.0 %shard_map.350 = (bf16[128,1536]{1,0:T(8,128)(2,1)}, bf16[128,1792]{1,0:T(8,128)(2,1)S(1)}, bf16[128,1792]{1,0:T(8,128)(2,1)S(1)}, f32[8,128]{1,0:T(8,128)S(1)}) custom-call(bf16[128,1536]{1,0:T(8,128)(2,1)S(1)} %collective-permute-done.74.refs_0_.refs_2_, f32[128,1792]{1,0:T(8,128)S(1)} %copy-done.93, f32[128,1792]{1,0:T(8,128)S(1)} %copy-done.95, ...), custom_call_target="tpu_custom_call" | custom-call | tf_op jit(solution)/shard_map/pallas_call | solution.py:131
  681.4 11.1 %shard_map.351 = (bf16[128,1536]{1,0:T(8,128)(2,1)}, bf16[128,1792]{1,0:T(8,128)(2,1)S(1)}, bf16[128,1792]{1,0:T(8,128)(2,1)S(1)}, f32[8,128]{1,0:T(8,128)S(1)}) custom-call(bf16[128,1536]{1,0:T(8,128)(2,1)S(1)} %collective-permute-done.77.refs_0_.refs_3_, f32[128,1792]{1,0:T(8,128)S(1)} %copy-done.89, f32[128,1792]{1,0:T(8,128)S(1)} %copy-done.91, ...), custom_call_target="tpu_custom_call" | custom-call | tf_op jit(solution)/shard_map/pallas_call | solution.py:131
  703.3 23.5 %collective-permute-done.76.refs_5_ = bf16[128,1536]{1,0:T(8,128)(2,1)} collective-permute-done((bf16[128,1536]{1,0:T(8,128)(2,1)}, bf16[128,1536]{1,0:T(8,128)(2,1)}, u32[]{:S(2)}, u32[]{:S(2)}) %collective-permute-start.76) | collective-permute-done | bytes 393248 | tf_op jit(solution)/shard_map/ppermute | solution.py:48
  726.9 10.3 collective-permute-done.78.refs_6_
  744.9 15.7 %shard_map.354 = (bf16[1536,3584]{1,0:T(8,128)(2,1)}, f32[8,128]{1,0:T(8,128)}) custom-call(bf16[128,1536]{1,0:T(8,128)(2,1)} %copy-done.133, bf16[128,1536]{1,0:T(8,128)(2,1)} %copy-done.134, bf16[128,1536]{1,0:T(8,128)(2,1)} %copy-done.129, bf16[128,1536]{1,0:T(8,128)(2,1)} %copy-done.130, bf16[256,1792]{1,0:T(8,128)(2,1)} %copy-done.176, ...), custom_call_target="tpu_custom_call" | custom-call | flops 16911433728 | bytes 66060288 | tf_op jit(solution)/shard_map/pallas_call | solution.py:131
  799.6 9.4 shard_map.359
  809.0 12.6 %collective-permute-done.88.refs_8_.refs_3_ = bf16[48,3584]{1,0:T(8,128)(2,1)S(1)} collective-permute-done((bf16[48,3584]{1,0:T(8,128)(2,1)}, bf16[48,3584]{1,0:T(8,128)(2,1)S(1)}, u32[]{:S(2)}, u32[]{:S(2)}) %collective-permute-start.88) | collective-permute-done | bytes 344096 | tf_op jit(solution)/shard_map/ppermute | solution.py:48
  850.2 11.5 %collective-permute-done.90.refs_2_ = bf16[8,48,768]{2,1,0:T(8,128)(2,1)S(1)} collective-permute-done((bf16[8,48,768]{2,1,0:T(8,128)(2,1)}, bf16[8,48,768]{2,1,0:T(8,128)(2,1)S(1)}, u32[]{:S(2)}, u32[]{:S(2)}) %collective-permute-start.90) | collective-permute-done | bytes 589856 | tf_op jit(solution)/shard_map/ppermute | solution.py:48
  879.4 26.6 %collective-permute-done.113 = f32[4,192]{1,0:T(4,128)S(1)} collective-permute-done((f32[4,192]{1,0:T(4,128)S(1)}, f32[4,192]{1,0:T(4,128)S(1)}, u32[]{:S(2)}, u32[]{:S(2)}) %collective-permute-start.113) | collective-permute-done | bytes 3104 | tf_op jit(solution)/shard_map/ppermute | solution.py:39
  923.7 14.8 %collective-permute-done.92.refs_2_.refs_4_ = bf16[8,48,768]{2,1,0:T(8,128)(2,1)} collective-permute-done((bf16[8,48,768]{2,1,0:T(8,128)(2,1)}, bf16[8,48,768]{2,1,0:T(8,128)(2,1)}, u32[]{:S(2)}, u32[]{:S(2)}) %collective-permute-start.92) | collective-permute-done | bytes 589856 | tf_op jit(solution)/shard_map/ppermute | solution.py:48
  966.9 11.7 %collective-permute-done.98.refs_3_ = bf16[2,48,768]{2,1,0:T(8,128)(2,1)S(1)} collective-permute-done((bf16[2,48,768]{2,1,0:T(8,128)(2,1)S(1)}, bf16[2,48,768]{2,1,0:T(8,128)(2,1)S(1)}, u32[]{:S(2)}, u32[]{:S(2)}) %collective-permute-start.98) | collective-permute-done | bytes 147488 | tf_op jit(solution)/shard_map/ppermute | solution.py:39
  (788 shorter events, 577.8 us)
Async XLA Ops:
  7.2 231.8 %all-gather.8.cloned.1.call-start = ((), (), s32[]{:S(2)}) async-start(), calls=%async_computation.4 | async-start | bytes 6193152 | tf_op jit(solution)/shard_map/all_gather | solution.py:338
  11.0 228.0 %all-gather.6.cloned.1.call-start = ((), (), s32[]{:S(2)}) async-start(), calls=%async_computation.3 | async-start | bytes 12386304 | tf_op jit(solution)/shard_map/all_gather | solution.py:338
  57.2 275.2 %all-gather.10.cloned.1.call-start = ((), (), s32[]{:S(2)}) async-start(), calls=%async_computation.5 | async-start | bytes 2949120 | tf_op jit(solution)/shard_map/all_gather | solution.py:1107
  85.4 303.4 %all-gather.14.cloned.1.call-start = ((), (), s32[]{:S(2)}) async-start(), calls=%async_computation.7 | async-start | bytes 6193152 | tf_op jit(solution)/shard_map/all_gather | solution.py:338
  86.2 40.5 %collective-permute-start.28 = (bf16[8,48,768]{2,1,0:T(8,128)(2,1)S(1)}, bf16[8,48,768]{2,1,0:T(8,128)(2,1)S(1)}, u32[]{:S(2)}, u32[]{:S(2)}) collective-permute-start(bf16[8,48,768]{2,1,0:T(8,128)(2,1)S(1)} %get-tuple-element.305.refs_2_), channel_id=1, source_target_pairs={{0,2},{1,3},{2,0},{3,1},{4,6},{5,7},{6,4},{7,5},{8,10},{9,11},{10,... | collective-permute-start | bytes 1769480 | tf_op jit(solution)/shard_map/ppermute | solution.py:48
  89.2 51.5 %collective-permute-start.29 = (bf16[8,48,768]{2,1,0:T(8,128)(2,1)S(1)}, bf16[8,48,768]{2,1,0:T(8,128)(2,1)S(1)}, u32[]{:S(2)}, u32[]{:S(2)}) collective-permute-start(bf16[8,48,768]{2,1,0:T(8,128)(2,1)S(1)} %get-tuple-element.305.refs_2_), channel_id=1, source_target_pairs={{0,3},{1,2},{2,1},{3,0},{4,7},{5,6},{6,5},{7,4},{8,11},{9,10},{10,... | collective-permute-start | bytes 1769480 | tf_op jit(solution)/shard_map/ppermute | solution.py:48
  91.2 49.5 %collective-permute-start.25 = (bf16[128,1536]{1,0:T(8,128)(2,1)S(1)}, bf16[128,1536]{1,0:T(8,128)(2,1)S(1)}, u32[]{:S(2)}, u32[]{:S(2)}) collective-permute-start(bf16[128,1536]{1,0:T(8,128)(2,1)S(1)} %get-tuple-element.311.refs_0_), channel_id=1, source_target_pairs={{0,8},{4,12},{8,0},{12,4},{16,24},{20,28},{24,16},{28,20},{1,9},{5... | collective-permute-start | bytes 1179656 | tf_op jit(solution)/shard_map/ppermute | solution.py:39
  92.7 48.0 %collective-permute-start.26 = (bf16[128,1536]{1,0:T(8,128)(2,1)S(1)}, bf16[128,1536]{1,0:T(8,128)(2,1)S(1)}, u32[]{:S(2)}, u32[]{:S(2)}) collective-permute-start(bf16[128,1536]{1,0:T(8,128)(2,1)S(1)} %get-tuple-element.311.refs_0_), channel_id=1, source_target_pairs={{0,16},{4,20},{8,24},{12,28},{16,0},{20,4},{24,8},{28,12},{1,17},{... | collective-permute-start | bytes 1179656 | tf_op jit(solution)/shard_map/ppermute | solution.py:39
  94.4 46.3 %collective-permute-start.27 = (bf16[128,1536]{1,0:T(8,128)(2,1)S(1)}, bf16[128,1536]{1,0:T(8,128)(2,1)S(1)}, u32[]{:S(2)}, u32[]{:S(2)}) collective-permute-start(bf16[128,1536]{1,0:T(8,128)(2,1)S(1)} %get-tuple-element.311.refs_0_), channel_id=1, source_target_pairs={{0,24},{4,28},{8,16},{12,20},{16,8},{20,12},{24,0},{28,4},{1,25},{... | collective-permute-start | bytes 1179656 | tf_op jit(solution)/shard_map/ppermute | solution.py:39
  140.8 248.1 %all-gather.12.cloned.1.call-start = ((), (), s32[]{:S(2)}) async-start(), calls=%async_computation.6 | async-start | bytes 12386304 | tf_op jit(solution)/shard_map/all_gather | solution.py:338
  166.5 56.4 %collective-permute-start.38 = (bf16[1,48,3584]{2,1,0:T(8,128)(2,1)S(1)}, bf16[1,48,3584]{2,1,0:T(8,128)(2,1)S(1)}, u32[]{:S(2)}, u32[]{:S(2)}) collective-permute-start(bf16[1,48,3584]{2,1,0:T(8,128)(2,1)S(1)} %get-tuple-element.558), channel_id=1, source_target_pairs={{0,3},{1,2},{2,1},{3,0},{4,7},{5,6},{6,5},{7,4},{8,11},{9,10},{10,... | collective-permute-start | bytes 1032200 | tf_op jit(solution)/shard_map/ppermute | solution.py:48
  224.1 536.5 %reduce-scatter.4.cloned.1.call-start = ((), (), s32[]{:S(2)}) async-start(), calls=%async_computation.8 | async-start | bytes 12386304 | tf_op jit(solution)/shard_map/reduce_scatter | solution.py:453
  226.6 38.8 %collective-permute-start.42 = (bf16[128,1536]{1,0:T(8,128)(2,1)S(1)}, bf16[128,1536]{1,0:T(8,128)(2,1)S(1)}, u32[]{:S(2)}, u32[]{:S(2)}) collective-permute-start(bf16[128,1536]{1,0:T(8,128)(2,1)S(1)} %get-tuple-element.329.refs_0_), channel_id=1, source_target_pairs={{0,3},{1,2},{2,1},{3,0},{4,7},{5,6},{6,5},{7,4},{8,11},{9,10},{10,... | collective-permute-start | bytes 1179656 | tf_op jit(solution)/shard_map/ppermute | solution.py:48
  341.1 41.3 %collective-permute-start.48 = (bf16[4,128,1536]{2,1,0:T(8,128)(2,1)S(1)}, bf16[4,128,1536]{2,1,0:T(8,128)(2,1)S(1)}, u32[]{:S(2)}, u32[]{:S(2)}) collective-permute-start(bf16[4,128,1536]{2,1,0:T(8,128)(2,1)S(1)} %get-tuple-element.351), channel_id=1, source_target_pairs={{0,4},{4,0},{8,12},{12,8},{16,20},{20,16},{24,28},{28,24},{1,5},{5... | collective-permute-start | bytes 4718600 | tf_op jit(solution)/shard_map/ppermute | solution.py:39
  418.0 52.9 %collective-permute-start.59 = (bf16[128,1536]{1,0:T(8,128)(2,1)S(1)}, bf16[128,1536]{1,0:T(8,128)(2,1)S(1)}, u32[]{:S(2)}, u32[]{:S(2)}) collective-permute-start(bf16[128,1536]{1,0:T(8,128)(2,1)S(1)} %get-tuple-element.363.refs_0_), channel_id=1, source_target_pairs={{0,3},{1,2},{2,1},{3,0},{4,7},{5,6},{6,5},{7,4},{8,11},{9,10},{10,... | collective-permute-start | bytes 1179656 | tf_op jit(solution)/shard_map/ppermute | solution.py:48
  436.3 77.4 %collective-permute-start.56 = (bf16[128,1536]{1,0:T(8,128)(2,1)S(1)}, bf16[128,1536]{1,0:T(8,128)(2,1)S(1)}, u32[]{:S(2)}, u32[]{:S(2)}) collective-permute-start(bf16[128,1536]{1,0:T(8,128)(2,1)S(1)} %get-tuple-element.366), channel_id=1, source_target_pairs={{0,1},{1,0},{2,3},{3,2},{4,5},{5,4},{6,7},{7,6},{8,9},{9,8},{10,11... | collective-permute-start | bytes 1179656 | tf_op jit(solution)/shard_map/ppermute | solution.py:48
  450.2 64.8 %collective-permute-start.58 = (bf16[128,1536]{1,0:T(8,128)(2,1)S(1)}, bf16[128,1536]{1,0:T(8,128)(2,1)S(1)}, u32[]{:S(2)}, u32[]{:S(2)}) collective-permute-start(bf16[128,1536]{1,0:T(8,128)(2,1)S(1)} %get-tuple-element.368), channel_id=1, source_target_pairs={{0,2},{1,3},{2,0},{3,1},{4,6},{5,7},{6,4},{7,5},{8,10},{9,11},{10,... | collective-permute-start | bytes 1179656 | tf_op jit(solution)/shard_map/ppermute | solution.py:48
  558.3 386.0 %reduce-scatter.6.cloned.1.call-start = ((), (), s32[]{:S(2)}) async-start(), calls=%async_computation.9 | async-start | bytes 2949120 | tf_op jit(solution)/shard_map/reduce_scatter | solution.py:1207
  620.1 39.1 %collective-permute-start.75 = (bf16[4,224,1536]{2,1,0:T(8,128)(2,1)}, bf16[4,224,1536]{2,1,0:T(8,128)(2,1)}, u32[]{:S(2)}, u32[]{:S(2)}) collective-permute-start(bf16[4,224,1536]{2,1,0:T(8,128)(2,1)} %get-tuple-element.433), channel_id=1, source_target_pairs={{0,4},{4,0},{8,12},{12,8},{16,20},{20,16},{24,28},{28,24},{1,5},{5... | collective-permute-start | bytes 8257544 | tf_op jit(solution)/shard_map/ppermute | solution.py:39
  620.1 361.1 %reduce-scatter.8.cloned.1.call-start = ((), (), s32[]{:S(2)}) async-start(), calls=%async_computation.10 | async-start | bytes 12386304 | tf_op jit(solution)/shard_map/reduce_scatter | solution.py:453
  620.5 45.3 %collective-permute-start.74 = (bf16[128,1536]{1,0:T(8,128)(2,1)}, bf16[128,1536]{1,0:T(8,128)(2,1)S(1)}, u32[]{:S(2)}, u32[]{:S(2)}) collective-permute-start(bf16[128,1536]{1,0:T(8,128)(2,1)} %get-tuple-element.422.refs_0_), channel_id=1, source_target_pairs={{0,2},{1,3},{2,0},{3,1},{4,6},{5,7},{6,4},{7,5},{8,10},{9,11},{10,... | collective-permute-start | bytes 1179656 | tf_op jit(solution)/shard_map/ppermute | solution.py:48
  620.6 60.8 %collective-permute-start.77 = (bf16[128,1536]{1,0:T(8,128)(2,1)}, bf16[128,1536]{1,0:T(8,128)(2,1)S(1)}, u32[]{:S(2)}, u32[]{:S(2)}) collective-permute-start(bf16[128,1536]{1,0:T(8,128)(2,1)} %get-tuple-element.422.refs_0_), channel_id=1, source_target_pairs={{0,3},{1,2},{2,1},{3,0},{4,7},{5,6},{6,5},{7,4},{8,11},{9,10},{10,... | collective-permute-start | bytes 1179656 | tf_op jit(solution)/shard_map/ppermute | solution.py:48
  656.9 46.5 %collective-permute-start.73 = (bf16[128,1536]{1,0:T(8,128)(2,1)}, bf16[128,1536]{1,0:T(8,128)(2,1)}, u32[]{:S(2)}, u32[]{:S(2)}) collective-permute-start(bf16[128,1536]{1,0:T(8,128)(2,1)} %get-tuple-element.429), channel_id=1, source_target_pairs={{0,1},{1,0},{2,3},{3,2},{4,5},{5,4},{6,7},{7,6},{8,9},{9,8},{10,11... | collective-permute-start | bytes 1179656 | tf_op jit(solution)/shard_map/ppermute | solution.py:48
  679.5 47.4 %collective-permute-start.76 = (bf16[128,1536]{1,0:T(8,128)(2,1)}, bf16[128,1536]{1,0:T(8,128)(2,1)}, u32[]{:S(2)}, u32[]{:S(2)}) collective-permute-start(bf16[128,1536]{1,0:T(8,128)(2,1)} %get-tuple-element.436), channel_id=1, source_target_pairs={{0,2},{1,3},{2,0},{3,1},{4,6},{5,7},{6,4},{7,5},{8,10},{9,11},{10,... | collective-permute-start | bytes 1179656 | tf_op jit(solution)/shard_map/ppermute | solution.py:48
  694.0 43.2 %collective-permute-start.78 = (bf16[128,1536]{1,0:T(8,128)(2,1)}, bf16[128,1536]{1,0:T(8,128)(2,1)S(1)}, u32[]{:S(2)}, u32[]{:S(2)}) collective-permute-start(bf16[128,1536]{1,0:T(8,128)(2,1)} %get-tuple-element.440), channel_id=1, source_target_pairs={{0,3},{1,2},{2,1},{3,0},{4,7},{5,6},{6,5},{7,4},{8,11},{9,10},{10,... | collective-permute-start | bytes 1179656 | tf_op jit(solution)/shard_map/ppermute | solution.py:48
  871.5 67.0 %collective-permute-start.93 = (bf16[4,224,1536]{2,1,0:T(8,128)(2,1)}, bf16[4,224,1536]{2,1,0:T(8,128)(2,1)}, u32[]{:S(2)}, u32[]{:S(2)}) collective-permute-start(bf16[4,224,1536]{2,1,0:T(8,128)(2,1)} %get-tuple-element.491), channel_id=1, source_target_pairs={{0,4},{4,0},{8,12},{12,8},{16,20},{20,16},{24,28},{28,24},{1,5},{5... | collective-permute-start | bytes 8257544 | tf_op jit(solution)/shard_map/ppermute | solution.py:39
  872.4 41.8 %collective-permute-start.94 = (bf16[224,1536]{1,0:T(8,128)(2,1)}, bf16[224,1536]{1,0:T(8,128)(2,1)}, u32[]{:S(2)}, u32[]{:S(2)}) collective-permute-start(bf16[224,1536]{1,0:T(8,128)(2,1)} %copy-done.181), channel_id=1, source_target_pairs={{0,8},{4,12},{8,0},{12,4},{16,24},{20,28},{24,16},{28,20},{1,9},{5... | collective-permute-start | bytes 2064392 | tf_op jit(solution)/shard_map/ppermute | solution.py:39
  874.2 40.0 %collective-permute-start.95 = (bf16[224,1536]{1,0:T(8,128)(2,1)}, bf16[224,1536]{1,0:T(8,128)(2,1)}, u32[]{:S(2)}, u32[]{:S(2)}) collective-permute-start(bf16[224,1536]{1,0:T(8,128)(2,1)} %copy-done.180), channel_id=1, source_target_pairs={{0,16},{4,20},{8,24},{12,28},{16,0},{20,4},{24,8},{28,12},{1,17},{... | collective-permute-start | bytes 2064392 | tf_op jit(solution)/shard_map/ppermute | solution.py:39
  875.7 38.6 %collective-permute-start.96 = (bf16[224,1536]{1,0:T(8,128)(2,1)}, bf16[224,1536]{1,0:T(8,128)(2,1)}, u32[]{:S(2)}, u32[]{:S(2)}) collective-permute-start(bf16[224,1536]{1,0:T(8,128)(2,1)} %copy-done.179), channel_id=1, source_target_pairs={{0,24},{4,28},{8,16},{12,20},{16,8},{20,12},{24,0},{28,4},{1,25},{... | collective-permute-start | bytes 2064392 | tf_op jit(solution)/shard_map/ppermute | solution.py:39
  942.7 46.9 %collective-permute-start.104 = (bf16[224,1536]{1,0:T(8,128)(2,1)}, bf16[224,1536]{1,0:T(8,128)(2,1)}, u32[]{:S(2)}, u32[]{:S(2)}) collective-permute-start(bf16[224,1536]{1,0:T(8,128)(2,1)} %get-tuple-element.502), channel_id=1, source_target_pairs={{0,8},{4,12},{8,0},{12,4},{16,24},{20,28},{24,16},{28,20},{1,9},{5... | collective-permute-start | bytes 2064392 | tf_op jit(solution)/shard_map/ppermute | solution.py:39
  950.8 41.7 %collective-permute-start.105 = (bf16[224,1536]{1,0:T(8,128)(2,1)}, bf16[224,1536]{1,0:T(8,128)(2,1)S(1)}, u32[]{:S(2)}, u32[]{:S(2)}) collective-permute-start(bf16[224,1536]{1,0:T(8,128)(2,1)} %get-tuple-element.503), channel_id=1, source_target_pairs={{0,16},{4,20},{8,24},{12,28},{16,0},{20,4},{24,8},{28,12},{1,17},{... | collective-permute-start | bytes 2064392 | tf_op jit(solution)/shard_map/ppermute | solution.py:39
  951.4 41.9 %collective-permute-start.106 = (bf16[224,1536]{1,0:T(8,128)(2,1)}, bf16[224,1536]{1,0:T(8,128)(2,1)}, u32[]{:S(2)}, u32[]{:S(2)}) collective-permute-start(bf16[224,1536]{1,0:T(8,128)(2,1)} %get-tuple-element.504), channel_id=1, source_target_pairs={{0,24},{4,28},{8,16},{12,20},{16,8},{20,12},{24,0},{28,4},{1,25},{... | collective-permute-start | bytes 2064392 | tf_op jit(solution)/shard_map/ppermute | solution.py:39
  (311 other events, 3932.6 us)
Sparse Core Ops, SparseCore 0:
  11.1 46.5 all-gather.7
  60.2 83.2 all-gather.5
  145.6 76.0 all-gather.9
  224.0 44.5 all-gather.13
  271.0 79.6 all-gather.11
  558.4 92.9 reduce-scatter.3
  654.3 75.8 reduce-scatter.5
  774.1 94.9 reduce-scatter.7

commit v5 on v4

--- a/solution.py
+++ b/solution.py
@@ -137,7 +137,7 @@
         input_output_aliases=aliases,
         compiler_params=pltpu.CompilerParams(
             vmem_limit_bytes=56 << 20
-            if cost[0]
+            if cost[0] or aliases and not grid
             else min(vmem_of(operands, in_specs, out_shape, out_specs, scratch, grid), 60 << 20)
         ),
         cost_estimate=pl.CostEstimate(
@@ -398,7 +398,7 @@
     )(*scalars, *grads, *state, *(previous or ()), *earlier)
 
 
-def mix_reduce(layers):
+def mix_reduce(layers, earlier):
     seqs, rows, width = layers[0][0].shape
     count = len(layers)
     chunk = width // 4
@@ -419,6 +419,7 @@
         body,
         [shaped((seqs, count, rows, width), low), shaped((count, rows, seqs * chunk))],
         scalars=1,
+        earlier=earlier,
     )(place_of("seq"), *sum((list(pieces) for pieces in layers), []))
     return [inner[0]] + [seq_swap(inner[j], j) for j in range(1, seqs)] + [last]
 
@@ -495,14 +496,14 @@
     )
 
 
-def down_adam(parts, state, layer, previous):
+def down_adam(parts, state, layer, previous, earlier=()):
     def load(scalars, grads, scratch, total):
         sums = grads[0][...].astype(jnp.float32)
         for grad in grads[1:]:
             sums = sums + grad[...].astype(jnp.float32)
         total[...] = sums[: total.shape[0]]
 
-    return adam_kernel(load, [], parts, state, layer, previous)
+    return adam_kernel(load, [], parts, state, layer, previous, earlier=earlier)
 
 
 def split_down(part, earlier):
@@ -545,12 +546,13 @@
     return gather_fsdp(jnp.concatenate([gains, taps], axis=0).astype(low))
 
 
-def vectors_middle(blocks):
+def vectors_middle(blocks, earlier):
     rings = lax.axis_size("fsdp")
     both = place_blocks(
         blocks,
         lambda place: [lax.bitwise_xor(place, jnp.int32(j)) for j in range(rings)],
         place_of("fsdp"),
+        earlier,
     )
     return both, send_seq(both)
 
@@ -1040,11 +1042,16 @@
 
 
 def join_blocks(blocks):
-    def body(*refs):
-        for i in range(len(blocks)):
-            refs[len(blocks) + i][...] = refs[i][...]
-
-    return plain_call(body, [shaped(block.shape, block.dtype) for block in blocks])(*blocks)
+    rings = lax.axis_size("fsdp")
+    blocks = blocks.reshape(rings, -1, blocks.shape[-1])
+
+    def body(place, blocks, *outs):
+        for j in range(rings):
+            outs[j][...] = blocks[lax.bitwise_xor(place[0], jnp.int32(j))]
+
+    return plain_call(body, [shaped(blocks.shape[1:], blocks.dtype)] * rings, scalars=1)(
+        place_of("fsdp"), blocks
+    )
 
 
 def groups_of(blocks):
@@ -1094,10 +1101,11 @@
     mixes, feeds = [None] * LAYERS, [None] * LAYERS
     vector_blocks = vectors_start(gain_weight, tap_weight)
     feed_swap = swap_feed(pack_feed(feed_weight, 0))
+    later_feed = swap_feed(pack_feed(feed_weight, 1))
     mix_packed = pack_mix(mix_weight, 0, vector_blocks[1:])
     mix_swap = swap_mix(mix_packed)
     down_rows = gather_rows(pack_down(down_weight, 0))
-    both, vector_blocks = vectors_middle(vector_blocks)
+    both, vector_blocks = vectors_middle(vector_blocks, later_feed[1:])
     mix_pieces = gather_fsdp(join_mix(mix_swap, mix_packed))
     feeds[0] = (gather_rows(assemble_feed(feed_swap)), down_rows)
     later_packed = pack_mix(mix_weight, 1)
@@ -1110,9 +1118,8 @@
     gain_rows, tap_rows = vectors_end(both, vector_blocks)
     stream, normed = first_norm(inputs.reshape(-1, features), gain_rows[0, 0], ())
     blocks = send_seq(normed)
-    later_feed = pack_feed(feed_weight, 1)
-    *blocks, down_packed = stack_pairs(blocks, mix_pieces[2:], [pack_down(down_weight, 1)])
-    later_down = gather_rows(down_packed)
+    later_feed = assemble_feed(later_feed)
+    blocks = stack_pairs(blocks, mix_pieces[2:])
     mixes[0] = assemble_mix(mix_pieces, wide)
 
     kept = []
@@ -1121,29 +1128,31 @@
         gathered = blocks
         projected, even, odd = mixer_forward(blocks, *mixes[layer], tap_rows[layer])
         odd = seq_swap(odd, 1)
-        if last:
-            flow_low = join_blocks(gather_fsdp(flow_low))
-            (sums,) = pair_sum(even, odd)
-        else:
-            sums, later_feed = pair_sum(even, odd, (), [later_feed])
-            later_feed = swap_feed(later_feed)
-        middle, normed_two = finish(
-            stream, sums, gain_rows[layer, 1], feeds[layer] if last else ()
+        (sums,) = pair_sum(even, odd)
+        middle, normed_two, *later = finish(
+            stream,
+            sums,
+            gain_rows[layer, 1],
+            feeds[layer] if last else (),
+            () if last else (later_feed, pack_down(down_weight, 1)),
         )
         two_blocks = gather_fsdp(normed_two)
         if not last:
-            feeds[1] = (gather_rows(assemble_feed(later_feed)), later_down)
+            feeds[1] = tuple(gather_rows(part) for part in later)
         sums, values = [], []
         for number, group in enumerate(groups_of(two_blocks)):
             outs, saved = feed_forward(group, *feeds[layer], number == 0)
             sums += outs
             values.append(saved)
+            if number == 0 and last:
+                flow_low = join_blocks(flow_low)
         kept.append((stream, middle, gathered, projected, two_blocks, values))
         sums = return_sums(sums)
         if not last:
             stream, normed, flow_low = finish(
                 middle, sums, gain_rows[layer + 1, 0], (), [cotangent]
             )
+            flow_low = lax.all_gather(flow_low, "fsdp", axis=0, tiled=True)
             blocks = stack_pairs(send_seq(normed))
             mixes[1] = assemble_mix([later_mix], wide)
 
@@ -1159,9 +1168,6 @@
         last = layer + 1 == LAYERS
         stream, middle, gathered, projected, two_blocks, values = kept[layer]
         back_sums, gate_flows, up_flows = [], [], []
-        if not last:
-            even, odd = split_down(later_down, ())
-            odd = seq_swap(odd, 1)
         for number, group in enumerate(groups_of(flow_low)):
             gates, ups, _ = values[number]
             outs, (gate_flow, up_flow) = feed_backward(
@@ -1170,15 +1176,23 @@
             back_sums += outs
             gate_flows.append(gate_flow)
             up_flows.append(up_flow)
-            if number == 0 and not last:
-                (later_down,) = pair_sum(even, odd)
         if last:
             outputs = finish(middle, sums, None).reshape(inputs.shape)
         back_sums = return_sums(back_sums)
         down_part = down_grads([value[2] for value in values], flow_low)
-        middle_flow, middle_low, gain_two = finish_back(
-            flow, back_sums, middle, gain_rows[layer, 1]
+        middle_flow, middle_low, gain_two, *later_mix = finish_back(
+            flow, back_sums, middle, gain_rows[layer, 1], [down_part] if last else [later_mix]
         )
+        if last:
+            (down_part,) = later_mix
+            down_part = [scatter_rows(down_part)]
+        else:
+            later_mix = lax.psum_scatter(
+                later_mix[0].reshape(-1, later_mix[0].shape[-1]),
+                "fsdp",
+                scatter_dimension=0,
+                tiled=True,
+            ).reshape(later_mix[0].shape[1:])
         blocks = send_seq(middle_low)
         feed_part = feed_grads(two_blocks, gate_flows, up_flows)
         if not last:
@@ -1204,22 +1218,17 @@
         gain_grads[layer] = jnp.concatenate([gain_one, gain_two])
         if last:
             flow_low = gather_fsdp(low_flow)
-            later_mix = lax.psum_scatter(
-                mix_part[0].reshape(-1, mix_part[0].shape[-1]),
-                "fsdp",
-                scatter_dimension=0,
-                tiled=True,
-            ).reshape(mix_part[0].shape[1:])
+            (later_mix,) = mix_part
             later_feed, later_down = feed_part, down_part
     new[1] = feed_adam(later_feed, states[1], 1, new[1])
-    even, odd = split_down(down_part, mix_part[1:3])
-    odd = seq_swap(odd, 1)
-    new[2] = down_adam(later_down, states[2], 1, new[2])
-    (down_part,) = pair_sum(even, odd, mix_part[3:])
     gain_grad, tap_grad = vector_gradients(
         jnp.stack(gain_grads), jnp.stack(tap_grads), gain_weight.shape[-1]
     )
-    mix_part = mix_reduce([mix_part, [later_mix]])
+    new[2] = down_adam(later_down, states[2], 1, new[2], [gain_grad])
+    even, odd = split_down(down_part, mix_part[1:])
+    odd = seq_swap(odd, 1)
+    mix_part = mix_reduce([mix_part, [later_mix]], ())
+    (down_part,) = pair_sum(even, odd)
     feed_part = split_feed(feed_part, rows)
     new[2] = down_adam(down_part, states[2], 0, new[2])
     new[0] = mix_adam(mix_part, states[0])

time: 1050 us -> 1020 us (0.971)
  waiting for transfers between devices: 482 us -> 456 us
  local copies, waits for them, and re-layouts: 155 us -> 140 us
  Pallas kernels: 256 us -> 268 us
    ppermute x69 -> x65, waiting for transfers between devices: 171 us -> 156 us  [seq_swap(): return lax.ppermute(array, 'seq', [(i, i ^ by) for i in range(count)])]
    unnamed x446 -> x438, local copies, waits for them, and re-layouts: 148 us -> 134 us
    ppermute x48 -> x45, waiting for transfers between devices: 312 us -> 298 us  [fsdp_swap(): return lax.ppermute(array, 'fsdp', [(i, i ^ by) for i in range(count)])]
    pallas_call x65 -> x63, Pallas kernels: 256 us -> 268 us  [ordered_call(): pl.pallas_call(marked, in_specs=list(in_specs) + [anywhere], out_specs=li...]
    ppermute x48 -> x45, starting transfers between devices: 54.4 us -> 62.8 us  [fsdp_swap(): return lax.ppermute(array, 'fsdp', [(i, i ^ by) for i in range(count)])]
    ppermute x69 -> x65, starting transfers between devices: 68.4 us -> 62 us  [seq_swap(): return lax.ppermute(array, 'seq', [(i, i ^ by) for i in range(count)])]
  transfers between devices with their start and end apart: 125 -> 120, of which waited for: 63 -> 52; matrix products, arithmetic and copies ran while one was open for 1% -> 1% of each run, Pallas kernels for 24% -> 25%
where the time goes in v5:
time: 1020 us; the launch traced here: 1010 us
  waiting for transfers between devices  456 us (45%)
  Pallas kernels  268 us (26%)
  local copies, waits for them, and re-layouts  140 us (14%)
  starting transfers between devices  126 us (12%)
  between operations  16.4 us (2%)
    ppermute x45, waiting for transfers between devices, fsdp_swap(): return lax.ppermute(array, 'fsdp', [(i, i ^ by) for i in range(count)])  298 us
    pallas_call x63, Pallas kernels, ordered_call(): pl.pallas_call(marked, in_specs=list(in_specs) + [anywhere], out_specs=li...  268 us
    ppermute x65, waiting for transfers between devices, seq_swap(): return lax.ppermute(array, 'seq', [(i, i ^ by) for i in range(count)])  156 us
    unnamed x438, local copies, waits for them, and re-layouts  134 us
    ppermute x45, starting transfers between devices, fsdp_swap(): return lax.ppermute(array, 'fsdp', [(i, i ^ by) for i in range(count)])  62.8 us
    ppermute x65, starting transfers between devices, seq_swap(): return lax.ppermute(array, 'seq', [(i, i ^ by) for i in range(count)])  62 us
  transfers between devices with their start and end apart: 120, of which 52 were waited for; matrix products, arithmetic and copies ran while one was open for 1% of the time, Pallas kernels for 25%

profile of v5, /device:TPU:8, one launch (start us, length us, event | category | flops | bytes accessed | tf_op | source)
XLA Modules:
  0.0 1010.1 jit_solution(11307786425566579541)
XLA Ops:
  44.9 8.8 collective-permute-done.4.refs_6_.refs_3_
  56.2 20.7 %collective-permute-done.5.refs_7_.refs_4_ = bf16[1,48,3584]{2,1,0:T(8,128)(2,1)S(1)} collective-permute-done((bf16[1,48,3584]{2,1,0:T(8,128)(2,1)S(1)}, bf16[1,48,3584]{2,1,0:T(8,128)(2,1)S(1)}, u32[]{:S(2)}, u32[]{:S(2)}) %collective-permute-start.5) | collective-permute-done | bytes 344096 | tf_op jit(solution)/shard_map/ppermute | solution.py:48
  129.8 30.9 %collective-permute-done.31.refs_4_ = bf16[8,48,768]{2,1,0:T(8,128)(2,1)S(1)} collective-permute-done((bf16[8,48,768]{2,1,0:T(8,128)(2,1)}, bf16[8,48,768]{2,1,0:T(8,128)(2,1)S(1)}, u32[]{:S(2)}, u32[]{:S(2)}) %collective-permute-start.31) | collective-permute-done | bytes 589856 | tf_op jit(solution)/shard_map/ppermute | solution.py:48
  160.7 13.6 %collective-permute-done.32.refs_5_ = bf16[8,48,768]{2,1,0:T(8,128)(2,1)S(1)} collective-permute-done((bf16[8,48,768]{2,1,0:T(8,128)(2,1)}, bf16[8,48,768]{2,1,0:T(8,128)(2,1)S(1)}, u32[]{:S(2)}, u32[]{:S(2)}) %collective-permute-start.32) | collective-permute-done | bytes 589856 | tf_op jit(solution)/shard_map/ppermute | solution.py:48
  201.3 8.9 collective-permute-done.36.refs_3_
  218.5 25.5 %collective-permute-done.38.refs_1_ = bf16[128,1536]{1,0:T(8,128)(2,1)S(1)} collective-permute-done((bf16[128,1536]{1,0:T(8,128)(2,1)}, bf16[128,1536]{1,0:T(8,128)(2,1)S(1)}, u32[]{:S(2)}, u32[]{:S(2)}) %collective-permute-start.38) | collective-permute-done | bytes 393248 | tf_op jit(solution)/shard_map/ppermute | solution.py:48
  280.3 16.6 %collective-permute-done.41.refs_3_ = bf16[128,1536]{1,0:T(8,128)(2,1)S(1)} collective-permute-done((bf16[128,1536]{1,0:T(8,128)(2,1)S(1)}, bf16[128,1536]{1,0:T(8,128)(2,1)S(1)}, u32[]{:S(2)}, u32[]{:S(2)}) %collective-permute-start.41) | collective-permute-done | bytes 393248 | tf_op jit(solution)/shard_map/ppermute | solution.py:48
  296.9 9.1 collective-permute-done.43.refs_4_
  313.1 11.5 %collective-permute-done.44.refs_1_ = bf16[128,1536]{1,0:T(8,128)(2,1)S(1)} collective-permute-done((bf16[128,1536]{1,0:T(8,128)(2,1)}, bf16[128,1536]{1,0:T(8,128)(2,1)S(1)}, u32[]{:S(2)}, u32[]{:S(2)}) %collective-permute-start.44) | collective-permute-done | bytes 393248 | tf_op jit(solution)/shard_map/ppermute | solution.py:39
  324.9 8.5 collective-permute-done.46.refs_3_
  363.0 15.9 %collective-permute-done.49.refs_2_ = bf16[128,1536]{1,0:T(8,128)(2,1)S(1)} collective-permute-done((bf16[128,1536]{1,0:T(8,128)(2,1)}, bf16[128,1536]{1,0:T(8,128)(2,1)S(1)}, u32[]{:S(2)}, u32[]{:S(2)}) %collective-permute-start.49) | collective-permute-done | bytes 393248 | tf_op jit(solution)/shard_map/ppermute | solution.py:39
  378.9 9.1 collective-permute-done.51.refs_4_
  403.0 29.0 %collective-permute-done.52.refs_1_ = bf16[128,1536]{1,0:T(8,128)(2,1)S(1)} collective-permute-done((bf16[128,1536]{1,0:T(8,128)(2,1)}, bf16[128,1536]{1,0:T(8,128)(2,1)S(1)}, u32[]{:S(2)}, u32[]{:S(2)}) %collective-permute-start.52) | collective-permute-done | bytes 393248 | tf_op jit(solution)/shard_map/ppermute | solution.py:48
  432.0 9.2 shard_map.331
  470.4 11.3 %shard_map.335 = (f32[128,1536]{1,0:T(8,128)S(1)}, bf16[128,1536]{1,0:T(8,128)(2,1)}, bf16[256,1792]{1,0:T(8,128)(2,1)S(1)}, bf16[256,1792]{1,0:T(8,128)(2,1)S(1)}, f32[8,128]{1,0:T(8,128)S(1)}) custom-call(bf16[128,1536]{1,0:T(8,128)(2,1)S(1)} %get-tuple-element.371.refs_0_, bf16[128,1536]{1,0:T(8,128)(2,1)S(1)} %get-tuple-element.372.refs_1_, ...), custom_call_target="tpu_custom_call" | custom-call | tf_op jit(solution)/shard_map/pallas_call | solution.py:131
  484.5 10.3 %shard_map.336 = (bf16[128,1536]{1,0:T(8,128)(2,1)S(1)}, bf16[128,1792]{1,0:T(8,128)(2,1)S(1)}, bf16[128,1792]{1,0:T(8,128)(2,1)S(1)}, f32[8,128]{1,0:T(8,128)S(1)}) custom-call(bf16[128,1536]{1,0:T(8,128)(2,1)S(1)} %get-tuple-element.368.refs_0_.refs_2_, f32[128,1792]{1,0:T(8,128)S(1)} %get-tuple-element.369.refs_1_, ...), custom_call_target="tpu_custom_call" | custom-call | tf_op jit(solution)/shard_map/pallas_call | solution.py:131
  497.5 10.2 %shard_map.337 = (bf16[128,1536]{1,0:T(8,128)(2,1)S(1)}, bf16[128,1792]{1,0:T(8,128)(2,1)S(1)}, bf16[128,1792]{1,0:T(8,128)(2,1)S(1)}, f32[8,128]{1,0:T(8,128)S(1)}) custom-call(bf16[128,1536]{1,0:T(8,128)(2,1)S(1)} %get-tuple-element.365.refs_0_.refs_3_, f32[128,1792]{1,0:T(8,128)S(1)} %get-tuple-element.366.refs_1_, ...), custom_call_target="tpu_custom_call" | custom-call | tf_op jit(solution)/shard_map/pallas_call | solution.py:131
  511.0 8.6 shard_map.339
  539.7 15.5 %shard_map.341 = (bf16[1536,3584]{1,0:T(8,128)(2,1)}, f32[8,128]{1,0:T(8,128)}) custom-call(bf16[128,1536]{1,0:T(8,128)(2,1)} %get-tuple-element.355.refs_0_, bf16[128,1536]{1,0:T(8,128)(2,1)} %copy-done.120, bf16[128,1536]{1,0:T(8,128)(2,1)} %collective-permute-done.54.refs_0_.refs_2_, bf16[128,1536]{1,0:T(8,128)(2,1)} %collective-permute-done.56.refs_0_.refs_3_, ...), custom_call_target="tpu_custom_call" | custom-call | flops 16911433728 | bytes 66060288 | tf_op jit(solution)/shard_map/pallas_call | solution.py:131
  599.0 10.8 %collective-permute-done.68.refs_6_ = bf16[128,1536]{1,0:T(8,128)(2,1)S(1)} collective-permute-done((bf16[128,1536]{1,0:T(8,128)(2,1)S(1)}, bf16[128,1536]{1,0:T(8,128)(2,1)S(1)}, u32[]{:S(2)}, u32[]{:S(2)}) %collective-permute-start.68) | collective-permute-done | bytes 393248 | tf_op jit(solution)/shard_map/ppermute | solution.py:39
  618.3 10.1 collective-permute-done.69.refs_1_
  637.5 11.3 %shard_map.347 = (f32[128,1536]{1,0:T(8,128)S(1)}, bf16[128,1536]{1,0:T(8,128)(2,1)}, bf16[256,1792]{1,0:T(8,128)(2,1)S(1)}, bf16[256,1792]{1,0:T(8,128)(2,1)S(1)}, f32[8,128]{1,0:T(8,128)S(1)}) custom-call(bf16[128,1536]{1,0:T(8,128)(2,1)S(1)} %copy-done.110, bf16[128,1536]{1,0:T(8,128)(2,1)S(1)} %collective-permute-done.69.refs_1_, ...), custom_call_target="tpu_custom_call" | custom-call | tf_op jit(solution)/shard_map/pallas_call | solution.py:131
  651.5 11.0 %shard_map.348 = (bf16[128,1536]{1,0:T(8,128)(2,1)}, bf16[128,1792]{1,0:T(8,128)(2,1)S(1)}, bf16[128,1792]{1,0:T(8,128)(2,1)S(1)}, f32[8,128]{1,0:T(8,128)S(1)}) custom-call(bf16[128,1536]{1,0:T(8,128)(2,1)S(1)} %collective-permute-done.71.refs_0_.refs_2_, f32[128,1792]{1,0:T(8,128)S(1)} %copy-done.88, f32[128,1792]{1,0:T(8,128)S(1)} %copy-done.90, ...), custom_call_target="tpu_custom_call" | custom-call | tf_op jit(solution)/shard_map/pallas_call | solution.py:131
  664.1 11.0 %shard_map.349 = (bf16[128,1536]{1,0:T(8,128)(2,1)}, bf16[128,1792]{1,0:T(8,128)(2,1)S(1)}, bf16[128,1792]{1,0:T(8,128)(2,1)S(1)}, f32[8,128]{1,0:T(8,128)S(1)}) custom-call(bf16[128,1536]{1,0:T(8,128)(2,1)S(1)} %collective-permute-done.73.refs_0_.refs_3_, f32[128,1792]{1,0:T(8,128)S(1)} %copy-done.84, f32[128,1792]{1,0:T(8,128)S(1)} %copy-done.86, ...), custom_call_target="tpu_custom_call" | custom-call | tf_op jit(solution)/shard_map/pallas_call | solution.py:131
  678.8 8.7 shard_map.350
  688.2 8.4 collective-permute-done.74.refs_6_
  706.2 15.7 %shard_map.352 = (bf16[1536,3584]{1,0:T(8,128)(2,1)}, f32[8,128]{1,0:T(8,128)}) custom-call(bf16[128,1536]{1,0:T(8,128)(2,1)} %get-tuple-element.325.refs_0_, bf16[128,1536]{1,0:T(8,128)(2,1)} %copy-done.119, bf16[128,1536]{1,0:T(8,128)(2,1)} %copy-done.116, bf16[128,1536]{1,0:T(8,128)(2,1)} %copy-done.117, bf16[256,1792]{1,0:T(8,128)(2,1)} %copy-done.148, ...), custom_call_target="tpu_custom_call" | custom-call | flops 16911433728 | bytes 66060288 | tf_op jit(solution)/shard_map/pallas_call | solution.py:131
  752.7 24.1 %collective-permute-done.83.refs_7_.refs_2_ = bf16[48,3584]{1,0:T(8,128)(2,1)S(1)} collective-permute-done((bf16[48,3584]{1,0:T(8,128)(2,1)}, bf16[48,3584]{1,0:T(8,128)(2,1)S(1)}, u32[]{:S(2)}, u32[]{:S(2)}) %collective-permute-start.83) | collective-permute-done | bytes 344096 | tf_op jit(solution)/shard_map/ppermute | solution.py:48
  777.2 8.5 shard_map.357
  785.7 22.8 %collective-permute-done.85.refs_9_.refs_4_ = bf16[48,3584]{1,0:T(8,128)(2,1)S(1)} collective-permute-done((bf16[48,3584]{1,0:T(8,128)(2,1)}, bf16[48,3584]{1,0:T(8,128)(2,1)S(1)}, u32[]{:S(2)}, u32[]{:S(2)}) %collective-permute-start.85) | collective-permute-done | bytes 344096 | tf_op jit(solution)/shard_map/ppermute | solution.py:48
  826.3 47.3 %collective-permute-done.95 = f32[10,48]{1,0:T(8,128)S(1)} collective-permute-done((f32[10,48]{1,0:T(8,128)S(1)}, f32[10,48]{1,0:T(8,128)S(1)}, u32[]{:S(2)}, u32[]{:S(2)}) %collective-permute-start.95) | collective-permute-done | bytes 1952 | tf_op jit(solution)/shard_map/ppermute | solution.py:48
  922.0 28.8 %collective-permute-done.97.refs_3_ = bf16[2,48,768]{2,1,0:T(8,128)(2,1)S(1)} collective-permute-done((bf16[2,48,768]{2,1,0:T(8,128)(2,1)S(1)}, bf16[2,48,768]{2,1,0:T(8,128)(2,1)S(1)}, u32[]{:S(2)}, u32[]{:S(2)}) %collective-permute-start.97) | collective-permute-done | bytes 147488 | tf_op jit(solution)/shard_map/ppermute | solution.py:39
  (771 shorter events, 501.7 us)
Async XLA Ops:
  7.2 236.8 %all-gather.9.cloned.1.call-start = ((), (), s32[]{:S(2)}) async-start(), calls=%async_computation.5 | async-start | bytes 6193152 | tf_op jit(solution)/shard_map/all_gather | solution.py:338
  11.0 233.0 %all-gather.7.cloned.1.call-start = ((), (), s32[]{:S(2)}) async-start(), calls=%async_computation.4 | async-start | bytes 12386304 | tf_op jit(solution)/shard_map/all_gather | solution.py:338
  35.4 47.7 %collective-permute-start.9 = (bf16[1,48,3584]{2,1,0:T(8,128)(2,1)S(1)}, bf16[1,48,3584]{2,1,0:T(8,128)(2,1)S(1)}, u32[]{:S(2)}, u32[]{:S(2)}) collective-permute-start(bf16[1,48,3584]{2,1,0:T(8,128)(2,1)S(1)} %get-tuple-element.552), channel_id=1, source_target_pairs={{0,1},{1,0},{2,3},{3,2},{4,5},{5,4},{6,7},{7,6},{8,9},{9,8},{10,11... | collective-permute-start | bytes 1032200 | tf_op jit(solution)/shard_map/ppermute | solution.py:48
  43.5 47.5 %collective-permute-start.11 = (bf16[1,48,3584]{2,1,0:T(8,128)(2,1)S(1)}, bf16[1,48,3584]{2,1,0:T(8,128)(2,1)S(1)}, u32[]{:S(2)}, u32[]{:S(2)}) collective-permute-start(bf16[1,48,3584]{2,1,0:T(8,128)(2,1)S(1)} %get-tuple-element.550), channel_id=1, source_target_pairs={{0,3},{1,2},{2,1},{3,0},{4,7},{5,6},{6,5},{7,4},{8,11},{9,10},{10,... | collective-permute-start | bytes 1032200 | tf_op jit(solution)/shard_map/ppermute | solution.py:48
  92.3 244.2 %all-gather.11.cloned.1.call-start = ((), (), s32[]{:S(2)}) async-start(), calls=%async_computation.6 | async-start | bytes 2949120 | tf_op jit(solution)/shard_map/all_gather | solution.py:1115
  122.0 52.3 %collective-permute-start.32 = (bf16[8,48,768]{2,1,0:T(8,128)(2,1)}, bf16[8,48,768]{2,1,0:T(8,128)(2,1)S(1)}, u32[]{:S(2)}, u32[]{:S(2)}) collective-permute-start(bf16[8,48,768]{2,1,0:T(8,128)(2,1)} %get-tuple-element.301.refs_2_), channel_id=1, source_target_pairs={{0,3},{1,2},{2,1},{3,0},{4,7},{5,6},{6,5},{7,4},{8,11},{9,10},{10,... | collective-permute-start | bytes 1769480 | tf_op jit(solution)/shard_map/ppermute | solution.py:48
  126.2 48.1 %collective-permute-start.28 = (bf16[128,1536]{1,0:T(8,128)(2,1)S(1)}, bf16[128,1536]{1,0:T(8,128)(2,1)S(1)}, u32[]{:S(2)}, u32[]{:S(2)}) collective-permute-start(bf16[128,1536]{1,0:T(8,128)(2,1)S(1)} %get-tuple-element.307.refs_0_), channel_id=1, source_target_pairs={{0,8},{4,12},{8,0},{12,4},{16,24},{20,28},{24,16},{28,20},{1,9},{5... | collective-permute-start | bytes 1179656 | tf_op jit(solution)/shard_map/ppermute | solution.py:39
  127.9 46.4 %collective-permute-start.30 = (bf16[128,1536]{1,0:T(8,128)(2,1)S(1)}, bf16[128,1536]{1,0:T(8,128)(2,1)S(1)}, u32[]{:S(2)}, u32[]{:S(2)}) collective-permute-start(bf16[128,1536]{1,0:T(8,128)(2,1)S(1)} %get-tuple-element.307.refs_0_), channel_id=1, source_target_pairs={{0,24},{4,28},{8,16},{12,20},{16,8},{20,12},{24,0},{28,4},{1,25},{... | collective-permute-start | bytes 1179656 | tf_op jit(solution)/shard_map/ppermute | solution.py:39
  175.4 187.6 %all-gather.15.cloned.1.call-start = ((), (), s32[]{:S(2)}) async-start(), calls=%async_computation.8 | async-start | bytes 6193152 | tf_op jit(solution)/shard_map/all_gather | solution.py:338
  214.1 174.0 %all-gather.13.cloned.1.call-start = ((), (), s32[]{:S(2)}) async-start(), calls=%async_computation.7 | async-start | bytes 12386304 | tf_op jit(solution)/shard_map/all_gather | solution.py:338
  214.7 232.2 %all-gather.17.cloned.1.call-start = ((), (), s32[]{:S(2)}) async-start(), calls=%async_computation.9 | async-start | bytes 1966080 | tf_op jit(solution)/shard_map/all_gather | solution.py:1155
  215.0 47.8 %collective-permute-start.40 = (bf16[128,1536]{1,0:T(8,128)(2,1)}, bf16[128,1536]{1,0:T(8,128)(2,1)S(1)}, u32[]{:S(2)}, u32[]{:S(2)}) collective-permute-start(bf16[128,1536]{1,0:T(8,128)(2,1)} %get-tuple-element.325.refs_0_), channel_id=1, source_target_pairs={{0,2},{1,3},{2,0},{3,1},{4,6},{5,7},{6,4},{7,5},{8,10},{9,11},{10,... | collective-permute-start | bytes 1179656 | tf_op jit(solution)/shard_map/ppermute | solution.py:48
  217.9 52.9 %collective-permute-start.42 = (bf16[128,1536]{1,0:T(8,128)(2,1)}, bf16[128,1536]{1,0:T(8,128)(2,1)S(1)}, u32[]{:S(2)}, u32[]{:S(2)}) collective-permute-start(bf16[128,1536]{1,0:T(8,128)(2,1)} %get-tuple-element.325.refs_0_), channel_id=1, source_target_pairs={{0,3},{1,2},{2,1},{3,0},{4,7},{5,6},{6,5},{7,4},{8,11},{9,10},{10,... | collective-permute-start | bytes 1179656 | tf_op jit(solution)/shard_map/ppermute | solution.py:48
  350.4 371.5 %reduce-scatter.5.cloned.1.call-start = ((), (), s32[]{:S(2)}) async-start(), calls=%async_computation.10 | async-start | bytes 12386304 | tf_op jit(solution)/shard_map/reduce_scatter | solution.py:454
  399.9 48.5 %collective-permute-start.54 = (bf16[128,1536]{1,0:T(8,128)(2,1)}, bf16[128,1536]{1,0:T(8,128)(2,1)}, u32[]{:S(2)}, u32[]{:S(2)}) collective-permute-start(bf16[128,1536]{1,0:T(8,128)(2,1)} %get-tuple-element.355.refs_0_), channel_id=1, source_target_pairs={{0,2},{1,3},{2,0},{3,1},{4,6},{5,7},{6,4},{7,5},{8,10},{9,11},{10,... | collective-permute-start | bytes 1179656 | tf_op jit(solution)/shard_map/ppermute | solution.py:48
  402.4 60.7 %collective-permute-start.56 = (bf16[128,1536]{1,0:T(8,128)(2,1)}, bf16[128,1536]{1,0:T(8,128)(2,1)}, u32[]{:S(2)}, u32[]{:S(2)}) collective-permute-start(bf16[128,1536]{1,0:T(8,128)(2,1)} %get-tuple-element.355.refs_0_), channel_id=1, source_target_pairs={{0,3},{1,2},{2,1},{3,0},{4,7},{5,6},{6,5},{7,4},{8,11},{9,10},{10,... | collective-permute-start | bytes 1179656 | tf_op jit(solution)/shard_map/ppermute | solution.py:48
  444.5 63.3 %collective-permute-start.53 = (bf16[128,1536]{1,0:T(8,128)(2,1)}, bf16[128,1536]{1,0:T(8,128)(2,1)}, u32[]{:S(2)}, u32[]{:S(2)}) collective-permute-start(bf16[128,1536]{1,0:T(8,128)(2,1)} %get-tuple-element.358), channel_id=1, source_target_pairs={{0,1},{1,0},{2,3},{3,2},{4,5},{5,4},{6,7},{7,6},{8,9},{9,8},{10,11... | collective-permute-start | bytes 1179656 | tf_op jit(solution)/shard_map/ppermute | solution.py:48
  462.0 46.5 %collective-permute-start.55 = (bf16[128,1536]{1,0:T(8,128)(2,1)S(1)}, bf16[128,1536]{1,0:T(8,128)(2,1)S(1)}, u32[]{:S(2)}, u32[]{:S(2)}) collective-permute-start(bf16[128,1536]{1,0:T(8,128)(2,1)S(1)} %get-tuple-element.362), channel_id=1, source_target_pairs={{0,2},{1,3},{2,0},{3,1},{4,6},{5,7},{6,4},{7,5},{8,10},{9,11},{10,... | collective-permute-start | bytes 1179656 | tf_op jit(solution)/shard_map/ppermute | solution.py:48
  559.8 331.5 %reduce-scatter.9.cloned.1.call-start = ((), (), s32[]{:S(2)}) async-start(), calls=%async_computation.12 | async-start | bytes 6193152 | tf_op jit(solution)/shard_map/reduce_scatter | solution.py:454
  560.6 344.0 %reduce-scatter.7.cloned.1.call-start = ((), (), s32[]{:S(2)}) async-start(), calls=%async_computation.11 | async-start | bytes 2949120 | tf_op jit(solution)/shard_map/reduce_scatter | solution.py:1190
  701.0 253.8 %reduce-scatter.11.cloned.1.call-start = ((), (), s32[]{:S(2)}) async-start(), calls=%async_computation.13 | async-start | bytes 12386304 | tf_op jit(solution)/shard_map/reduce_scatter | solution.py:454
  748.8 59.6 %collective-permute-start.85 = (bf16[48,3584]{1,0:T(8,128)(2,1)}, bf16[48,3584]{1,0:T(8,128)(2,1)S(1)}, u32[]{:S(2)}, u32[]{:S(2)}) collective-permute-start(bf16[48,3584]{1,0:T(8,128)(2,1)} %get-tuple-element.462), channel_id=1, source_target_pairs={{0,3},{1,2},{2,1},{3,0},{4,7},{5,6},{6,5},{7,4},{8,11},{9,10},{10,... | collective-permute-start | bytes 1032200 | tf_op jit(solution)/shard_map/ppermute | solution.py:48
  750.8 57.6 %collective-permute-start.80 = (bf16[128,1536]{1,0:T(8,128)(2,1)S(1)}, bf16[128,1536]{1,0:T(8,128)(2,1)S(1)}, u32[]{:S(2)}, u32[]{:S(2)}) collective-permute-start(bf16[128,1536]{1,0:T(8,128)(2,1)S(1)} %get-tuple-element.457), channel_id=1, source_target_pairs={{0,8},{4,12},{8,0},{12,4},{16,24},{20,28},{24,16},{28,20},{1,9},{5... | collective-permute-start | bytes 1179656 | tf_op jit(solution)/shard_map/ppermute | solution.py:39
  752.4 56.1 %collective-permute-start.81 = (bf16[128,1536]{1,0:T(8,128)(2,1)S(1)}, bf16[128,1536]{1,0:T(8,128)(2,1)S(1)}, u32[]{:S(2)}, u32[]{:S(2)}) collective-permute-start(bf16[128,1536]{1,0:T(8,128)(2,1)S(1)} %get-tuple-element.458), channel_id=1, source_target_pairs={{0,16},{4,20},{8,24},{12,28},{16,0},{20,4},{24,8},{28,12},{1,17},{... | collective-permute-start | bytes 1179656 | tf_op jit(solution)/shard_map/ppermute | solution.py:39
  819.0 79.4 %collective-permute-start.86 = (bf16[8,48,768]{2,1,0:T(8,128)(2,1)}, bf16[8,48,768]{2,1,0:T(8,128)(2,1)S(1)}, u32[]{:S(2)}, u32[]{:S(2)}) collective-permute-start(bf16[8,48,768]{2,1,0:T(8,128)(2,1)} %get-tuple-element.473), channel_id=1, source_target_pairs={{0,1},{1,0},{2,3},{3,2},{4,5},{5,4},{6,7},{7,6},{8,9},{9,8},{10,11... | collective-permute-start | bytes 1769480 | tf_op jit(solution)/shard_map/ppermute | solution.py:48
  819.0 79.4 %collective-permute-start.87 = (bf16[8,48,768]{2,1,0:T(8,128)(2,1)}, bf16[8,48,768]{2,1,0:T(8,128)(2,1)}, u32[]{:S(2)}, u32[]{:S(2)}) collective-permute-start(bf16[8,48,768]{2,1,0:T(8,128)(2,1)} %get-tuple-element.474), channel_id=1, source_target_pairs={{0,2},{1,3},{2,0},{3,1},{4,6},{5,7},{6,4},{7,5},{8,10},{9,11},{10,... | collective-permute-start | bytes 1769480 | tf_op jit(solution)/shard_map/ppermute | solution.py:48
  821.0 77.4 %collective-permute-start.88 = (bf16[8,48,768]{2,1,0:T(8,128)(2,1)}, bf16[8,48,768]{2,1,0:T(8,128)(2,1)}, u32[]{:S(2)}, u32[]{:S(2)}) collective-permute-start(bf16[8,48,768]{2,1,0:T(8,128)(2,1)} %get-tuple-element.475), channel_id=1, source_target_pairs={{0,3},{1,2},{2,1},{3,0},{4,7},{5,6},{6,5},{7,4},{8,11},{9,10},{10,... | collective-permute-start | bytes 1769480 | tf_op jit(solution)/shard_map/ppermute | solution.py:48
  822.9 50.7 %collective-permute-start.95 = (f32[10,48]{1,0:T(8,128)S(1)}, f32[10,48]{1,0:T(8,128)S(1)}, u32[]{:S(2)}, u32[]{:S(2)}) collective-permute-start(f32[10,48]{1,0:T(8,128)S(1)} %bitcast.136), channel_id=1, source_target_pairs={{0,3},{1,2},{2,1},{3,0},{4,7},{5,6},{6,5},{7,4},{8,11},{9,10},{10,... | collective-permute-start | bytes 5768 | tf_op jit(solution)/shard_map/ppermute | solution.py:48
  823.5 67.7 %collective-permute-start.94 = (f32[10,48]{1,0:T(8,128)S(1)}, f32[10,48]{1,0:T(8,128)S(1)}, u32[]{:S(2)}, u32[]{:S(2)}) collective-permute-start(f32[10,48]{1,0:T(8,128)S(1)} %bitcast.134), channel_id=1, source_target_pairs={{0,2},{1,3},{2,0},{3,1},{4,6},{5,7},{6,4},{7,5},{8,10},{9,11},{10,... | collective-permute-start | bytes 5768 | tf_op jit(solution)/shard_map/ppermute | solution.py:48
  914.3 47.5 %collective-permute-start.104 = (bf16[224,1536]{1,0:T(8,128)(2,1)}, bf16[224,1536]{1,0:T(8,128)(2,1)S(1)}, u32[]{:S(2)}, u32[]{:S(2)}) collective-permute-start(bf16[224,1536]{1,0:T(8,128)(2,1)} %get-tuple-element.496), channel_id=1, source_target_pairs={{0,8},{4,12},{8,0},{12,4},{16,24},{20,28},{24,16},{28,20},{1,9},{5... | collective-permute-start | bytes 2064392 | tf_op jit(solution)/shard_map/ppermute | solution.py:39
  915.9 49.9 %collective-permute-start.105 = (bf16[224,1536]{1,0:T(8,128)(2,1)}, bf16[224,1536]{1,0:T(8,128)(2,1)}, u32[]{:S(2)}, u32[]{:S(2)}) collective-permute-start(bf16[224,1536]{1,0:T(8,128)(2,1)} %get-tuple-element.497), channel_id=1, source_target_pairs={{0,16},{4,20},{8,24},{12,28},{16,0},{20,4},{24,8},{28,12},{1,17},{... | collective-permute-start | bytes 2064392 | tf_op jit(solution)/shard_map/ppermute | solution.py:39
  917.4 50.1 %collective-permute-start.106 = (bf16[224,1536]{1,0:T(8,128)(2,1)}, bf16[224,1536]{1,0:T(8,128)(2,1)}, u32[]{:S(2)}, u32[]{:S(2)}) collective-permute-start(bf16[224,1536]{1,0:T(8,128)(2,1)} %get-tuple-element.498), channel_id=1, source_target_pairs={{0,24},{4,28},{8,16},{12,20},{16,8},{20,12},{24,0},{28,4},{1,25},{... | collective-permute-start | bytes 2064392 | tf_op jit(solution)/shard_map/ppermute | solution.py:39
  (302 other events, 3812.6 us)
Sparse Core Ops, SparseCore 0:
  11.1 44.6 all-gather.8
  92.4 86.9 all-gather.6
  181.5 58.7 all-gather.10
  242.0 45.6 all-gather.14
  290.0 89.6 all-gather.12
  381.1 49.8 all-gather.16
  559.9 94.1 reduce-scatter.4
  657.6 73.5 reduce-scatter.8
  734.2 74.7 reduce-scatter.6
  812.9 83.5 reduce-scatter.10

commit v6 on v3

--- a/solution.py
+++ b/solution.py
@@ -137,7 +137,7 @@
         input_output_aliases=aliases,
         compiler_params=pltpu.CompilerParams(
             vmem_limit_bytes=56 << 20
-            if cost[0]
+            if cost[0] or aliases and not grid
             else min(vmem_of(operands, in_specs, out_shape, out_specs, scratch, grid), 60 << 20)
         ),
         cost_estimate=pl.CostEstimate(
@@ -1107,7 +1107,6 @@
     feeds[0] = (gather_rows(feed_part), down_rows)
     mixes[0] = assemble_mix(mix_pieces, wide)
     later_mix = [None, None, fsdp_swap(later_piece, 2)] if rings > 2 else [None, None]
-    later_feed = swap_feed(later_feed)
 
     kept = []
     for layer in range(LAYERS):
@@ -1119,32 +1118,39 @@
             sums, flow_low = pair_sum(even, odd, (), [cotangent])
             flow_low = gather_fsdp(flow_low)
             middle, normed_two = finish(stream, sums, gain_rows[layer, 1])
-            flow_low = join_blocks(flow_low)
         else:
-            (sums,) = pair_sum(even, odd, later_feed[1:])
-            middle, normed_two, later_piece, down_packed = finish(
+            (sums,) = pair_sum(even, odd)
+            middle, normed_two, later_piece, down_packed, later_feed = finish(
                 stream,
                 sums,
                 gain_rows[layer, 1],
                 later_mix[2:],
-                (later_piece, pack_down(down_weight, 1)),
+                (later_piece, pack_down(down_weight, 1), later_feed),
             )
         two_blocks = gather_fsdp(normed_two)
         if not last:
             later_mix[0] = later_piece
             later_mix[1] = fsdp_swap(later_piece, 1)
-            feeds[1] = (gather_rows(assemble_feed(later_feed)), gather_rows(down_packed))
+            later_down = gather_rows(down_packed)
+            later_feed = swap_feed(later_feed)
         sums, values = [], []
         for number, group in enumerate(groups_of(two_blocks)):
             outs, saved = feed_forward(group, *feeds[layer], number == 0)
             sums += outs
             values.append(saved)
+        if last:
+            flow_low = join_blocks(flow_low)
         kept.append((stream, middle, gathered, projected, two_blocks, values))
         sums = return_sums(sums)
         if not last:
-            stream, normed, later_piece = finish(
-                middle, sums, gain_rows[layer + 1, 0], later_mix[1:2], [later_piece]
+            stream, normed, later_piece, later_feed = finish(
+                middle,
+                sums,
+                gain_rows[layer + 1, 0],
+                later_mix[1:2],
+                [later_piece, assemble_feed(later_feed)],
             )
+            feeds[1] = gather_rows(later_feed), later_down
             blocks = send_seq(normed)
             later_mix += [fsdp_swap(later_piece, by) for by in range(3, rings)]
             blocks = stack_pairs(blocks)
@@ -1210,10 +1216,10 @@
             flow_low = gather_fsdp(low_flow)
             later_mix, later_feed, later_down = mix_part, feed_part, down_part
     new[1] = feed_adam(later_feed, states[1], 1, new[1])
-    even, odd = split_down(down_part, mix_part[1:3])
+    even, odd = split_down(down_part, mix_part[1:])
     odd = seq_swap(odd, 1)
     new[2] = down_adam(later_down, states[2], 1, new[2])
-    (down_part,) = pair_sum(even, odd, mix_part[3:])
+    (down_part,) = pair_sum(even, odd)
     gain_grad, tap_grad = vector_gradients(
         jnp.stack(gain_grads), jnp.stack(tap_grads), gain_weight.shape[-1]
     )

time: 1010 us -> 1020 us (level)
  local copies, waits for them, and re-layouts: 148 us -> 124 us
  Pallas kernels: 253 us -> 272 us
  waiting for transfers between devices: 441 us -> 458 us
    unnamed x491 -> x485, local copies, waits for them, and re-layouts: 144 us -> 117 us
    pallas_call x63, Pallas kernels: 253 us -> 272 us  [ordered_call(): pl.pallas_call(marked, in_specs=list(in_specs) + [anywhere], out_specs=li...]
    all_gather x4, waiting for transfers between devices: 0.01 us -> 14.5 us  [gather_rows(): lax.all_gather(part.reshape(-1, part.shape[-1]), 'seq', axis=0, tiled=True)]
  transfers between devices with their start and end apart: 126 -> 126, of which waited for: 62 -> 62; matrix products, arithmetic and copies ran while one was open for 1% -> 1% of each run, Pallas kernels for 25% -> 26%
where the time goes in v6:
time: 1020 us; the launch traced here: 1010 us
  waiting for transfers between devices  458 us (45%)
  Pallas kernels  272 us (27%)
  starting transfers between devices  133 us (13%)
  local copies, waits for them, and re-layouts  124 us (12%)
  between operations  16.7 us (2%)
    ppermute x54, waiting for transfers between devices, fsdp_swap(): return lax.ppermute(array, 'fsdp', [(i, i ^ by) for i in range(count)])  303 us
    pallas_call x63, Pallas kernels, ordered_call(): pl.pallas_call(marked, in_specs=list(in_specs) + [anywhere], out_specs=li...  272 us
    ppermute x65, waiting for transfers between devices, seq_swap(): return lax.ppermute(array, 'seq', [(i, i ^ by) for i in range(count)])  139 us
    unnamed x485, local copies, waits for them, and re-layouts  117 us
    ppermute x54, starting transfers between devices, fsdp_swap(): return lax.ppermute(array, 'fsdp', [(i, i ^ by) for i in range(count)])  70.3 us
    ppermute x65, starting transfers between devices, seq_swap(): return lax.ppermute(array, 'seq', [(i, i ^ by) for i in range(count)])  62 us
  transfers between devices with their start and end apart: 126, of which 62 were waited for; matrix products, arithmetic and copies ran while one was open for 1% of the time, Pallas kernels for 26%

profile of v6, /device:TPU:8, one launch (start us, length us, event | category | flops | bytes accessed | tf_op | source)
XLA Modules:
  0.0 1006.5 jit_solution(12850963821784927927)
XLA Ops:
  43.7 10.8 %collective-permute-done.7.refs_3_ = bf16[1,48,3584]{2,1,0:T(8,128)(2,1)S(1)} collective-permute-done((bf16[1,48,3584]{2,1,0:T(8,128)(2,1)S(1)}, bf16[1,48,3584]{2,1,0:T(8,128)(2,1)S(1)}, u32[]{:S(2)}, u32[]{:S(2)}) %collective-permute-start.7) | collective-permute-done | bytes 344096 | tf_op jit(solution)/shard_map/ppermute | solution.py:48
  101.1 22.0 %collective-permute-done.28.refs_4_ = bf16[8,48,768]{2,1,0:T(8,128)(2,1)S(1)} collective-permute-done((bf16[8,48,768]{2,1,0:T(8,128)(2,1)S(1)}, bf16[8,48,768]{2,1,0:T(8,128)(2,1)S(1)}, u32[]{:S(2)}, u32[]{:S(2)}) %collective-permute-start.28) | collective-permute-done | bytes 589856 | tf_op jit(solution)/shard_map/ppermute | solution.py:48
  123.1 14.9 %collective-permute-done.29.refs_5_ = bf16[8,48,768]{2,1,0:T(8,128)(2,1)S(1)} collective-permute-done((bf16[8,48,768]{2,1,0:T(8,128)(2,1)S(1)}, bf16[8,48,768]{2,1,0:T(8,128)(2,1)S(1)}, u32[]{:S(2)}, u32[]{:S(2)}) %collective-permute-start.29) | collective-permute-done | bytes 589856 | tf_op jit(solution)/shard_map/ppermute | solution.py:48
  160.0 17.5 %collective-permute-done.35.refs_6_.refs_4_ = bf16[8,48,768]{2,1,0:T(8,128)(2,1)S(1)} collective-permute-done((bf16[8,48,768]{2,1,0:T(8,128)(2,1)S(1)}, bf16[8,48,768]{2,1,0:T(8,128)(2,1)S(1)}, u32[]{:S(2)}, u32[]{:S(2)}) %collective-permute-start.35) | collective-permute-done | bytes 589856 | tf_op jit(solution)/shard_map/ppermute | solution.py:48
  208.9 14.5 %all-gather.5.cloned.1.call-done.refs_2_.refs_3_.refs_1_.refs_4_.refs_5_ = bf16[1536,3584]{1,0:T(8,128)(2,1)} async-done(((bf16[192,3584]{1,0:T(8,128)(2,1)}), bf16[1536,3584]{1,0:T(8,128)(2,1)}) %all-gather.5.cloned.1.call-update) | async-done | bytes 11010064 | tf_op jit(solution)/shard_map/all_gather | solution.py:336
  256.4 41.2 %collective-permute-done.45.refs_4_ = bf16[1,48,3584]{2,1,0:T(8,128)(2,1)S(1)} collective-permute-done((bf16[1,48,3584]{2,1,0:T(8,128)(2,1)S(1)}, bf16[1,48,3584]{2,1,0:T(8,128)(2,1)S(1)}, u32[]{:S(2)}, u32[]{:S(2)}) %collective-permute-start.45) | collective-permute-done | bytes 344096 | tf_op jit(solution)/shard_map/ppermute | solution.py:48
  308.8 10.9 %collective-permute-done.46.refs_1_ = bf16[128,1536]{1,0:T(8,128)(2,1)S(1)} collective-permute-done((bf16[128,1536]{1,0:T(8,128)(2,1)}, bf16[128,1536]{1,0:T(8,128)(2,1)S(1)}, u32[]{:S(2)}, u32[]{:S(2)}) %collective-permute-start.46) | collective-permute-done | bytes 393248 | tf_op jit(solution)/shard_map/ppermute | solution.py:39
  324.9 9.8 collective-permute-done.48.refs_3_
  339.2 14.2 %collective-permute-done.50.refs_5_ = bf16[8,48,768]{2,1,0:T(8,128)(2,1)S(1)} collective-permute-done((bf16[8,48,768]{2,1,0:T(8,128)(2,1)S(1)}, bf16[8,48,768]{2,1,0:T(8,128)(2,1)S(1)}, u32[]{:S(2)}, u32[]{:S(2)}) %collective-permute-start.50) | collective-permute-done | bytes 589856 | tf_op jit(solution)/shard_map/ppermute | solution.py:48
  387.6 9.5 collective-permute-done.53.refs_3_
  407.3 10.8 %collective-permute-done.55.refs_1_ = bf16[128,1536]{1,0:T(8,128)(2,1)S(1)} collective-permute-done((bf16[128,1536]{1,0:T(8,128)(2,1)}, bf16[128,1536]{1,0:T(8,128)(2,1)S(1)}, u32[]{:S(2)}, u32[]{:S(2)}) %collective-permute-start.55) | collective-permute-done | bytes 393248 | tf_op jit(solution)/shard_map/ppermute | solution.py:48
  427.6 9.7 shard_map.331
  447.2 9.7 collective-permute-done.59.refs_0_.refs_3_
  465.6 15.5 %collective-permute-done.62.refs_2_ = bf16[128,1536]{1,0:T(8,128)(2,1)} collective-permute-done((bf16[128,1536]{1,0:T(8,128)(2,1)S(1)}, bf16[128,1536]{1,0:T(8,128)(2,1)}, u32[]{:S(2)}, u32[]{:S(2)}) %collective-permute-start.62) | collective-permute-done | bytes 393248 | tf_op jit(solution)/shard_map/ppermute | solution.py:48
  481.1 9.5 collective-permute-done.63.refs_3_
  491.9 11.4 %shard_map.335 = (f32[128,1536]{1,0:T(8,128)S(1)}, bf16[128,1536]{1,0:T(8,128)(2,1)}, bf16[256,1792]{1,0:T(8,128)(2,1)S(1)}, bf16[256,1792]{1,0:T(8,128)(2,1)S(1)}, f32[8,128]{1,0:T(8,128)S(1)}) custom-call(bf16[128,1536]{1,0:T(8,128)(2,1)S(1)} %get-tuple-element.389.refs_0_, bf16[128,1536]{1,0:T(8,128)(2,1)S(1)} %get-tuple-element.390.refs_1_, ...), custom_call_target="tpu_custom_call" | custom-call | tf_op jit(solution)/shard_map/pallas_call | solution.py:131
  503.4 11.0 %shard_map.336 = (bf16[128,1536]{1,0:T(8,128)(2,1)}, bf16[128,1792]{1,0:T(8,128)(2,1)S(1)}, bf16[128,1792]{1,0:T(8,128)(2,1)S(1)}, f32[8,128]{1,0:T(8,128)S(1)}) custom-call(bf16[128,1536]{1,0:T(8,128)(2,1)S(1)} %get-tuple-element.386.refs_0_.refs_2_, f32[128,1792]{1,0:T(8,128)S(1)} %get-tuple-element.387.refs_1_, ...), custom_call_target="tpu_custom_call" | custom-call | tf_op jit(solution)/shard_map/pallas_call | solution.py:131
  518.1 11.0 %shard_map.337 = (bf16[128,1536]{1,0:T(8,128)(2,1)}, bf16[128,1792]{1,0:T(8,128)(2,1)S(1)}, bf16[128,1792]{1,0:T(8,128)(2,1)S(1)}, f32[8,128]{1,0:T(8,128)S(1)}) custom-call(bf16[128,1536]{1,0:T(8,128)(2,1)S(1)} %get-tuple-element.383.refs_0_.refs_3_, f32[128,1792]{1,0:T(8,128)S(1)} %get-tuple-element.384.refs_1_, ...), custom_call_target="tpu_custom_call" | custom-call | tf_op jit(solution)/shard_map/pallas_call | solution.py:131
  556.7 15.4 %shard_map.341 = (bf16[1536,3584]{1,0:T(8,128)(2,1)}, f32[8,128]{1,0:T(8,128)}) custom-call(bf16[128,1536]{1,0:T(8,128)(2,1)} %get-tuple-element.371.refs_0_, bf16[128,1536]{1,0:T(8,128)(2,1)} %copy-done.130, bf16[128,1536]{1,0:T(8,128)(2,1)} %collective-permute-done.57.refs_0_.refs_2_, bf16[128,1536]{1,0:T(8,128)(2,1)} %collective-permute-done.59.refs_0_.refs_3_, ...), custom_call_target="tpu_custom_call" | custom-call | flops 16911433728 | bytes 66060288 | tf_op jit(solution)/shard_map/pallas_call | solution.py:131
  616.4 12.0 %collective-permute-done.74.refs_6_ = bf16[128,1536]{1,0:T(8,128)(2,1)S(1)} collective-permute-done((bf16[128,1536]{1,0:T(8,128)(2,1)S(1)}, bf16[128,1536]{1,0:T(8,128)(2,1)S(1)}, u32[]{:S(2)}, u32[]{:S(2)}) %collective-permute-start.74) | collective-permute-done | bytes 393248 | tf_op jit(solution)/shard_map/ppermute | solution.py:39
  636.6 9.9 collective-permute-done.75.refs_1_
  656.2 11.6 %shard_map.347 = (f32[128,1536]{1,0:T(8,128)S(1)}, bf16[128,1536]{1,0:T(8,128)(2,1)}, bf16[256,1792]{1,0:T(8,128)(2,1)S(1)}, bf16[256,1792]{1,0:T(8,128)(2,1)S(1)}, f32[8,128]{1,0:T(8,128)S(1)}) custom-call(bf16[128,1536]{1,0:T(8,128)(2,1)S(1)} %copy-done.115, bf16[128,1536]{1,0:T(8,128)(2,1)S(1)} %collective-permute-done.75.refs_1_, ...), custom_call_target="tpu_custom_call" | custom-call | tf_op jit(solution)/shard_map/pallas_call | solution.py:131
  670.0 11.0 %shard_map.348 = (bf16[128,1536]{1,0:T(8,128)(2,1)}, bf16[128,1792]{1,0:T(8,128)(2,1)S(1)}, bf16[128,1792]{1,0:T(8,128)(2,1)S(1)}, f32[8,128]{1,0:T(8,128)S(1)}) custom-call(bf16[128,1536]{1,0:T(8,128)(2,1)S(1)} %collective-permute-done.77.refs_0_.refs_2_, f32[128,1792]{1,0:T(8,128)S(1)} %copy-done.94, f32[128,1792]{1,0:T(8,128)S(1)} %copy-done.96, ...), custom_call_target="tpu_custom_call" | custom-call | tf_op jit(solution)/shard_map/pallas_call | solution.py:131
  683.3 11.1 %shard_map.349 = (bf16[128,1536]{1,0:T(8,128)(2,1)}, bf16[128,1792]{1,0:T(8,128)(2,1)S(1)}, bf16[128,1792]{1,0:T(8,128)(2,1)S(1)}, f32[8,128]{1,0:T(8,128)S(1)}) custom-call(bf16[128,1536]{1,0:T(8,128)(2,1)S(1)} %collective-permute-done.79.refs_0_.refs_3_, f32[128,1792]{1,0:T(8,128)S(1)} %copy-done.90, f32[128,1792]{1,0:T(8,128)S(1)} %copy-done.92, ...), custom_call_target="tpu_custom_call" | custom-call | tf_op jit(solution)/shard_map/pallas_call | solution.py:131
  697.3 9.1 shard_map.350
  724.3 16.0 %shard_map.352 = (bf16[1536,3584]{1,0:T(8,128)(2,1)}, f32[8,128]{1,0:T(8,128)}) custom-call(bf16[128,1536]{1,0:T(8,128)(2,1)} %get-tuple-element.339.refs_0_, bf16[128,1536]{1,0:T(8,128)(2,1)} %copy-done.129, bf16[128,1536]{1,0:T(8,128)(2,1)} %copy-done.126, bf16[128,1536]{1,0:T(8,128)(2,1)} %copy-done.127, bf16[256,1792]{1,0:T(8,128)(2,1)} %copy-done.164, ...), custom_call_target="tpu_custom_call" | custom-call | flops 16911433728 | bytes 66060288 | tf_op jit(solution)/shard_map/pallas_call | solution.py:131
  772.5 10.4 %collective-permute-done.87.refs_2_ = bf16[48,3584]{1,0:T(8,128)(2,1)S(1)} collective-permute-done((bf16[48,3584]{1,0:T(8,128)(2,1)S(1)}, bf16[48,3584]{1,0:T(8,128)(2,1)S(1)}, u32[]{:S(2)}, u32[]{:S(2)}) %collective-permute-start.87) | collective-permute-done | bytes 344096 | tf_op jit(solution)/shard_map/ppermute | solution.py:48
  815.3 10.2 %collective-permute-done.94.refs_8_ = bf16[8,48,768]{2,1,0:T(8,128)(2,1)S(1)} collective-permute-done((bf16[8,48,768]{2,1,0:T(8,128)(2,1)}, bf16[8,48,768]{2,1,0:T(8,128)(2,1)S(1)}, u32[]{:S(2)}, u32[]{:S(2)}) %collective-permute-start.94) | collective-permute-done | bytes 589856 | tf_op jit(solution)/shard_map/ppermute | solution.py:48
  848.7 10.0 collective-permute-done.95.refs_2_
  858.7 17.6 %collective-permute-done.96.refs_3_ = bf16[8,48,768]{2,1,0:T(8,128)(2,1)S(1)} collective-permute-done((bf16[8,48,768]{2,1,0:T(8,128)(2,1)}, bf16[8,48,768]{2,1,0:T(8,128)(2,1)S(1)}, u32[]{:S(2)}, u32[]{:S(2)}) %collective-permute-start.96) | collective-permute-done | bytes 589856 | tf_op jit(solution)/shard_map/ppermute | solution.py:48
  876.2 11.8 %collective-permute-done.97.refs_4_ = bf16[8,48,768]{2,1,0:T(8,128)(2,1)S(1)} collective-permute-done((bf16[8,48,768]{2,1,0:T(8,128)(2,1)}, bf16[8,48,768]{2,1,0:T(8,128)(2,1)S(1)}, u32[]{:S(2)}, u32[]{:S(2)}) %collective-permute-start.97) | collective-permute-done | bytes 589856 | tf_op jit(solution)/shard_map/ppermute | solution.py:48
  933.2 16.3 %collective-permute-done.100.refs_3_ = bf16[2,48,768]{2,1,0:T(8,128)(2,1)S(1)} collective-permute-done((bf16[2,48,768]{2,1,0:T(8,128)(2,1)S(1)}, bf16[2,48,768]{2,1,0:T(8,128)(2,1)S(1)}, u32[]{:S(2)}, u32[]{:S(2)}) %collective-permute-start.100) | collective-permute-done | bytes 147488 | tf_op jit(solution)/shard_map/ppermute | solution.py:39
  (828 shorter events, 563.4 us)
Async XLA Ops:
  7.2 201.7 %all-gather.7.cloned.1.call-start = ((), (), s32[]{:S(2)}) async-start(), calls=%async_computation.4 | async-start | bytes 6193152 | tf_op jit(solution)/shard_map/all_gather | solution.py:336
  11.0 212.4 %all-gather.5.cloned.1.call-start = ((), (), s32[]{:S(2)}) async-start(), calls=%async_computation.3 | async-start | bytes 12386304 | tf_op jit(solution)/shard_map/all_gather | solution.py:336
  39.5 47.2 %collective-permute-start.24 = (bf16[8,48,768]{2,1,0:T(8,128)(2,1)S(1)}, bf16[8,48,768]{2,1,0:T(8,128)(2,1)S(1)}, u32[]{:S(2)}, u32[]{:S(2)}) collective-permute-start(bf16[8,48,768]{2,1,0:T(8,128)(2,1)S(1)} %get-tuple-element.313.refs_2_), channel_id=1, source_target_pairs={{0,1},{1,0},{2,3},{3,2},{4,5},{5,4},{6,7},{7,6},{8,9},{9,8},{10,11... | collective-permute-start | bytes 1769480 | tf_op jit(solution)/shard_map/ppermute | solution.py:48
  84.1 53.8 %collective-permute-start.29 = (bf16[8,48,768]{2,1,0:T(8,128)(2,1)S(1)}, bf16[8,48,768]{2,1,0:T(8,128)(2,1)S(1)}, u32[]{:S(2)}, u32[]{:S(2)}) collective-permute-start(bf16[8,48,768]{2,1,0:T(8,128)(2,1)S(1)} %get-tuple-element.313.refs_2_), channel_id=1, source_target_pairs={{0,3},{1,2},{2,1},{3,0},{4,7},{5,6},{6,5},{7,4},{8,11},{9,10},{10,... | collective-permute-start | bytes 1769480 | tf_op jit(solution)/shard_map/ppermute | solution.py:48
  89.6 48.3 %collective-permute-start.25 = (bf16[128,1536]{1,0:T(8,128)(2,1)S(1)}, bf16[128,1536]{1,0:T(8,128)(2,1)S(1)}, u32[]{:S(2)}, u32[]{:S(2)}) collective-permute-start(bf16[128,1536]{1,0:T(8,128)(2,1)S(1)} %get-tuple-element.319.refs_0_), channel_id=1, source_target_pairs={{0,8},{4,12},{8,0},{12,4},{16,24},{20,28},{24,16},{28,20},{1,9},{5... | collective-permute-start | bytes 1179656 | tf_op jit(solution)/shard_map/ppermute | solution.py:39
  92.0 46.0 %collective-permute-start.26 = (bf16[128,1536]{1,0:T(8,128)(2,1)S(1)}, bf16[128,1536]{1,0:T(8,128)(2,1)S(1)}, u32[]{:S(2)}, u32[]{:S(2)}) collective-permute-start(bf16[128,1536]{1,0:T(8,128)(2,1)S(1)} %get-tuple-element.319.refs_0_), channel_id=1, source_target_pairs={{0,16},{4,20},{8,24},{12,28},{16,0},{20,4},{24,8},{28,12},{1,17},{... | collective-permute-start | bytes 1179656 | tf_op jit(solution)/shard_map/ppermute | solution.py:39
  92.0 46.0 %collective-permute-start.27 = (bf16[128,1536]{1,0:T(8,128)(2,1)S(1)}, bf16[128,1536]{1,0:T(8,128)(2,1)S(1)}, u32[]{:S(2)}, u32[]{:S(2)}) collective-permute-start(bf16[128,1536]{1,0:T(8,128)(2,1)S(1)} %get-tuple-element.319.refs_0_), channel_id=1, source_target_pairs={{0,24},{4,28},{8,16},{12,20},{16,8},{20,12},{24,0},{28,4},{1,25},{... | collective-permute-start | bytes 1179656 | tf_op jit(solution)/shard_map/ppermute | solution.py:39
  141.8 278.1 %all-gather.11.cloned.1.call-start = ((), (), s32[]{:S(2)}) async-start(), calls=%async_computation.6 | async-start | bytes 6193152 | tf_op jit(solution)/shard_map/all_gather | solution.py:336
  188.2 231.7 %all-gather.9.cloned.1.call-start = ((), (), s32[]{:S(2)}) async-start(), calls=%async_computation.5 | async-start | bytes 12386304 | tf_op jit(solution)/shard_map/all_gather | solution.py:336
  189.0 48.7 %collective-permute-start.38 = (bf16[128,1536]{1,0:T(8,128)(2,1)}, bf16[128,1536]{1,0:T(8,128)(2,1)S(1)}, u32[]{:S(2)}, u32[]{:S(2)}) collective-permute-start(bf16[128,1536]{1,0:T(8,128)(2,1)} %get-tuple-element.339.refs_0_), channel_id=1, source_target_pairs={{0,2},{1,3},{2,0},{3,1},{4,6},{5,7},{6,4},{7,5},{8,10},{9,11},{10,... | collective-permute-start | bytes 1179656 | tf_op jit(solution)/shard_map/ppermute | solution.py:48
  191.5 54.2 %collective-permute-start.40 = (bf16[128,1536]{1,0:T(8,128)(2,1)}, bf16[128,1536]{1,0:T(8,128)(2,1)S(1)}, u32[]{:S(2)}, u32[]{:S(2)}) collective-permute-start(bf16[128,1536]{1,0:T(8,128)(2,1)} %get-tuple-element.339.refs_0_), channel_id=1, source_target_pairs={{0,3},{1,2},{2,1},{3,0},{4,7},{5,6},{6,5},{7,4},{8,11},{9,10},{10,... | collective-permute-start | bytes 1179656 | tf_op jit(solution)/shard_map/ppermute | solution.py:48
  194.3 59.2 %collective-permute-start.43 = (bf16[1,48,3584]{2,1,0:T(8,128)(2,1)}, bf16[1,48,3584]{2,1,0:T(8,128)(2,1)}, u32[]{:S(2)}, u32[]{:S(2)}) collective-permute-start(bf16[1,48,3584]{2,1,0:T(8,128)(2,1)} %get-tuple-element.576), channel_id=1, source_target_pairs={{0,1},{1,0},{2,3},{3,2},{4,5},{5,4},{6,7},{7,6},{8,9},{9,8},{10,11... | collective-permute-start | bytes 1032200 | tf_op jit(solution)/shard_map/ppermute | solution.py:48
  195.7 58.4 %collective-permute-start.44 = (bf16[1,48,3584]{2,1,0:T(8,128)(2,1)}, bf16[1,48,3584]{2,1,0:T(8,128)(2,1)}, u32[]{:S(2)}, u32[]{:S(2)}) collective-permute-start(bf16[1,48,3584]{2,1,0:T(8,128)(2,1)} %get-tuple-element.575), channel_id=1, source_target_pairs={{0,2},{1,3},{2,0},{3,1},{4,6},{5,7},{6,4},{7,5},{8,10},{9,11},{10,... | collective-permute-start | bytes 1032200 | tf_op jit(solution)/shard_map/ppermute | solution.py:48
  206.5 94.0 %collective-permute-start.42 = (bf16[8,48,768]{2,1,0:T(8,128)(2,1)S(1)}, bf16[8,48,768]{2,1,0:T(8,128)(2,1)S(1)}, u32[]{:S(2)}, u32[]{:S(2)}) collective-permute-start(bf16[8,48,768]{2,1,0:T(8,128)(2,1)S(1)} %copy-done.34), channel_id=1, source_target_pairs={{0,1},{1,0},{2,3},{3,2},{4,5},{5,4},{6,7},{7,6},{8,9},{9,8},{10,11... | collective-permute-start | bytes 1769480 | tf_op jit(solution)/shard_map/ppermute | solution.py:48
  237.7 62.8 %collective-permute-start.37 = (bf16[128,1536]{1,0:T(8,128)(2,1)S(1)}, bf16[128,1536]{1,0:T(8,128)(2,1)S(1)}, u32[]{:S(2)}, u32[]{:S(2)}) collective-permute-start(bf16[128,1536]{1,0:T(8,128)(2,1)S(1)} %get-tuple-element.343), channel_id=1, source_target_pairs={{0,1},{1,0},{2,3},{3,2},{4,5},{5,4},{6,7},{7,6},{8,9},{9,8},{10,11... | collective-permute-start | bytes 1179656 | tf_op jit(solution)/shard_map/ppermute | solution.py:48
  245.7 54.9 %collective-permute-start.39 = (bf16[128,1536]{1,0:T(8,128)(2,1)S(1)}, bf16[128,1536]{1,0:T(8,128)(2,1)S(1)}, u32[]{:S(2)}, u32[]{:S(2)}) collective-permute-start(bf16[128,1536]{1,0:T(8,128)(2,1)S(1)} %get-tuple-element.345), channel_id=1, source_target_pairs={{0,2},{1,3},{2,0},{3,1},{4,6},{5,7},{6,4},{7,5},{8,10},{9,11},{10,... | collective-permute-start | bytes 1179656 | tf_op jit(solution)/shard_map/ppermute | solution.py:48
  253.5 47.0 %collective-permute-start.41 = (bf16[128,1536]{1,0:T(8,128)(2,1)S(1)}, bf16[128,1536]{1,0:T(8,128)(2,1)S(1)}, u32[]{:S(2)}, u32[]{:S(2)}) collective-permute-start(bf16[128,1536]{1,0:T(8,128)(2,1)S(1)} %get-tuple-element.347), channel_id=1, source_target_pairs={{0,3},{1,2},{2,1},{3,0},{4,7},{5,6},{6,5},{7,4},{8,11},{9,10},{10,... | collective-permute-start | bytes 1179656 | tf_op jit(solution)/shard_map/ppermute | solution.py:48
  305.2 435.1 %reduce-scatter.4.cloned.1.call-start = ((), (), s32[]{:S(2)}) async-start(), calls=%async_computation.7 | async-start | bytes 12386304 | tf_op jit(solution)/shard_map/reduce_scatter | solution.py:450
  403.8 53.1 %collective-permute-start.59 = (bf16[128,1536]{1,0:T(8,128)(2,1)}, bf16[128,1536]{1,0:T(8,128)(2,1)}, u32[]{:S(2)}, u32[]{:S(2)}) collective-permute-start(bf16[128,1536]{1,0:T(8,128)(2,1)} %get-tuple-element.371.refs_0_), channel_id=1, source_target_pairs={{0,3},{1,2},{2,1},{3,0},{4,7},{5,6},{6,5},{7,4},{8,11},{9,10},{10,... | collective-permute-start | bytes 1179656 | tf_op jit(solution)/shard_map/ppermute | solution.py:48
  404.3 59.8 %collective-permute-start.61 = (bf16[128,1536]{1,0:T(8,128)(2,1)S(1)}, bf16[128,1536]{1,0:T(8,128)(2,1)S(1)}, u32[]{:S(2)}, u32[]{:S(2)}) collective-permute-start(bf16[128,1536]{1,0:T(8,128)(2,1)S(1)} %copy-done.36), channel_id=1, source_target_pairs={{0,1},{1,0},{2,3},{3,2},{4,5},{5,4},{6,7},{7,6},{8,9},{9,8},{10,11... | collective-permute-start | bytes 1179656 | tf_op jit(solution)/shard_map/ppermute | solution.py:48
  405.3 75.8 %collective-permute-start.62 = (bf16[128,1536]{1,0:T(8,128)(2,1)S(1)}, bf16[128,1536]{1,0:T(8,128)(2,1)}, u32[]{:S(2)}, u32[]{:S(2)}) collective-permute-start(bf16[128,1536]{1,0:T(8,128)(2,1)S(1)} %copy-done.36), channel_id=1, source_target_pairs={{0,2},{1,3},{2,0},{3,1},{4,6},{5,7},{6,4},{7,5},{8,10},{9,11},{10,... | collective-permute-start | bytes 1179656 | tf_op jit(solution)/shard_map/ppermute | solution.py:48
  418.9 71.8 %collective-permute-start.63 = (bf16[128,1536]{1,0:T(8,128)(2,1)S(1)}, bf16[128,1536]{1,0:T(8,128)(2,1)}, u32[]{:S(2)}, u32[]{:S(2)}) collective-permute-start(bf16[128,1536]{1,0:T(8,128)(2,1)S(1)} %copy-done.36), channel_id=1, source_target_pairs={{0,3},{1,2},{2,1},{3,0},{4,7},{5,6},{6,5},{7,4},{8,11},{9,10},{10,... | collective-permute-start | bytes 1179656 | tf_op jit(solution)/shard_map/ppermute | solution.py:48
  437.3 91.8 %collective-permute-start.56 = (bf16[128,1536]{1,0:T(8,128)(2,1)}, bf16[128,1536]{1,0:T(8,128)(2,1)S(1)}, u32[]{:S(2)}, u32[]{:S(2)}) collective-permute-start(bf16[128,1536]{1,0:T(8,128)(2,1)} %get-tuple-element.376), channel_id=1, source_target_pairs={{0,1},{1,0},{2,3},{3,2},{4,5},{5,4},{6,7},{7,6},{8,9},{9,8},{10,11... | collective-permute-start | bytes 1179656 | tf_op jit(solution)/shard_map/ppermute | solution.py:48
  456.9 72.8 %collective-permute-start.58 = (bf16[128,1536]{1,0:T(8,128)(2,1)S(1)}, bf16[128,1536]{1,0:T(8,128)(2,1)S(1)}, u32[]{:S(2)}, u32[]{:S(2)}) collective-permute-start(bf16[128,1536]{1,0:T(8,128)(2,1)S(1)} %get-tuple-element.378), channel_id=1, source_target_pairs={{0,2},{1,3},{2,0},{3,1},{4,6},{5,7},{6,4},{7,5},{8,10},{9,11},{10,... | collective-permute-start | bytes 1179656 | tf_op jit(solution)/shard_map/ppermute | solution.py:48
  464.1 65.6 %collective-permute-start.60 = (bf16[128,1536]{1,0:T(8,128)(2,1)S(1)}, bf16[128,1536]{1,0:T(8,128)(2,1)S(1)}, u32[]{:S(2)}, u32[]{:S(2)}) collective-permute-start(bf16[128,1536]{1,0:T(8,128)(2,1)S(1)} %get-tuple-element.380), channel_id=1, source_target_pairs={{0,3},{1,2},{2,1},{3,0},{4,7},{5,6},{6,5},{7,4},{8,11},{9,10},{10,... | collective-permute-start | bytes 1179656 | tf_op jit(solution)/shard_map/ppermute | solution.py:48
  576.7 326.0 %reduce-scatter.6.cloned.1.call-start = ((), (), s32[]{:S(2)}) async-start(), calls=%async_computation.8 | async-start | bytes 6193152 | tf_op jit(solution)/shard_map/reduce_scatter | solution.py:450
  577.3 374.5 %reduce-scatter.8.cloned.1.call-start = ((), (), s32[]{:S(2)}) async-start(), calls=%async_computation.9 | async-start | bytes 12386304 | tf_op jit(solution)/shard_map/reduce_scatter | solution.py:450
  636.1 47.2 %collective-permute-start.79 = (bf16[128,1536]{1,0:T(8,128)(2,1)}, bf16[128,1536]{1,0:T(8,128)(2,1)S(1)}, u32[]{:S(2)}, u32[]{:S(2)}) collective-permute-start(bf16[128,1536]{1,0:T(8,128)(2,1)} %get-tuple-element.438.refs_0_), channel_id=1, source_target_pairs={{0,3},{1,2},{2,1},{3,0},{4,7},{5,6},{6,5},{7,4},{8,11},{9,10},{10,... | collective-permute-start | bytes 1179656 | tf_op jit(solution)/shard_map/ppermute | solution.py:48
  769.7 45.6 %collective-permute-start.93 = (bf16[8,48,768]{2,1,0:T(8,128)(2,1)}, bf16[8,48,768]{2,1,0:T(8,128)(2,1)S(1)}, u32[]{:S(2)}, u32[]{:S(2)}) collective-permute-start(bf16[8,48,768]{2,1,0:T(8,128)(2,1)} %get-tuple-element.489), channel_id=1, source_target_pairs={{0,1},{1,0},{2,3},{3,2},{4,5},{5,4},{6,7},{7,6},{8,9},{9,8},{10,11... | collective-permute-start | bytes 1769480 | tf_op jit(solution)/shard_map/ppermute | solution.py:48
  836.9 51.2 %collective-permute-start.97 = (bf16[8,48,768]{2,1,0:T(8,128)(2,1)}, bf16[8,48,768]{2,1,0:T(8,128)(2,1)S(1)}, u32[]{:S(2)}, u32[]{:S(2)}) collective-permute-start(bf16[8,48,768]{2,1,0:T(8,128)(2,1)} %get-tuple-element.503), channel_id=1, source_target_pairs={{0,3},{1,2},{2,1},{3,0},{4,7},{5,6},{6,5},{7,4},{8,11},{9,10},{10,... | collective-permute-start | bytes 1769480 | tf_op jit(solution)/shard_map/ppermute | solution.py:48
  913.7 46.0 %collective-permute-start.106 = (bf16[224,1536]{1,0:T(8,128)(2,1)}, bf16[224,1536]{1,0:T(8,128)(2,1)}, u32[]{:S(2)}, u32[]{:S(2)}) collective-permute-start(bf16[224,1536]{1,0:T(8,128)(2,1)} %get-tuple-element.518), channel_id=1, source_target_pairs={{0,8},{4,12},{8,0},{12,4},{16,24},{20,28},{24,16},{28,20},{1,9},{5... | collective-permute-start | bytes 2064392 | tf_op jit(solution)/shard_map/ppermute | solution.py:39
  917.6 45.5 %collective-permute-start.108 = (bf16[224,1536]{1,0:T(8,128)(2,1)}, bf16[224,1536]{1,0:T(8,128)(2,1)}, u32[]{:S(2)}, u32[]{:S(2)}) collective-permute-start(bf16[224,1536]{1,0:T(8,128)(2,1)} %get-tuple-element.520), channel_id=1, source_target_pairs={{0,24},{4,28},{8,16},{12,20},{16,8},{20,12},{24,0},{28,4},{1,25},{... | collective-permute-start | bytes 2064392 | tf_op jit(solution)/shard_map/ppermute | solution.py:39
  (331 other events, 4207.1 us)
Sparse Core Ops, SparseCore 0:
  11.1 46.5 all-gather.6
  141.9 81.4 all-gather.4
  225.3 42.2 all-gather.10
  305.3 72.6 all-gather.8
  576.8 94.5 reduce-scatter.3
  674.8 74.3 reduce-scatter.5
  753.1 100.3 reduce-scatter.7
